TPU v7x, 128 devices: a whole 4x4x4 slice. The times are simulated.
128 devices in a mesh: group: 4 (over y), ctx: 4 (over x), tp: 8 (over z, core).
Axes of the slice: x: 4, y: 4, z: 4, core: 2. Of those that a mesh axis runs over, the one named last changes fastest.
Arguments:
- tokens: bfloat16 [2048, 8192], P('group', 'ctx'), may hold values from -200 to 200, as said below
- norm_gain: float32 [8192], P('ctx'), may hold values from 0.5 to 2
- w_query: bfloat16 [8192, 8192], P('ctx', 'tp'), may hold values from -0.25 to 0.25
- w_key: bfloat16 [8192, 1024], P('ctx', 'tp'), may hold values from -0.03125 to 0.03125
- w_value: bfloat16 [8192, 1024], P('ctx', 'tp'), may hold values from -0.03125 to 0.03125
- w_out: bfloat16 [8192, 8192], P('tp', 'ctx'), may hold values from -0.09375 to 0.09375
- kv_pool: bfloat16 [1024, 2, 8, 128, 128], P(('group', 'ctx'), None, 'tp'), may hold values from -80 to 80, as said below
- block_table: int32 [8, 256], replicated, may hold values from 0 to 1023, as said below
- prefix_len: int32 [8], replicated, may hold values from 8192 to 32768, as said below
- write_slot: int32 [8, 2], replicated, may hold values from 0 to 1023, as said below
Outputs:
- attention_out: bfloat16 [2048, 8192], P('group', ('ctx', 'tp'))
- new_pool: bfloat16 [1024, 2, 8, 128, 128], P(('group', 'ctx'), None, 'tp')
Inputs may be any that keep to these rules, and one draw needn't show every extreme that they name: `tokens`: hidden states of order one to some hundreds. `kv_pool`: keys and values mostly of order one, a few up to some tens. `block_table`: entry = o * 64 + j: pool block j of the device at index o // (size of ctx) of group and o % (size of ctx) of ctx. The list slots handled by one device, those of the 2 sessions of its group index with slot number b such that b modulo the size of ctx equals its ctx index, lie exactly 8 on each pool device. Blocks may be shared by several slots and sessions. `prefix_len`: some session has 32768 prefix tokens and some has 8192. `write_slot`: all entries are distinct.
All inputs are finite; a program needn't handle non-finite values.
Results may differ from a plain program's by a relative error of at most 0.02.
The roundings to bfloat16 on the way count: a program that leaves them out, or rounds other values in their place, can miss the bound.
Values may be sent and summed in bfloat16 or wider, within the bound.
No kernel may reach another device: no remote copies, remote signals or barrier semaphores. Data moves between devices by JAX's collectives and lax.ppermute only.
A program may use at most 128 MiB of HBM per device.

v0:
```python
import jax
import jax.numpy as jnp
from jax import lax
from jax.sharding import PartitionSpec as P

NEG_FILL = -1e30


def local(
    tokens, norm_gain, w_query, w_key, w_value, w_out, kv_pool, block_table, prefix_len, write_slot
):
    groups_count = lax.axis_size("group")
    ctx_count = lax.axis_size("ctx")
    owners_count = groups_count * ctx_count
    ctx_rank = lax.axis_index("ctx")
    group_rank = lax.axis_index("group")
    device_id = group_rank * ctx_count + ctx_rank
    pool_size = kv_pool.shape[0]
    kv_local = kv_pool.shape[2]
    block_len = kv_pool.shape[3]
    head_dim = kv_pool.shape[4]
    sessions_all, list_len = block_table.shape
    sess_here = sessions_all // groups_count
    per_ctx = list_len // ctx_count
    per_device = sess_here * per_ctx
    capacity = per_device // owners_count
    tok_here = tokens.shape[0]
    new_len = tok_here // sess_here
    q_local = w_query.shape[1] // head_dim
    group_size = q_local // kv_local
    row_count = new_len * group_size
    wide_rows = tokens.astype(jnp.float32)
    square_part = jnp.sum(wide_rows * wide_rows, axis=1)
    normalized = (wide_rows * norm_gain[None, :]).astype(jnp.bfloat16)
    query_part = jnp.dot(normalized, w_query, preferred_element_type=jnp.float32)
    key_part = jnp.dot(normalized, w_key, preferred_element_type=jnp.float32)
    value_part = jnp.dot(normalized, w_value, preferred_element_type=jnp.float32)
    square_sum, query_sum, key_sum, value_sum = lax.psum(
        (square_part, query_part, key_part, value_part), "ctx"
    )
    row_scale = lax.rsqrt(square_sum / (tokens.shape[1] * ctx_count) + 1e-05)[:, None]
    queries = (row_scale * query_sum).astype(jnp.bfloat16)
    keys_new = (row_scale * key_sum).astype(jnp.bfloat16)
    values_new = (row_scale * value_sum).astype(jnp.bfloat16)
    slot_table = (
        block_table.reshape(groups_count, sess_here, per_ctx, ctx_count)
        .transpose(0, 3, 1, 2)
        .reshape(owners_count, per_device)
    )
    owner_of = slot_table // pool_size
    local_slot = slot_table % pool_size
    is_mine = owner_of == device_id
    rank_among = jnp.cumsum(is_mine.astype(jnp.int32), axis=1) - 1
    picked = is_mine[:, :, None] & (
        rank_among[:, :, None] == jnp.arange(capacity, dtype=jnp.int32)[None, None, :]
    )
    send_index = jnp.sum(jnp.where(picked, local_slot[:, :, None], 0), axis=1)
    outgoing = kv_pool[send_index]
    incoming = lax.all_to_all(outgoing, ("group", "ctx"), split_axis=0, concat_axis=0, tiled=True)
    my_owners = lax.dynamic_index_in_dim(owner_of, device_id, 0, keepdims=False)
    same_owner = my_owners[:, None] == my_owners[None, :]
    slot_ids = jnp.arange(per_device, dtype=jnp.int32)
    earlier = slot_ids[None, :] < slot_ids[:, None]
    slot_rank = jnp.sum((same_owner & earlier).astype(jnp.int32), axis=1)
    flat_index = my_owners * capacity + slot_rank
    fetched = incoming.reshape((owners_count * capacity,) + incoming.shape[2:])[flat_index]
    step_blocks = min(per_ctx, max(1, 1024 // block_len))
    step_count = per_ctx // step_blocks
    score_scale = head_dim ** (-0.5)
    lengths = lax.dynamic_slice_in_dim(prefix_len, group_rank * sess_here, sess_here)
    query_sets = (
        queries.reshape(sess_here, new_len, kv_local, group_size, head_dim)
        .transpose(0, 2, 1, 3, 4)
        .reshape(sess_here, kv_local, row_count, head_dim)
    )
    fresh_keys = keys_new.reshape(sess_here, new_len, kv_local, head_dim)
    fresh_values = values_new.reshape(sess_here, new_len, kv_local, head_dim)
    token_of_row = jnp.arange(row_count, dtype=jnp.int32) // group_size
    fresh_index = jnp.arange(new_len, dtype=jnp.int32)
    fresh_live = (fresh_index[None, :] <= token_of_row[:, None]) & (
        fresh_index[None, :] % ctx_count == ctx_rank
    )
    top_list, total_list, accum_list = ([], [], [])
    for session in range(sess_here):
        query_set = query_sets[session]
        length = lengths[session]
        fresh_scores = (
            jnp.einsum(
                "hrd,jhd->hrj", query_set, fresh_keys[session], preferred_element_type=jnp.float32
            )
            * score_scale
        )
        fresh_masked = jnp.where(fresh_live[None], fresh_scores, NEG_FILL)
        top_start = jnp.max(fresh_masked, axis=2)
        fresh_weights = jnp.where(
            fresh_live[None], jnp.exp(fresh_masked - top_start[..., None]), 0.0
        )
        total_start = jnp.sum(fresh_weights, axis=2)
        accum_start = jnp.einsum(
            "hrj,jhd->hrd",
            fresh_weights.astype(jnp.bfloat16),
            fresh_values[session],
            preferred_element_type=jnp.float32,
        )
        session_blocks = fetched[session * per_ctx : (session + 1) * per_ctx].reshape(
            step_count, step_blocks, 2, kv_local, block_len, head_dim
        )

        def advance(
            position, state_now, session_blocks=session_blocks, query_set=query_set, length=length
        ):
            top_now, total_now, accum_now = state_now
            block_piece = lax.dynamic_index_in_dim(session_blocks, position, 0, keepdims=False)
            scores = (
                jnp.einsum(
                    "hrd,uhtd->hrut",
                    query_set,
                    block_piece[:, 0],
                    preferred_element_type=jnp.float32,
                )
                * score_scale
            )
            slot_numbers = (
                position * step_blocks + jnp.arange(step_blocks, dtype=jnp.int32)
            ) * ctx_count + ctx_rank
            positions = (
                slot_numbers[:, None] * block_len + jnp.arange(block_len, dtype=jnp.int32)[None, :]
            )
            live_mask = (positions < length)[None, None]
            masked = jnp.where(live_mask, scores, NEG_FILL)
            top_next = jnp.maximum(top_now, jnp.max(masked, axis=(2, 3)))
            shrink = jnp.exp(top_now - top_next)
            weights = jnp.where(live_mask, jnp.exp(masked - top_next[..., None, None]), 0.0)
            total_next = total_now * shrink + jnp.sum(weights, axis=(2, 3))
            accum_next = accum_now * shrink[..., None] + jnp.einsum(
                "hrut,uhtd->hrd",
                weights.astype(jnp.bfloat16),
                block_piece[:, 1],
                preferred_element_type=jnp.float32,
            )
            return (top_next, total_next, accum_next)

        top_end, total_end, accum_end = lax.fori_loop(
            0, step_count, advance, (top_start, total_start, accum_start)
        )
        top_list.append(top_end)
        total_list.append(total_end)
        accum_list.append(accum_end)
    top_all = jnp.stack(top_list)
    total_all = jnp.stack(total_list)
    accum_all = jnp.stack(accum_list)
    global_top = lax.pmax(top_all, "ctx")
    rescale = jnp.exp(top_all - global_top)
    total_all, accum_all = lax.psum((total_all * rescale, accum_all * rescale[..., None]), "ctx")
    attended = accum_all / total_all[..., None]
    attended = (
        attended.reshape(sess_here, kv_local, new_len, group_size, head_dim)
        .transpose(0, 2, 1, 3, 4)
        .reshape(tok_here, q_local * head_dim)
        .astype(jnp.bfloat16)
    )
    out_share = lax.psum_scatter(
        lax.dot_general(
            w_out, attended, (((0,), (1,)), ((), ())), preferred_element_type=jnp.float32
        ).astype(jnp.bfloat16),
        "tp",
        scatter_dimension=0,
        tiled=True,
    ).astype(jnp.float32)
    attention_out = out_share.T.astype(jnp.bfloat16)
    blocks_here = sess_here * new_len // block_len
    write_count = blocks_here // ctx_count
    packed = (
        jnp.stack([keys_new, values_new], axis=1)
        .reshape(blocks_here, block_len, 2, kv_local, head_dim)
        .transpose(0, 2, 3, 1, 4)
    )
    packed = packed.reshape((write_count, ctx_count) + packed.shape[1:])
    sent_blocks = lax.dynamic_index_in_dim(packed, ctx_rank, 1, keepdims=False)
    targets = (
        write_slot.reshape(groups_count, write_count, ctx_count)
        .transpose(0, 2, 1)
        .reshape(owners_count, write_count)
    )
    my_targets = lax.dynamic_index_in_dim(targets, device_id, 0, keepdims=False)
    destination = my_targets // pool_size
    routed = jnp.arange(owners_count, dtype=jnp.int32)[:, None] == destination[None, :]
    outgoing_new = jnp.where(routed[:, :, None, None, None, None], sent_blocks[None], 0)
    arrived = lax.all_to_all(
        outgoing_new, ("group", "ctx"), split_axis=0, concat_axis=0, tiled=True
    )
    keep_here = targets // pool_size == device_id
    placement = jnp.where(keep_here, targets % pool_size, pool_size).reshape(-1)
    new_pool = kv_pool.at[placement].set(
        arrived.reshape((owners_count * write_count,) + arrived.shape[2:]), mode="drop"
    )
    return (attention_out, new_pool)


def solution(mesh):
    placed = (
        P("group", "ctx"),
        P("ctx"),
        P("ctx", "tp"),
        P("ctx", "tp"),
        P("ctx", "tp"),
        P("tp", "ctx"),
        P(("group", "ctx"), None, "tp", None, None),
        P(),
        P(),
        P(),
    )
    return jax.shard_map(
        local,
        mesh=mesh,
        in_specs=placed,
        out_specs=(P("group", ("ctx", "tp")), P(("group", "ctx"), None, "tp", None, None)),
        check_vma=False,
    )
```

profile of v0, /device:TPU:24, one launch (start us, length us, event | category | flops | bytes accessed | tf_op | source)
XLA Modules:
  0.0 469.6 jit_solution(12429759382438884986)
XLA Ops:
  7.2 4.8 %copy.79 = bf16[64,2,1,128,128]{4,3,2,1,0:T(8,128)(2,1)} copy(bf16[64,2,1,128,128]{4,3,2,1,0:T(8,128)(2,1)} %param.20) | data formatting | bytes 8388608
  13.5 8.8 %gather_fusion = bf16[128,2,128,128]{3,2,1,0:T(8,128)(2,1)} fusion(bf16[64,2,128,128]{3,2,1,0:T(8,128)(2,1)} %bitcast.169, s32[1024]{0:T(1024)S(1)} %pad_clamp_fusion.1), kind=kCustom, calls=%fused_computation | custom fusion | bytes 16777728 | tf_op jit(solution)/shard_map/gather | solution.py:58
  22.2 7.4 %all-to-all-start = ((bf16[16,8,2,1,128,128]{5,4,2,1,3,0:T(8,128)(2,1)}), bf16[16,8,2,1,128,128]{5,4,2,1,3,0:T(8,128)(2,1)}, u32[]{:S(2)}, u32[]{:S(2)}) async-start(bf16[16,8,2,1,128,128]{5,4,2,1,3,0:T(8,128)(2,1)} %bitcast.172), calls=%async_computation | async-start | bytes 16777216 | tf_op jit(solution)/shard_map/all_to_all | solution.py:59
  32.6 3.7 fusion.46
  36.9 141.4 %psum.42 = f32[512]{0:T(512)S(1)} all-reduce(f32[512]{0:T(512)S(1)} %fusion.36), channel_id=1, replica_groups=mesh['group'=4,'ctx'=4,'tp'=8] {'ctx'}, use_global_device_ids=true, to_apply=%region_1.0 | all-reduce | flops 512 | bytes 4096 | tf_op jit(solution)/shard_map/psum | solution.py:38
  179.2 1.8 multiply_convert_fusion
  186.6 9.9 %gather_fusion.1 = bf16[128,2,128,128]{3,2,1,0:T(8,128)(2,1)} fusion(bf16[128,2,128,128]{3,2,1,0:T(8,128)(2,1)} %bitcast.32, s32[1024]{0:T(1024)S(1)} %pad_clamp_fusion), kind=kCustom, calls=%fused_computation.1 | custom fusion | bytes 16777728 | tf_op jit(solution)/shard_map/gather | solution.py:66
  196.6 6.0 %fusion.84 = (bf16[64,2,128,128]{3,2,1,0:T(8,128)(2,1)}, bf16[64,2,128,128]{3,2,1,0:T(8,128)(2,1)}) fusion(bf16[128,2,128,128]{3,2,1,0:T(8,128)(2,1)} %gather_fusion.1), kind=kLoop, calls=%fused_computation.146 | loop fusion | bytes 16777216 | tf_op jit(solution)/shard_map/slice | solution.py:105
  202.6 70.1 %while.35 = (s32[]{:T(128)}, f32[1,2048]{1,0:T(1,128)S(1)}, f32[1,2048]{1,0:T(1,128)S(1)}, f32[1,2048,128]{2,1,0:T(8,128)S(1)}, s32[]{:T(128)}, /*index=5*/s32[]...) while((s32[]{:T(128)}, f32[1,2048]{1,0:T(1,128)S(1)}, ...), condition=%wide.region_19.20_spmd, body=%wide.region_16.19_spmd.sunk | while | flops 1101535232 | bytes 29495496 | solution.py:143
  204.3 1.5 fusion.109
  205.9 2.6 fusion.110
  208.5 2.8 fusion.111
  214.7 2.6 fusion.110
  217.3 2.8 fusion.111
  221.8 1.6 fusion.109
  223.4 2.6 fusion.110
  226.0 2.8 fusion.111
  230.6 1.6 fusion.109
  232.2 2.6 fusion.110
  234.8 2.8 fusion.111
  239.4 1.6 fusion.109
  240.9 2.6 fusion.110
  243.6 2.8 fusion.111
  248.1 1.6 fusion.109
  249.7 2.6 fusion.110
  252.3 2.8 fusion.111
  256.9 1.6 fusion.109
  258.5 2.6 fusion.110
  261.1 2.8 fusion.111
  265.7 1.6 fusion.109
  267.2 2.6 fusion.110
  269.9 2.8 fusion.111
  272.7 70.6 %while.34 = (s32[]{:T(128)}, f32[1,2048]{1,0:T(1,128)S(1)}, f32[1,2048]{1,0:T(1,128)S(1)}, f32[1,2048,128]{2,1,0:T(8,128)S(1)}, s32[]{:T(128)}, /*index=5*/s32[]...) while((s32[]{:T(128)}, f32[1,2048]{1,0:T(1,128)S(1)}, ...), condition=%wide.region_13.14_spmd, body=%wide.region_10.13_spmd.sunk | while | flops 1101535232 | bytes 29495496 | solution.py:143
  274.5 1.6 fusion.105
  276.1 2.6 fusion.106
  278.7 2.8 fusion.107
  283.3 1.5 fusion.105
  284.9 2.6 fusion.106
  287.5 2.8 fusion.107
  292.2 1.6 fusion.105
  293.7 2.6 fusion.106
  296.3 2.8 fusion.107
  302.6 2.6 fusion.106
  305.2 2.8 fusion.107
  309.8 1.6 fusion.105
  311.4 2.6 fusion.106
  314.0 2.8 fusion.107
  320.2 2.6 fusion.106
  322.8 2.8 fusion.107
  327.5 1.6 fusion.105
  329.0 2.6 fusion.106
  331.6 2.8 fusion.107
  337.9 2.6 fusion.106
  340.5 2.8 fusion.107
  343.3 15.8 %pmax.7 = f32[2,1,2048]{2,0,1:T(2,128)S(1)} all-reduce(f32[2,1,2048]{2,0,1:T(2,128)S(1)} %pad_maximum_fusion), channel_id=1, replica_groups=mesh['group'=4,'ctx'=4,'tp'=8] {'ctx'}, use_global_device_ids=true, to_apply=%region_20.21 | all-reduce | flops 4096 | bytes 32768 | tf_op jit(solution)/shard_map/pmax | solution.py:152
  359.1 1.7 maximum_multiply_fusion
  360.9 14.6 %psum.47 = f32[2,2048]{1,0:T(2,128)S(1)} all-reduce(f32[2,2048]{1,0:T(2,128)S(1)} %get-tuple-element.390), channel_id=1, replica_groups=mesh['group'=4,'ctx'=4,'tp'=8] {'ctx'}, use_global_device_ids=true, to_apply=%region_22.23 | all-reduce | flops 4096 | bytes 32768 | tf_op jit(solution)/shard_map/psum | solution.py:154
  375.5 45.0 %all-reduce.4.cloned.1.call-done = f32[2,1,2048,128]{3,2,1,0:T(8,128)} async-done(((f32[2,1,2048,128]{3,2,1,0:T(8,128)}), f32[2,1,2048,128]{3,2,1,0:T(8,128)}) %all-reduce.4.cloned.1.call-update) | async-done | bytes 2097168 | tf_op jit(solution)/shard_map/psum | solution.py:154
  420.5 2.0 divide_convert_fusion
  423.0 5.9 %fusion.38 = bf16[2048,512]{0,1:T(8,128)(2,1)} fusion(bf16[512,1024]{1,0:T(8,128)(2,1)S(1)} %convert_element_type.78, bf16[1024,2048]{1,0:T(8,128)(2,1)} %param.19), kind=kOutput, calls=%fused_computation.54 | convolution fusion | flops 2148532224 | bytes 7340032 | tf_op jit(solution)/shard_map/dot_general | solution.py:163
  433.3 5.8 %all-to-all-start.1 = ((bf16[16,1,2,1,128,128]{5,4,2,3,1,0:T(8,128)(2,1)}), bf16[16,1,2,1,128,128]{5,4,2,3,1,0:T(8,128)(2,1)S(1)}, u32[]{:S(2)}, u32[]{:S(2)}) async-start(bf16[16,1,2,1,128,128]{5,4,2,3,1,0:T(8,128)(2,1)} %broadcast_select_fusion), calls=%async_computation.2 | async-start | bytes 2097152 | tf_op jit(solution)/shard_map/all_to_all | solution.py:189
  439.1 14.8 %all-to-all-done.1 = bf16[16,1,2,1,128,128]{5,4,2,3,1,0:T(8,128)(2,1)S(1)} async-done(((bf16[16,1,2,1,128,128]{5,4,2,3,1,0:T(8,128)(2,1)}), bf16[16,1,2,1,128,128]{5,4,2,3,1,0:T(8,128)(2,1)S(1)}, u32[]{:S(2)}, u32[]{:S(2)}) %all-to-all-start.1) | async-done | bytes 1048608 | tf_op jit(solution)/shard_map/all_to_all | solution.py:189
  454.0 2.8 scatter_fusion
  456.7 6.3 %reduce-scatter.2.cloned.1.call-done = bf16[256,512]{0,1:T(8,128)(2,1)} async-done(((bf16[2048,512]{0,1:T(8,128)(2,1)}), bf16[256,512]{0,1:T(8,128)(2,1)}) %reduce-scatter.2.cloned.1.call-update) | async-done | bytes 262160 | tf_op jit(solution)/shard_map/reduce_scatter | solution.py:162
  (175 shorter events, 48.7 us)
Async XLA Ops:
  7.2 22.5 %copy-start = (bf16[2048,128]{1,0:T(8,128)(2,1)S(1)}, bf16[2048,128]{1,0:T(8,128)(2,1)}, u32[]{:S(2)}) copy-start(bf16[2048,128]{1,0:T(8,128)(2,1)} %param.17) | copy-start | bytes 1572868
  7.2 4.9 %copy-start.5 = (s32[8,256]{1,0:T(8,128)S(1)}, s32[8,256]{1,0:T(8,128)}, u32[]{:S(2)}) copy-start(s32[8,256]{1,0:T(8,128)} %param.21) | copy-start | bytes 24580
  22.2 7.5 %copy-start.2 = (bf16[512,2048]{1,0:T(8,128)(2,1)S(1)}, bf16[512,2048]{1,0:T(8,128)(2,1)}, u32[]{:S(2)}) copy-start(bf16[512,2048]{1,0:T(8,128)(2,1)} %param.14) | copy-start | bytes 6291460
  22.2 7.5 %copy-start.9 = (f32[2048]{0:T(1024)S(1)}, f32[2048]{0:T(1024)}, u32[]{:S(2)}) copy-start(f32[2048]{0:T(1024)} %param.15) | copy-start | bytes 24580
  22.2 8.9 %copy-start.8 = (bf16[2048,128]{1,0:T(8,128)(2,1)S(1)}, bf16[2048,128]{1,0:T(8,128)(2,1)}, u32[]{:S(2)}) copy-start(bf16[2048,128]{1,0:T(8,128)(2,1)} %param.18) | copy-start | bytes 1572868
  22.2 164.4 %all-to-all-start = ((bf16[16,8,2,1,128,128]{5,4,2,1,3,0:T(8,128)(2,1)}), bf16[16,8,2,1,128,128]{5,4,2,1,3,0:T(8,128)(2,1)}, u32[]{:S(2)}, u32[]{:S(2)}) async-start(bf16[16,8,2,1,128,128]{5,4,2,1,3,0:T(8,128)(2,1)} %bitcast.172), calls=%async_computation | async-start | bytes 16777216 | tf_op jit(solution)/shard_map/all_to_all | solution.py:59
  29.7 149.5 %all-reduce.6.cloned.1.call-start = ((), (), s32[]{:S(2)}) async-start(), calls=%async_computation.5 | async-start | bytes 5242880 | tf_op jit(solution)/shard_map/psum | solution.py:38
  29.7 2.9 copy-start.7
  32.6 3.8 copy-start.10
  36.3 384.2 %all-reduce.4.cloned.1.call-start = ((), (), s32[]{:S(2)}) async-start(), calls=%async_computation.3 | async-start | bytes 4194304 | tf_op jit(solution)/shard_map/psum | solution.py:154
  179.2 2.9 copy-start.3
  179.2 2.9 copy-start.4
  360.9 102.2 %reduce-scatter.2.cloned.1.call-start = ((), (), s32[]{:S(2)}) async-start(), calls=%async_computation.4 | async-start | bytes 2359296 | tf_op jit(solution)/shard_map/reduce_scatter | solution.py:162
  423.0 5.9 %copy-start.6 = (s32[8,2]{0,1:T(2,128)S(1)}, s32[8,2]{0,1:T(2,128)}, u32[]{:S(2)}) copy-start(s32[8,2]{0,1:T(2,128)} %param.23) | copy-start | bytes 196
  428.9 34.2 %copy-start.1 = (bf16[2048,128]{1,0:T(8,128)(2,1)S(1)}, bf16[2048,128]{1,0:T(8,128)(2,1)}, u32[]{:S(2)}) copy-start(bf16[2048,128]{1,0:T(8,128)(2,1)} %param.17) | copy-start | bytes 1572868
  433.3 20.6 %all-to-all-start.1 = ((bf16[16,1,2,1,128,128]{5,4,2,3,1,0:T(8,128)(2,1)}), bf16[16,1,2,1,128,128]{5,4,2,3,1,0:T(8,128)(2,1)S(1)}, u32[]{:S(2)}, u32[]{:S(2)}) async-start(bf16[16,1,2,1,128,128]{5,4,2,3,1,0:T(8,128)(2,1)} %broadcast_select_fusion), calls=%async_computation.2 | async-start | bytes 2097152 | tf_op jit(solution)/shard_map/all_to_all | solution.py:189
Sparse Core Ops, SparseCore 0:
  36.4 130.0 all-reduce.5
  361.0 59.5 all-reduce.3
  429.0 33.9 reduce-scatter.1
where the time goes:
time: 471 us; the launch traced here: 470 us
  blocking collectives  172 us (37%)
  matrix products  85.7 us (18%)
  waiting for transfers between devices  66.3 us (14%)
  other arithmetic  61.7 us (13%)
  local copies, waits for them, and re-layouts  53.3 us (11%)
  between operations  16.6 us (4%)
  starting transfers between devices  13.3 us (3%)
    psum x1, blocking collectives, local(): lax.psum((square_part, query_part, key_part, value_part), 'ctx')  141 us
    dot_general x16, matrix products, advance(): jnp.einsum('hrut,uhtd->hrd', weights.astype(jnp.bfloat16), block_piece[:,...  45.2 us
    psum x1, waiting for transfers between devices, local(): lax.psum((total_all * rescale, accum_all * rescale[..., None]), 'ctx')  45 us
    reduce_sum x16, other arithmetic, advance(): total_next = total_now * shrink + jnp.sum(weights, axis=(2, 3))  41 us
    dot_general x16, matrix products, advance(): jnp.einsum('hrd,uhtd->hrut', query_set, block_piece[:, 0], preferred_elem...  24.8 us
    squeeze x16, local copies, waits for them, and re-layouts, advance(): lax.dynamic_index_in_dim(session_blocks, position, 0, keepdims=False)  17.2 us
    pmax x1, blocking collectives, local(): global_top = lax.pmax(top_all, 'ctx')  15.8 us
    all_to_all x1, waiting for transfers between devices, local(): lax.all_to_all(outgoing_new, ('group', 'ctx'), split_axis=0, concat_axis=...  14.8 us
  transfers between devices with their start and end apart: 5, of which 3 were waited for; matrix products, arithmetic and copies ran while one was open for 4% of the time, Pallas kernels for 0%

commit v1 on v0

v1 whole, which is shorter than its diff:
```python
import jax
import jax.numpy as jnp
from jax import lax
from jax.experimental import pallas as pl
from jax.experimental.pallas import tpu as pltpu
from jax.sharding import PartitionSpec as P

NEG_FILL = -1e30
LOG2E = 1.4426950408889634
F32 = jnp.float32
BF16 = jnp.bfloat16
VMEM_BYTES = 56 * 1024 * 1024
CHUNK = 4
CTX = 4
NT = (((1,), (1,)), ((), ()))


def params():
    return pltpu.CompilerParams(vmem_limit_bytes=VMEM_BYTES)


def vmem():
    return pl.BlockSpec(memory_space=pltpu.VMEM)


def smem():
    return pl.BlockSpec(memory_space=pltpu.SMEM)


def project_kernel(tok_ref, gain_ref, wq_ref, wk_ref, wv_ref, out_ref):
    wide = tok_ref[...].astype(F32)
    normalized = (wide * gain_ref[...]).astype(BF16)
    q_cols = wq_ref.shape[1]
    for j in range(0, q_cols, 256):
        out_ref[:, j : j + 256] = jnp.dot(
            normalized, wq_ref[:, j : j + 256], preferred_element_type=F32
        )
    out_ref[:, q_cols : q_cols + 128] = jnp.dot(
        normalized, wk_ref[...], preferred_element_type=F32
    )
    out_ref[:, q_cols + 128 : q_cols + 256] = jnp.dot(
        normalized, wv_ref[...], preferred_element_type=F32
    )
    squares = jnp.sum(wide * wide, axis=1, keepdims=True)
    out_ref[:, q_cols + 256 : q_cols + 384] = jnp.broadcast_to(
        squares, (tok_ref.shape[0], 128)
    )


def project(tokens, gain, w_query, w_key, w_value):
    rows = tokens.shape[0]
    cols = w_query.shape[1] + 384
    return pl.pallas_call(
        project_kernel,
        out_shape=jax.ShapeDtypeStruct((rows, cols), F32),
        in_specs=[vmem()] * 5,
        out_specs=vmem(),
        compiler_params=params(),
        cost_estimate=pl.CostEstimate(
            flops=2 * rows * cols * tokens.shape[1], bytes_accessed=10 << 20, transcendentals=0
        ),
        name="project",
    )(tokens, gain, w_query, w_key, w_value)


def finish_kernel(features, part_ref, out_ref):
    q_cols = out_ref.shape[1]
    total = part_ref[0]
    for c in range(1, part_ref.shape[0]):
        total = total + part_ref[c]
    scale = lax.rsqrt(total[:, q_cols : q_cols + 1] / features + 1e-05)
    out_ref[...] = (total[:, :q_cols] * scale).astype(BF16)


def finish(parts, features):
    count, rows, cols = parts.shape
    return pl.pallas_call(
        lambda *refs: finish_kernel(features, *refs),
        out_shape=jax.ShapeDtypeStruct((rows, cols - 128), BF16),
        in_specs=[vmem()],
        out_specs=vmem(),
        compiler_params=params(),
        name="finish",
    )(parts)


def update(q_ref, m_ref, l_ref, acc_ref, row0, new_len, head, keys, values_ext, mask, const, zero):
    rows = pl.ds(row0, new_len)
    cols = slice(head * 128, head * 128 + 128)
    scores = lax.dot_general(q_ref[rows, cols], keys, NT, preferred_element_type=F32)
    scores = jnp.where(mask, scores, NEG_FILL)
    m_old = m_ref[head, rows, :]
    m_new = jnp.maximum(m_old, jnp.max(scores, axis=1, keepdims=True))
    shift = m_new * const
    alpha = jnp.exp2(m_old * const - shift)
    reps = scores.shape[1] // 128
    weights = jnp.exp2(scores * const - jnp.concatenate([shift] * reps, axis=1))
    if zero:
        weights = jnp.where(mask, weights, 0.0)
    mixed = jnp.dot(weights.astype(BF16), values_ext, preferred_element_type=F32)
    m_ref[head, rows, :] = m_new
    l_ref[head, rows, :] = l_ref[head, rows, :] * alpha + mixed[:, 128:]
    acc_ref[rows, cols] = acc_ref[rows, cols] * alpha + mixed[:, :128]


def prefix_part(meta_ref, base, q_ref, buf_ref, vx_ref, m_ref, l_ref, acc_ref, new_len, const):
    blocks = buf_ref.shape[0]
    heads = m_ref.shape[0]
    span = CHUNK * 128
    vx_ref[:, :128] = buf_ref[:, 1].reshape(blocks * 128, 128)
    vx_ref[:, 128:] = jnp.ones((blocks * 128, 128), BF16)
    sessions = q_ref.shape[0] // new_len
    for session in range(sessions):
        first = meta_ref[base + 2 * session]
        keys_live = meta_ref[base + 2 * session + 1]
        high = first * 128 + keys_live

        def body(step, carry, first=first, high=high, row0=session * new_len):
            wanted = first + step * CHUNK
            begin = jnp.minimum(wanted, blocks - CHUNK)
            keys = buf_ref[pl.ds(begin, CHUNK), 0].reshape(span, 128)
            values_ext = vx_ref[pl.ds(pl.multiple_of(begin * 128, 128), span), :]
            index = begin * 128 + lax.broadcasted_iota(jnp.int32, (1, span), 1)
            mask = (index >= wanted * 128) & (index < high)
            for head in range(heads):
                update(
                    q_ref, m_ref, l_ref, acc_ref, row0, new_len, head, keys, values_ext, mask,
                    const, False,
                )
            return carry

        lax.fori_loop(0, (keys_live + span - 1) // span, body, 0)


def pack_lanes(ref, rows):
    lane = lax.broadcasted_iota(jnp.int32, (rows, 128), 1)
    packed = jnp.zeros((rows, 128), F32)
    for head in range(ref.shape[0]):
        packed = jnp.where(lane == head, ref[head], packed)
    return packed


def first_kernel(
    new_len, const, meta_ref, quarter_refs, kv_refs, buf_ref, q_ref, acc_ref, mp_ref, lp_ref,
    vx_ref, m_ref, l_ref,
):
    tokens = q_ref.shape[0]
    part = quarter_refs[0].shape[0]
    rank = meta_ref[0]
    q_cols = q_ref.shape[1]
    for step, ref in enumerate(quarter_refs):
        place = lax.rem(rank + CTX - step, CTX)
        q_ref[pl.ds(pl.multiple_of(place * part, part), part), :] = ref[:, :q_cols]
    m_ref[...] = jnp.full(m_ref.shape, NEG_FILL, F32)
    l_ref[...] = jnp.zeros(l_ref.shape, F32)
    acc_ref[...] = jnp.zeros(acc_ref.shape, F32)
    own = quarter_refs[0]
    keys = own[:, q_cols : q_cols + 128]
    values_ext = jnp.concatenate(
        [own[:, q_cols + 128 : q_cols + 256], jnp.ones((part, 128), BF16)], axis=1
    )
    per_session = new_len // part
    row0 = pl.multiple_of(lax.div(rank, per_session) * new_len, new_len)
    offset = lax.rem(rank, per_session) * part
    token = lax.broadcasted_iota(jnp.int32, (new_len, part), 0)
    fresh = lax.broadcasted_iota(jnp.int32, (new_len, part), 1) + offset
    mask = fresh <= token
    for head in range(m_ref.shape[0]):
        update(
            q_ref, m_ref, l_ref, acc_ref, row0, new_len, head, keys, values_ext, mask, const, True
        )
    prefix_part(meta_ref, 1, q_ref, buf_ref, vx_ref, m_ref, l_ref, acc_ref, new_len, const)
    mp_ref[...] = pack_lanes(m_ref, tokens)
    lp_ref[...] = pack_lanes(l_ref, tokens)


def load_state(acc_in, mp_in, lp_in, acc_ref, m_ref, l_ref):
    acc_ref[...] = acc_in[...]
    shape = m_ref.shape[1:]
    for head in range(m_ref.shape[0]):
        m_ref[head] = jnp.broadcast_to(mp_in[:, head : head + 1], shape)
        l_ref[head] = jnp.broadcast_to(lp_in[:, head : head + 1], shape)


def middle_kernel(
    new_len, const, meta_ref, q_ref, buf_refs, acc_in, mp_in, lp_in, acc_ref, mp_ref, lp_ref,
    vx_ref, m_ref, l_ref,
):
    load_state(acc_in, mp_in, lp_in, acc_ref, m_ref, l_ref)
    for n, buf_ref in enumerate(buf_refs):
        prefix_part(
            meta_ref, 4 * n, q_ref, buf_ref, vx_ref, m_ref, l_ref, acc_ref, new_len, const
        )
    tokens = q_ref.shape[0]
    mp_ref[...] = pack_lanes(m_ref, tokens)
    lp_ref[...] = pack_lanes(l_ref, tokens)


def last_kernel(
    new_len, const, meta_ref, q_ref, buf_refs, acc_in, mp_in, lp_in, out_ref, vx_ref, m_ref, l_ref,
    acc_ref,
):
    load_state(acc_in, mp_in, lp_in, acc_ref, m_ref, l_ref)
    for n, buf_ref in enumerate(buf_refs):
        prefix_part(
            meta_ref, 4 * n, q_ref, buf_ref, vx_ref, m_ref, l_ref, acc_ref, new_len, const
        )
    tokens = q_ref.shape[0]
    heads = m_ref.shape[0]
    part = tokens // CTX
    for head in range(heads):
        cols = slice(head * 128, head * 128 + 128)
        total = l_ref[head]
        empty = total == 0.0
        safe = jnp.where(empty, 1.0, total)
        done = (acc_ref[:, cols] / safe).astype(BF16)
        for c in range(CTX):
            out_ref[c, :part, cols] = done[c * part : (c + 1) * part]
        m_ref[head] = jnp.where(empty, NEG_FILL, m_ref[head] * const + jnp.log2(safe))
    packed = pack_lanes(m_ref, tokens)
    row = lax.broadcasted_iota(jnp.int32, (16, heads * 128), 0)
    for c in range(CTX):
        turned = packed[c * part : (c + 1) * part].T
        line = jnp.concatenate([turned[h : h + 1] for h in range(heads)], axis=1)
        high = line.astype(BF16).astype(F32)
        rest = line - high
        mid = rest.astype(BF16).astype(F32)
        low = rest - mid
        tile = jnp.where(row == 0, high, jnp.where(row == 1, mid, jnp.where(row == 2, low, 0.0)))
        out_ref[c, part : part + 16, :] = tile.astype(BF16)


def attend_cost(blocks, tokens, heads):
    pairs = blocks * 128 * tokens // 2 * heads
    return pl.CostEstimate(flops=pairs * 512, bytes_accessed=8 << 20, transcendentals=pairs)


def scratch(tokens, heads, blocks):
    return [
        pltpu.VMEM((blocks * 128, 256), BF16),
        pltpu.VMEM((heads, tokens, 128), F32),
        pltpu.VMEM((heads, tokens, 128), F32),
    ]


def state_shapes(tokens, q_cols):
    return [
        jax.ShapeDtypeStruct((tokens, q_cols), F32),
        jax.ShapeDtypeStruct((tokens, 128), F32),
        jax.ShapeDtypeStruct((tokens, 128), F32),
    ]


def attend_first(meta, quarters, buf, new_len, const):
    part = quarters[0].shape[0]
    q_cols = quarters[0].shape[1] - 256
    tokens = part * CTX
    heads = q_cols // 128

    def kernel(meta_ref, a, b, c, d, buf_ref, q_ref, acc, mp, lp, vx, m, l):
        first_kernel(
            new_len, const, meta_ref, [a, b, c, d], None, buf_ref, q_ref, acc, mp, lp, vx, m, l
        )

    return pl.pallas_call(
        kernel,
        out_shape=[jax.ShapeDtypeStruct((tokens, q_cols), BF16)] + state_shapes(tokens, q_cols),
        in_specs=[smem()] + [vmem()] * 5,
        out_specs=[vmem()] * 4,
        scratch_shapes=scratch(tokens, heads, buf.shape[0]),
        compiler_params=params(),
        cost_estimate=attend_cost(buf.shape[0], tokens, heads),
        name="attend_own",
    )(meta, *quarters, buf)


def attend_more(meta, queries, bufs, state, new_len, const, last):
    tokens, q_cols = queries.shape
    heads = q_cols // 128
    count = len(bufs)

    def kernel(meta_ref, q_ref, *refs):
        buf_refs = refs[:count]
        acc_in, mp_in, lp_in = refs[count : count + 3]
        rest = refs[count + 3 :]
        body = last_kernel if last else middle_kernel
        body(new_len, const, meta_ref, q_ref, buf_refs, acc_in, mp_in, lp_in, *rest)

    if last:
        out_shape = jax.ShapeDtypeStruct((CTX, tokens // CTX + 16, q_cols), BF16)
        out_specs = vmem()
        more = [pltpu.VMEM((tokens, q_cols), F32)]
    else:
        out_shape = state_shapes(tokens, q_cols)
        out_specs = [vmem()] * 3
        more = []
    return pl.pallas_call(
        kernel,
        out_shape=out_shape,
        in_specs=[smem()] + [vmem()] * (4 + count),
        out_specs=out_specs,
        scratch_shapes=scratch(tokens, heads, bufs[0].shape[0]) + more,
        compiler_params=params(),
        cost_estimate=attend_cost(bufs[0].shape[0] * count, tokens, heads),
        name="attend_last" if last else "attend_near",
    )(meta, queries, *bufs, *state)


def combine_kernel(in_ref, out_ref):
    part, q_cols = out_ref.shape
    heads = q_cols // 128
    lines = []
    for c in range(CTX):
        tile = in_ref[c, part : part + 16, :].astype(F32)
        lines.append(tile[0:1] + tile[1:2] + tile[2:3])
    top = lines[0]
    for line in lines[1:]:
        top = jnp.maximum(top, line)
    shares = [jnp.exp2(line - top) for line in lines]
    total = shares[0] + shares[1] + shares[2] + shares[3]
    pieces = []
    for share in shares:
        share = share / total
        pieces += [share[:, h * 128 : h * 128 + 128] for h in range(heads)]
    pieces.append(jnp.zeros((128 - CTX * heads, 128), F32))
    turned = jnp.concatenate(pieces, axis=0).T
    for head in range(heads):
        cols = slice(head * 128, head * 128 + 128)
        mixed = jnp.zeros((part, 128), F32)
        for c in range(CTX):
            at = c * heads + head
            mixed = mixed + in_ref[c, :part, cols].astype(F32) * turned[:, at : at + 1]
        out_ref[:, cols] = mixed.astype(BF16)


def combine(arrived):
    count, rows, q_cols = arrived.shape
    return pl.pallas_call(
        combine_kernel,
        out_shape=jax.ShapeDtypeStruct((rows - 16, q_cols), BF16),
        in_specs=[vmem()],
        out_specs=vmem(),
        compiler_params=params(),
        name="combine",
    )(arrived)


def out_kernel(meta_ref, a, b, c, d, w_ref, own_ref, send_ref, rows_ref):
    rank = meta_ref[0]
    core = meta_ref[1]
    part = a.shape[0]
    half = own_ref.shape[2]

    @pl.when(pl.program_id(0) == 0)
    def _():
        for step, ref in enumerate((a, b, c, d)):
            place = lax.rem(rank + CTX - step, CTX)
            rows_ref[pl.ds(pl.multiple_of(place * part, part), part), :] = ref[...]

    product = jnp.dot(rows_ref[...], w_ref[...], preferred_element_type=F32)

    @pl.when(core == 0)
    def _():
        own_ref[0] = product[:, :half]
        send_ref[0] = product[:, half:].astype(BF16)

    @pl.when(core != 0)
    def _():
        own_ref[0] = product[:, half:]
        send_ref[0] = product[:, :half].astype(BF16)


def project_out(meta, quarters, w_out, planes):
    part, depth = quarters[0].shape
    tokens = part * CTX
    width = w_out.shape[1] // planes
    whole = pl.BlockSpec((part, depth), lambda i: (0, 0))
    return pl.pallas_call(
        out_kernel,
        grid=(planes,),
        out_shape=[
            jax.ShapeDtypeStruct((planes, tokens, width // 2), F32),
            jax.ShapeDtypeStruct((planes, tokens, width // 2), BF16),
        ],
        in_specs=[smem(), whole, whole, whole, whole, pl.BlockSpec((depth, width), lambda i: (0, i))],
        out_specs=[pl.BlockSpec((1, tokens, width // 2), lambda i: (i, 0, 0))] * 2,
        scratch_shapes=[pltpu.VMEM((tokens, depth), BF16)],
        compiler_params=params(),
        cost_estimate=pl.CostEstimate(
            flops=2 * tokens * depth * w_out.shape[1], bytes_accessed=8 << 20, transcendentals=0
        ),
        name="project_out",
    )(meta, *quarters, w_out)


def shifted(value, axis, step):
    size = lax.axis_size(axis)
    return lax.ppermute(value, axis, [(i, (i + step) % size) for i in range(size)])


def around(value, axis):
    return [value] + [shifted(value, axis, step) for step in (1, 2, 3)]


def local(
    tokens, norm_gain, w_query, w_key, w_value, w_out, kv_pool, block_table, prefix_len, write_slot
):
    groups = lax.axis_size("group")
    ranks = lax.axis_size("ctx")
    tp_size = lax.axis_size("tp")
    rank = lax.axis_index("ctx")
    group = lax.axis_index("group")
    core = lax.axis_index("tp") % 2
    pool_size = kv_pool.shape[0]
    sessions, list_len = block_table.shape
    sess_here = sessions // groups
    per_pair = sess_here * list_len // (groups * ranks)
    new_len = tokens.shape[0] // sess_here
    head_dim = kv_pool.shape[4]
    const = head_dim**-0.5 * LOG2E
    device_id = group * ranks + rank
    pool = kv_pool.reshape(pool_size, 2, head_dim, head_dim)

    table = block_table.reshape(groups, sess_here * list_len)
    steps = jnp.arange(groups, dtype=jnp.int32)
    send_table = jnp.roll(table, -group, axis=0)
    here = send_table // pool_size == device_id
    upper = jnp.triu(jnp.ones((sess_here * list_len,) * 2, BF16))
    order = jnp.dot(here.astype(BF16), upper, preferred_element_type=F32).astype(jnp.int32)
    wanted = jnp.arange(1, per_pair + 1, dtype=jnp.int32)
    picked = here[:, None, :] & (order[:, None, :] == wanted[None, :, None])
    send_index = jnp.sum(jnp.where(picked, send_table[:, None, :] % pool_size, 0), axis=2)
    blocks = [pool[send_index[step]] for step in range(groups)]
    arrived = [blocks[0]] + [shifted(blocks[step], "group", step) for step in range(1, groups)]

    mine = lax.dynamic_index_in_dim(table, group, 0, keepdims=False).reshape(sess_here, list_len)
    lengths = lax.dynamic_slice_in_dim(prefix_len, group * sess_here, sess_here)
    source = ((group - steps) % groups) * ranks + rank
    from_there = mine[None] // pool_size == source[:, None, None]
    slots = jnp.arange(list_len, dtype=jnp.int32)
    keys_in = jnp.clip(lengths[:, None] - slots[None, :] * head_dim, 0, head_dim)
    live_keys = jnp.sum(jnp.where(from_there, keys_in[None], 0), axis=2)
    counts = jnp.sum(from_there.astype(jnp.int32), axis=2)
    starts = jnp.cumsum(counts, axis=1) - counts
    meta = jnp.stack([starts, live_keys], axis=2).reshape(groups, 2 * sess_here).astype(jnp.int32)

    parts = project(tokens, norm_gain[None, :], w_query, w_key, w_value)
    part_rows = tokens.shape[0] // ranks
    parts = parts.reshape(ranks, part_rows, parts.shape[1])
    parts = lax.all_to_all(parts, "ctx", split_axis=0, concat_axis=0, tiled=True)
    fresh = finish(parts, tokens.shape[1] * ranks)
    quarters = around(fresh, "ctx")
    q_cols = w_query.shape[1]

    first_meta = jnp.concatenate([rank[None].astype(jnp.int32), meta[0]])
    queries, *state = attend_first(first_meta, quarters, arrived[0], new_len, const)
    near_meta = jnp.concatenate([meta[1], meta[3]])
    state = attend_more(
        near_meta, queries, [arrived[1], arrived[3]], state, new_len, const, False
    )
    partial = attend_more(meta[2], queries, [arrived[2]], state, new_len, const, True)
    partial = lax.all_to_all(partial, "ctx", split_axis=0, concat_axis=0, tiled=True)
    attended = combine(partial)

    planes = tp_size // 2
    out_meta = jnp.stack([rank, core]).astype(jnp.int32)
    own, send = project_out(out_meta, around(attended, "ctx"), w_out, planes)
    other = lax.ppermute(send, "tp", [(i, i ^ 1) for i in range(tp_size)])
    pair = (own + other.astype(F32)).astype(BF16)
    terms = lax.all_to_all(
        pair,
        "tp",
        split_axis=0,
        concat_axis=0,
        axis_index_groups=[[2 * z + c for z in range(planes)] for c in range(2)],
        tiled=True,
    )
    attention_out = jnp.sum(terms.astype(F32), axis=0).astype(BF16)

    block = fresh[:, q_cols:].reshape(part_rows, 2, 1, head_dim).transpose(1, 2, 0, 3)
    every = lax.all_gather(block, ("group", "ctx"))
    targets = write_slot.reshape(-1)
    placement = jnp.where(targets // pool_size == device_id, targets % pool_size, pool_size)
    new_pool = kv_pool.at[placement].set(every, mode="drop")
    return (attention_out, new_pool)


def solution(mesh):
    placed = (
        P("group", "ctx"),
        P("ctx"),
        P("ctx", "tp"),
        P("ctx", "tp"),
        P("ctx", "tp"),
        P("tp", "ctx"),
        P(("group", "ctx"), None, "tp", None, None),
        P(),
        P(),
        P(),
    )
    return jax.shard_map(
        local,
        mesh=mesh,
        in_specs=placed,
        out_specs=(P("group", ("ctx", "tp")), P(("group", "ctx"), None, "tp", None, None)),
        check_vma=False,
    )
```

time: 471 us -> 275 us (0.58)
  blocking collectives: 172 us -> 16.6 us
  matrix products: 85.7 us -> 0.25 us
  Pallas kernels: 0 us -> 83 us
  other arithmetic: 61.7 us -> 6.34 us
  waiting for transfers between devices: 66.3 us -> 102 us
  local copies, waits for them, and re-layouts: 53.3 us -> 31.4 us
  starting transfers between devices: 13.3 us -> 19.4 us
    psum x2 -> x0, blocking collectives: 156 us -> none  [the longest x1 141 us: local(): lax.psum((square_part, query_part, key_part, value_part), 'ctx')]
    dot_general x40 -> x1, matrix products: 85.7 us -> 0.25 us  [local(): jnp.dot(here.astype(BF16), upper, preferred_element_type=F32)]
    pallas_call x0 -> x7, Pallas kernels: none -> 83 us  [the longest x2 45.4 us: attend_more(): pl.pallas_call(kernel, out_shape=out_shape, in_specs=[smem()] + [vmem()]...]
    ppermute x0 -> x10, waiting for transfers between devices: none -> 48.9 us  [the longest x9 47.6 us: shifted(): lax.ppermute(value, axis, [(i, (i + step) % size) for i in range(size)])]
    psum x2 -> x0, waiting for transfers between devices: 45 us -> none  [the longest x1 45 us: local(): lax.psum((total_all * rescale, accum_all * rescale[..., None]), 'ctx')]
    reduce_sum x20 -> x3, other arithmetic: 43.1 us -> 1.35 us  [the longest x1 0.9 us: local(): attention_out = jnp.sum(terms.astype(F32), axis=0).astype(BF16)]
    all_gather x0 -> x1, waiting for transfers between devices: none -> 40.1 us  [local(): every = lax.all_gather(block, ('group', 'ctx'))]
    squeeze x18 -> x4, local copies, waits for them, and re-layouts: 17.7 us -> 0.87 us  [the longest x1 0.62 us: local(): meta[2]]
  transfers between devices with their start and end apart: 5 -> 13, of which waited for: 3 -> 9; matrix products, arithmetic and copies ran while one was open for 4% -> 11% of each run, Pallas kernels for 0% -> 17%
where the time goes in v1:
time: 275 us; the launch traced here: 273 us
  waiting for transfers between devices  102 us (37%)
  Pallas kernels  83 us (30%)
  local copies, waits for them, and re-layouts  31.4 us (11%)
  starting transfers between devices  19.4 us (7%)
  blocking collectives  16.6 us (6%)
  between operations  14.1 us (5%)
  other arithmetic  6.34 us (2%)
    ppermute x9, waiting for transfers between devices, shifted(): lax.ppermute(value, axis, [(i, (i + step) % size) for i in range(size)])  47.6 us
    pallas_call x2, Pallas kernels, attend_more(): pl.pallas_call(kernel, out_shape=out_shape, in_specs=[smem()] + [vmem()]...  45.4 us
    all_gather x1, waiting for transfers between devices, local(): every = lax.all_gather(block, ('group', 'ctx'))  40.1 us
    pallas_call x1, Pallas kernels, attend_first(): pl.pallas_call(kernel, out_shape=[jax.ShapeDtypeStruct((tokens, q_cols),...  17.5 us
    gather x4, local copies, waits for them, and re-layouts, local(): blocks = [pool[send_index[step]] for step in range(groups)]  17.4 us
    all_to_all x1, blocking collectives, local(): lax.all_to_all(partial, 'ctx', split_axis=0, concat_axis=0, tiled=True)  16.6 us
    all_to_all x1, waiting for transfers between devices, local(): lax.all_to_all(parts, 'ctx', split_axis=0, concat_axis=0, tiled=True)  13.2 us
    ppermute x9, starting transfers between devices, shifted(): lax.ppermute(value, axis, [(i, (i + step) % size) for i in range(size)])  9.54 us
  transfers between devices with their start and end apart: 13, of which 9 were waited for; matrix products, arithmetic and copies ran while one was open for 11% of the time, Pallas kernels for 17%

profile of v1, /device:TPU:24, one launch (start us, length us, event | category | flops | bytes accessed | tf_op | source)
XLA Modules:
  0.0 273.3 jit_solution(8008346913820987108)
XLA Ops:
  7.2 4.8 %copy.40 = bf16[64,2,1,128,128]{4,3,2,1,0:T(8,128)(2,1)} copy(bf16[64,2,1,128,128]{4,3,2,1,0:T(8,128)(2,1)} %param.16) | data formatting | bytes 8388608
  12.0 8.1 %project.1 = f32[512,1408]{1,0:T(8,128)} custom-call(bf16[512,2048]{1,0:T(8,128)(2,1)} %tok_ref.1, f32[1,2048]{1,0:T(1,128)} %bitcast.43, bf16[2048,1024]{1,0:T(8,128)(2,1)} %wq_ref.1, bf16[2048,128]{1,0:T(8,128)(2,1)} %wk_ref.1, bf16[2048,128]{1,0:T(8,128)(2,1)} %wv_ref.1), custom_call_target="tpu_custom_call" | custom-call | flops 2952790016 | bytes 10485760 | tf_op jit(solution)/shard_map/project/pallas_call | solution.py:53
  20.0 4.4 %all-to-all-start = ((f32[4,128,1408]{2,1,0:T(8,128)}), f32[4,128,1408]{2,1,0:T(8,128)S(1)}, u32[]{:S(2)}, u32[]{:S(2)}) async-start(f32[4,128,1408]{2,1,0:T(8,128)} %bitcast.38), calls=%async_computation | async-start | bytes 5767168 | tf_op jit(solution)/shard_map/all_to_all | solution.py:450
  24.6 0.3 convolution_convert_fusion
  24.9 0.2 select_reduce_fusion
  25.1 4.4 %gather_fusion.2 = bf16[32,2,128,128]{3,2,1,0:T(8,128)(2,1)} fusion(bf16[64,2,128,128]{3,2,1,0:T(8,128)(2,1)} %bitcast.32, s32[1024]{0:T(1024)S(1)} %pad_clamp_fusion.1), kind=kCustom, calls=%fused_computation.2 | custom fusion | bytes 4194432 | tf_op jit(solution)/shard_map/gather | solution.py:433
  29.5 0.2 collective-permute-start.4
  29.7 4.4 %gather_fusion.3 = bf16[32,2,128,128]{3,2,1,0:T(8,128)(2,1)} fusion(bf16[64,2,128,128]{3,2,1,0:T(8,128)(2,1)} %bitcast.33, s32[1024]{0:T(1024)S(1)} %pad_clamp_fusion), kind=kCustom, calls=%fused_computation.3 | custom fusion | bytes 4194432 | tf_op jit(solution)/shard_map/gather | solution.py:433
  34.1 1.8 collective-permute-start.5
  35.9 4.3 %gather_fusion.1 = bf16[32,2,128,128]{3,2,1,0:T(8,128)(2,1)} fusion(bf16[64,2,128,128]{3,2,1,0:T(8,128)(2,1)} %bitcast.34, s32[1024]{0:T(1024)S(1)} %pad_clamp_fusion.2), kind=kCustom, calls=%fused_computation.1 | custom fusion | bytes 4194432 | tf_op jit(solution)/shard_map/gather | solution.py:433
  40.2 1.2 collective-permute-start.3
  41.5 4.4 %gather_fusion = bf16[32,2,128,128]{3,2,1,0:T(8,128)(2,1)} fusion(bf16[64,2,128,128]{3,2,1,0:T(8,128)(2,1)} %bitcast.35, s32[1024]{0:T(1024)S(1)} %pad_clamp_fusion.3), kind=kCustom, calls=%fused_computation | custom fusion | bytes 4194432 | tf_op jit(solution)/shard_map/gather | solution.py:433
  45.9 0.1 dynamic_slice.12
  46.0 0.1 and_select_fusion
  46.0 13.2 %all-to-all-done.refs_0_ = f32[4,128,1408]{2,1,0:T(8,128)S(1)} async-done(((f32[4,128,1408]{2,1,0:T(8,128)}), f32[4,128,1408]{2,1,0:T(8,128)S(1)}, u32[]{:S(2)}, u32[]{:S(2)}) %all-to-all-start) | async-done | bytes 2883616 | tf_op jit(solution)/shard_map/all_to_all | solution.py:450
  59.2 1.5 copy-done
  60.8 2.7 finish.1.a
  63.5 0.6 collective-permute-start
  64.0 0.2 fusion.6
  64.3 2.1 collective-permute-start.1
  66.4 13.7 %collective-permute-done.b = bf16[128,1280]{1,0:T(8,128)(2,1)S(1)} collective-permute-done((bf16[128,1280]{1,0:T(8,128)(2,1)}, bf16[128,1280]{1,0:T(8,128)(2,1)S(1)}, u32[]{:S(2)}, u32[]{:S(2)}) %collective-permute-start) | collective-permute-done | bytes 327712 | tf_op jit(solution)/shard_map/ppermute | solution.py:398
  80.2 0.0 collective-permute-start.2
  80.2 0.1 fusion.10
  80.2 0.1 copy.31
  80.3 0.1 squeeze.27
  80.4 0.1 copy.32
  80.5 0.1 squeeze.30
  80.6 0.1 copy.33
  80.7 0.1 squeeze.31
  80.8 0.1 copy.30
  80.9 0.6 squeeze.26.meta_ref
  81.5 0.7 pad_add_fusion.2.meta_ref
  82.1 0.6 pad_add_fusion.3.meta_ref
  82.7 0.0 collective-permute-done.1.c
  82.7 4.7 %collective-permute-done.2.d = bf16[128,1280]{1,0:T(8,128)(2,1)S(1)} collective-permute-done((bf16[128,1280]{1,0:T(8,128)(2,1)}, bf16[128,1280]{1,0:T(8,128)(2,1)S(1)}, u32[]{:S(2)}, u32[]{:S(2)}) %collective-permute-start.2) | collective-permute-done | bytes 327712 | tf_op jit(solution)/shard_map/ppermute | solution.py:398
  87.4 0.7 copy-done.5
  88.2 17.5 %attend_own.1 = (bf16[512,1024]{1,0:T(8,128)(2,1)}, f32[512,1024]{1,0:T(8,128)}, f32[512,128]{1,0:T(8,128)}, f32[512,128]{1,0:T(8,128)}) custom-call(s32[5]{0:T(128)} %pad_add_fusion.2.meta_ref, bf16[128,1280]{1,0:T(8,128)(2,1)} %finish.1.a, bf16[128,1280]{1,0:T(8,128)(2,1)} %copy-done.3, bf16[128,1280]{1,0:T(8,128)(2,1)} %copy-done.4, ...), custom_call_target="tpu_custom_call" | custom-call | flops 4294967296 | bytes 8388608 | tf_op jit(solution)/shard_map/attend_own/pallas_call | solution.py:265
  105.6 0.0 collective-permute-done.4.refs_0_
  105.6 21.8 %collective-permute-done.5.refs_1_ = bf16[32,2,128,128]{3,2,1,0:T(8,128)(2,1)} collective-permute-done((bf16[32,2,128,128]{3,2,1,0:T(8,128)(2,1)}, bf16[32,2,128,128]{3,2,1,0:T(8,128)(2,1)}, u32[]{:S(2)}, u32[]{:S(2)}) %collective-permute-start.5) | collective-permute-done | bytes 2097184 | tf_op jit(solution)/shard_map/ppermute | solution.py:398
  127.4 26.0 %attend_near.1 = (f32[512,1024]{1,0:T(8,128)}, f32[512,128]{1,0:T(8,128)}, f32[512,128]{1,0:T(8,128)}) custom-call(s32[8]{0:T(128)} %pad_add_fusion.3.meta_ref, bf16[512,1024]{1,0:T(8,128)(2,1)} %get-tuple-element.11.q_ref, bf16[32,2,128,128]{3,2,1,0:T(8,128)(2,1)} %collective-permute-done.4.refs_0_, ...), custom_call_target="tpu_custom_call" | custom-call | flops 8589934592 | bytes 8388608 | tf_op jit(solution)/shard_map/attend_near/pallas_call | solution.py:297
  153.4 0.0 collective-permute-done.3.refs_0_
  153.4 19.5 %attend_last.1 = bf16[4,144,1024]{2,1,0:T(8,128)(2,1)} custom-call(s32[4]{0:T(128)} %squeeze.26.meta_ref, bf16[512,1024]{1,0:T(8,128)(2,1)} %get-tuple-element.11.q_ref, bf16[32,2,128,128]{3,2,1,0:T(8,128)(2,1)} %collective-permute-done.3.refs_0_, f32[512,1024]{1,0:T(8,128)} %get-tuple-element.15.refs_1_, f32[512,128]{1,0:T(8,128)} %get-tuple-element.16.refs_2_, ...), custom_call_target="tpu_custom_call" | custom-call | flops 4294967296 | bytes 8388608 | tf_op jit(solution)/shard_map/attend_last/pallas_call | solution.py:297
  172.9 16.6 %all_to_all.15.in_ref = bf16[4,144,1024]{2,1,0:T(8,128)(2,1)} all-to-all(bf16[4,144,1024]{2,1,0:T(8,128)(2,1)} %attend_last.1), channel_id=1, replica_groups=mesh['group'=4,'ctx'=4,'tp'=8] {'ctx'}, dimensions={0} | all-to-all | bytes 2359296 | tf_op jit(solution)/shard_map/all_to_all | solution.py:462
  189.5 2.8 %combine.1.a = bf16[128,1024]{1,0:T(8,128)(2,1)} custom-call(bf16[4,144,1024]{2,1,0:T(8,128)(2,1)} %all_to_all.15.in_ref), custom_call_target="tpu_custom_call" | custom-call | tf_op jit(solution)/shard_map/combine/pallas_call | solution.py:338
  192.3 0.6 collective-permute-start.6
  192.9 3.0 %collective-permute-start.7 = (bf16[128,1024]{1,0:T(8,128)(2,1)}, bf16[128,1024]{1,0:T(8,128)(2,1)S(1)}, u32[]{:S(2)}, u32[]{:S(2)}) collective-permute-start(bf16[128,1024]{1,0:T(8,128)(2,1)} %combine.1.a), channel_id=1, source_target_pairs={{0,16},{8,24},{16,0},{24,8},{1,17},{9,25},{17,1},{25,9},{2,18},{10... | collective-permute-start | bytes 786440 | tf_op jit(solution)/shard_map/ppermute | solution.py:398
  195.9 0.6 pad_add_fusion.1.meta_ref
  196.5 3.6 %collective-permute-done.6.b = bf16[128,1024]{1,0:T(8,128)(2,1)S(1)} collective-permute-done((bf16[128,1024]{1,0:T(8,128)(2,1)}, bf16[128,1024]{1,0:T(8,128)(2,1)S(1)}, u32[]{:S(2)}, u32[]{:S(2)}) %collective-permute-start.6) | collective-permute-done | bytes 262176 | tf_op jit(solution)/shard_map/ppermute | solution.py:398
  200.1 3.1 %collective-permute-done.7.c = bf16[128,1024]{1,0:T(8,128)(2,1)S(1)} collective-permute-done((bf16[128,1024]{1,0:T(8,128)(2,1)}, bf16[128,1024]{1,0:T(8,128)(2,1)S(1)}, u32[]{:S(2)}, u32[]{:S(2)}) %collective-permute-start.7) | collective-permute-done | bytes 262176 | tf_op jit(solution)/shard_map/ppermute | solution.py:398
  203.3 0.6 collective-permute-done.8.d
  203.8 0.1 copy-done.7
  204.0 0.7 copy-done.8
  204.7 6.5 %project_out.1 = (f32[4,512,256]{2,1,0:T(8,128)}, bf16[4,512,256]{2,1,0:T(8,128)(2,1)}) custom-call(s32[2]{0:T(128)} %pad_add_fusion.1.meta_ref, bf16[128,1024]{1,0:T(8,128)(2,1)} %combine.1.a, bf16[128,1024]{1,0:T(8,128)(2,1)} %copy-done.6, bf16[128,1024]{1,0:T(8,128)(2,1)} %copy-done.7, bf16[128,1024]{1,0:T(8,128)(2,1)} %copy-done.8, bf16[1024,2048]{1,0:T(8,128)(2,1)} %w_ref.1), custom_call_target="tpu_custom_call" | custom-call | flops 2147483648 | bytes 8388608 | tf_op jit(solution)/shard_map/project_out/pallas_call | solution.py:378
  211.1 0.8 slice.54
  212.0 0.6 copy.37
  212.6 0.0 all-gather.3.cloned.1.call-update
  212.7 1.3 collective-permute-done.9
  214.0 2.8 %add_convert_fusion = bf16[4,512,256]{2,1,0:T(8,128)(2,1)} fusion(f32[4,512,256]{2,1,0:T(8,128)} %get-tuple-element.18, bf16[4,512,256]{2,1,0:T(8,128)(2,1)S(1)} %collective-permute-done.9), kind=kLoop, calls=%fused_computation.5 | loop fusion | flops 1572864 | bytes 4194304 | tf_op jit(solution)/shard_map/convert_element_type | solution.py:469
  216.8 5.4 %all-to-all-start.2 = ((bf16[4,512,256]{2,1,0:T(8,128)(2,1)}), bf16[4,512,256]{2,1,0:T(8,128)(2,1)S(1)}, u32[]{:S(2)}, u32[]{:S(2)}) async-start(bf16[4,512,256]{2,1,0:T(8,128)(2,1)} %add_convert_fusion), calls=%async_computation.2 | async-start | bytes 2097152 | tf_op jit(solution)/shard_map/all_to_all | solution.py:470
  222.3 0.1 copy.34
  222.4 0.1 reshape.387
  222.5 40.1 %all-gather.3.cloned.1.call-done = bf16[32,1,128,128]{3,2,1,0:T(8,128)(2,1)} async-done(((bf16[2,1,128,128]{3,2,1,0:T(8,128)(2,1)}), bf16[32,1,128,128]{3,2,1,0:T(8,128)(2,1)}) %all-gather.3.cloned.1.call-update) | async-done | bytes 1048592 | tf_op jit(solution)/shard_map/all_gather | solution.py:481
  262.6 3.0 %scatter_fusion = bf16[64,2,128,128]{3,2,1,0:T(8,128)(2,1)} fusion(bf16[64,2,128,128]{3,2,1,0:T(8,128)(2,1)} %bitcast.36, s32[16]{0:T(128)S(1)} %fusion.20, bf16[16,2,128,128]{3,2,1,0:T(8,128)(2,1)} %bitcast.39), kind=kCustom, calls=%fused_computation.4 | custom fusion | bytes 3145792 | tf_op jit(solution)/shard_map/scatter | solution.py:484
  265.6 0.9 reduce_sum.42
  (38 shorter events, 0.3 us)
Async XLA Ops:
  20.0 4.4 %copy-start.1 = (s32[8,256]{1,0:T(8,128)S(1)}, s32[8,256]{1,0:T(8,128)}, u32[]{:S(2)}) copy-start(s32[8,256]{1,0:T(8,128)} %param.17) | copy-start | bytes 24580
  20.0 39.2 %all-to-all-start = ((f32[4,128,1408]{2,1,0:T(8,128)}), f32[4,128,1408]{2,1,0:T(8,128)S(1)}, u32[]{:S(2)}, u32[]{:S(2)}) async-start(f32[4,128,1408]{2,1,0:T(8,128)} %bitcast.38), calls=%async_computation | async-start | bytes 5767168 | tf_op jit(solution)/shard_map/all_to_all | solution.py:450
  24.5 238.1 %all-gather.3.cloned.1.call-start = ((), (), s32[]{:S(2)}) async-start(), calls=%async_computation.3 | async-start | bytes 1114112 | tf_op jit(solution)/shard_map/all_gather | solution.py:481
  29.5 76.1 %collective-permute-start.4 = (bf16[32,2,128,128]{3,2,1,0:T(8,128)(2,1)}, bf16[32,2,128,128]{3,2,1,0:T(8,128)(2,1)}, u32[]{:S(2)}, u32[]{:S(2)}) collective-permute-start(bf16[32,2,128,128]{3,2,1,0:T(8,128)(2,1)} %gather_fusion.2), channel_id=1, source_target_pairs={{0,32},{32,64},{64,96},{96,0},{1,33},{33,65},{65,97},{97,1},{2,34}... | collective-permute-start | bytes 6291464 | tf_op jit(solution)/shard_map/ppermute | solution.py:398
  34.1 93.3 %collective-permute-start.5 = (bf16[32,2,128,128]{3,2,1,0:T(8,128)(2,1)}, bf16[32,2,128,128]{3,2,1,0:T(8,128)(2,1)}, u32[]{:S(2)}, u32[]{:S(2)}) collective-permute-start(bf16[32,2,128,128]{3,2,1,0:T(8,128)(2,1)} %gather_fusion.3), channel_id=1, source_target_pairs={{0,96},{32,0},{64,32},{96,64},{1,97},{33,1},{65,33},{97,65},{2,98}... | collective-permute-start | bytes 6291464 | tf_op jit(solution)/shard_map/ppermute | solution.py:398
  40.2 113.2 %collective-permute-start.3 = (bf16[32,2,128,128]{3,2,1,0:T(8,128)(2,1)}, bf16[32,2,128,128]{3,2,1,0:T(8,128)(2,1)}, u32[]{:S(2)}, u32[]{:S(2)}) collective-permute-start(bf16[32,2,128,128]{3,2,1,0:T(8,128)(2,1)} %gather_fusion.1), channel_id=1, source_target_pairs={{0,64},{32,96},{64,0},{96,32},{1,65},{33,97},{65,1},{97,33},{2,66}... | collective-permute-start | bytes 6291464 | tf_op jit(solution)/shard_map/ppermute | solution.py:398
  41.5 4.4 %copy-start.9 = (s32[8]{0:T(128)S(1)}, s32[8]{0:T(128)}, u32[]{:S(2)}) copy-start(s32[8]{0:T(128)} %param.18) | copy-start | bytes 100
  59.2 1.6 copy-start
  63.5 16.7 %collective-permute-start = (bf16[128,1280]{1,0:T(8,128)(2,1)}, bf16[128,1280]{1,0:T(8,128)(2,1)S(1)}, u32[]{:S(2)}, u32[]{:S(2)}) collective-permute-start(bf16[128,1280]{1,0:T(8,128)(2,1)} %finish.1.a), channel_id=1, source_target_pairs={{0,8},{8,16},{16,24},{24,0},{1,9},{9,17},{17,25},{25,1},{2,10},{10... | collective-permute-start | bytes 983048 | tf_op jit(solution)/shard_map/ppermute | solution.py:398
  64.3 18.5 %collective-permute-start.1 = (bf16[128,1280]{1,0:T(8,128)(2,1)}, bf16[128,1280]{1,0:T(8,128)(2,1)S(1)}, u32[]{:S(2)}, u32[]{:S(2)}) collective-permute-start(bf16[128,1280]{1,0:T(8,128)(2,1)} %finish.1.a), channel_id=1, source_target_pairs={{0,16},{8,24},{16,0},{24,8},{1,17},{9,25},{17,1},{25,9},{2,18},{10... | collective-permute-start | bytes 983048 | tf_op jit(solution)/shard_map/ppermute | solution.py:398
  80.1 7.3 %copy-start.3 = (bf16[128,1280]{1,0:T(8,128)(2,1)}, bf16[128,1280]{1,0:T(8,128)(2,1)S(1)}, u32[]{:S(2)}) copy-start(bf16[128,1280]{1,0:T(8,128)(2,1)S(1)} %collective-permute-done.b) | copy-start | bytes 983044
  80.2 7.3 %collective-permute-start.2 = (bf16[128,1280]{1,0:T(8,128)(2,1)}, bf16[128,1280]{1,0:T(8,128)(2,1)S(1)}, u32[]{:S(2)}, u32[]{:S(2)}) collective-permute-start(bf16[128,1280]{1,0:T(8,128)(2,1)} %finish.1.a), channel_id=1, source_target_pairs={{0,24},{8,0},{16,8},{24,16},{1,25},{9,1},{17,9},{25,17},{2,26},{10... | collective-permute-start | bytes 983048 | tf_op jit(solution)/shard_map/ppermute | solution.py:398
  82.7 4.7 %copy-start.4 = (bf16[128,1280]{1,0:T(8,128)(2,1)}, bf16[128,1280]{1,0:T(8,128)(2,1)S(1)}, u32[]{:S(2)}) copy-start(bf16[128,1280]{1,0:T(8,128)(2,1)S(1)} %collective-permute-done.1.c) | copy-start | bytes 983044
  87.4 0.7 copy-start.5
  192.3 7.8 %collective-permute-start.6 = (bf16[128,1024]{1,0:T(8,128)(2,1)}, bf16[128,1024]{1,0:T(8,128)(2,1)S(1)}, u32[]{:S(2)}, u32[]{:S(2)}) collective-permute-start(bf16[128,1024]{1,0:T(8,128)(2,1)} %combine.1.a), channel_id=1, source_target_pairs={{0,8},{8,16},{16,24},{24,0},{1,9},{9,17},{17,25},{25,1},{2,10},{10... | collective-permute-start | bytes 786440 | tf_op jit(solution)/shard_map/ppermute | solution.py:398
  192.9 10.4 %collective-permute-start.7 = (bf16[128,1024]{1,0:T(8,128)(2,1)}, bf16[128,1024]{1,0:T(8,128)(2,1)S(1)}, u32[]{:S(2)}, u32[]{:S(2)}) collective-permute-start(bf16[128,1024]{1,0:T(8,128)(2,1)} %combine.1.a), channel_id=1, source_target_pairs={{0,16},{8,24},{16,0},{24,8},{1,17},{9,25},{17,1},{25,9},{2,18},{10... | collective-permute-start | bytes 786440 | tf_op jit(solution)/shard_map/ppermute | solution.py:398
  195.9 7.9 %collective-permute-start.8 = (bf16[128,1024]{1,0:T(8,128)(2,1)}, bf16[128,1024]{1,0:T(8,128)(2,1)S(1)}, u32[]{:S(2)}, u32[]{:S(2)}) collective-permute-start(bf16[128,1024]{1,0:T(8,128)(2,1)} %combine.1.a), channel_id=1, source_target_pairs={{0,24},{8,0},{16,8},{24,16},{1,25},{9,1},{17,9},{25,17},{2,26},{10... | collective-permute-start | bytes 786440 | tf_op jit(solution)/shard_map/ppermute | solution.py:398
  200.1 3.7 %copy-start.6 = (bf16[128,1024]{1,0:T(8,128)(2,1)}, bf16[128,1024]{1,0:T(8,128)(2,1)S(1)}, u32[]{:S(2)}) copy-start(bf16[128,1024]{1,0:T(8,128)(2,1)S(1)} %collective-permute-done.6.b) | copy-start | bytes 786436
  203.3 0.7 copy-start.7
  204.0 0.7 copy-start.8
  211.1 2.9 %collective-permute-start.9 = (bf16[4,512,256]{2,1,0:T(8,128)(2,1)}, bf16[4,512,256]{2,1,0:T(8,128)(2,1)S(1)}, u32[]{:S(2)}, u32[]{:S(2)}) collective-permute-start(bf16[4,512,256]{2,1,0:T(8,128)(2,1)} %get-tuple-element.19), channel_id=1, source_target_pairs={{0,1},{1,0},{2,3},{3,2},{4,5},{5,4},{6,7},{7,6},{8,9},{9,8},{10,11... | collective-permute-start | bytes 3145736 | tf_op jit(solution)/shard_map/ppermute | solution.py:468
  216.8 5.4 %copy-start.2 = (s32[8,2]{0,1:T(2,128)S(1)}, s32[8,2]{0,1:T(2,128)}, u32[]{:S(2)}) copy-start(s32[8,2]{0,1:T(2,128)} %param.19) | copy-start | bytes 196
  216.8 48.7 %all-to-all-start.2 = ((bf16[4,512,256]{2,1,0:T(8,128)(2,1)}), bf16[4,512,256]{2,1,0:T(8,128)(2,1)S(1)}, u32[]{:S(2)}, u32[]{:S(2)}) async-start(bf16[4,512,256]{2,1,0:T(8,128)(2,1)} %add_convert_fusion), calls=%async_computation.2 | async-start | bytes 2097152 | tf_op jit(solution)/shard_map/all_to_all | solution.py:470
Sparse Core Ops, SparseCore 0:
  212.8 49.7 all-gather.2

commit v2 on v1

v2 whole, which is shorter than its diff:
```python
import jax
import jax.numpy as jnp
from jax import lax
from jax.experimental import pallas as pl
from jax.experimental.pallas import tpu as pltpu
from jax.sharding import PartitionSpec as P

NEG_FILL = -1e30
LOG2E = 1.4426950408889634
F32 = jnp.float32
BF16 = jnp.bfloat16
VMEM_BYTES = 30 * 1024 * 1024
CHUNK = 4
TAIL = 2
ROOM = 60.0
CTX = 4
NT = (((1,), (1,)), ((), ()))


def params():
    return pltpu.CompilerParams(vmem_limit_bytes=VMEM_BYTES)


def vmem():
    return pl.BlockSpec(memory_space=pltpu.VMEM)


def smem():
    return pl.BlockSpec(memory_space=pltpu.SMEM)


def anywhere():
    return pl.BlockSpec(memory_space=pl.ANY)


def project_kernel(tok_ref, gain_ref, wq_ref, wk_ref, wv_ref, out_ref):
    wide = tok_ref[...].astype(F32)
    normalized = (wide * gain_ref[...]).astype(BF16)
    q_cols = wq_ref.shape[1]
    rows = tok_ref.shape[0]
    start = pl.program_id(0) == 0

    def add(cols, value):
        @pl.when(start)
        def _():
            out_ref[:, cols] = value

        @pl.when(jnp.logical_not(start))
        def _():
            out_ref[:, cols] += value

    for j in range(0, q_cols, 512):
        add(
            slice(j, j + 512),
            jnp.dot(normalized, wq_ref[:, j : j + 512], preferred_element_type=F32),
        )
    both = jnp.concatenate([wk_ref[...], wv_ref[...]], axis=1)
    add(slice(q_cols, q_cols + 256), jnp.dot(normalized, both, preferred_element_type=F32))
    squares = jnp.sum(wide * wide, axis=1, keepdims=True)
    add(slice(q_cols + 256, q_cols + 384), jnp.broadcast_to(squares, (rows, 128)))


def project(tokens, gain, w_query, w_key, w_value):
    rows, features = tokens.shape
    cols = w_query.shape[1] + 384
    deep = features // 4
    return pl.pallas_call(
        project_kernel,
        grid=(4,),
        out_shape=jax.ShapeDtypeStruct((rows, cols), F32),
        in_specs=[
            pl.BlockSpec((rows, deep), lambda i: (0, i)),
            pl.BlockSpec((1, deep), lambda i: (0, i)),
            pl.BlockSpec((deep, w_query.shape[1]), lambda i: (i, 0)),
            pl.BlockSpec((deep, 128), lambda i: (i, 0)),
            pl.BlockSpec((deep, 128), lambda i: (i, 0)),
        ],
        out_specs=pl.BlockSpec((rows, cols), lambda i: (0, 0)),
        compiler_params=params(),
        cost_estimate=pl.CostEstimate(
            flops=2 * rows * cols * features, bytes_accessed=10 << 20, transcendentals=0
        ),
        name="project",
    )(tokens, gain, w_query, w_key, w_value)


def finish_kernel(features, part_ref, out_ref, block_ref):
    q_cols = out_ref.shape[1]
    total = part_ref[0]
    for c in range(1, part_ref.shape[0]):
        total = total + part_ref[c]
    scale = lax.rsqrt(total[:, q_cols : q_cols + 1] / features + 1e-05)
    done = (total[:, :q_cols] * scale).astype(BF16)
    out_ref[...] = done
    block_ref[0] = done[:, q_cols - 256 : q_cols - 128]
    block_ref[1] = done[:, q_cols - 128 :]


def finish(parts, features):
    count, rows, cols = parts.shape
    return pl.pallas_call(
        lambda *refs: finish_kernel(features, *refs),
        out_shape=[
            jax.ShapeDtypeStruct((rows, cols - 128), BF16),
            jax.ShapeDtypeStruct((2, rows, 128), BF16),
        ],
        in_specs=[vmem()],
        out_specs=[vmem()] * 2,
        compiler_params=params(),
        name="finish",
    )(parts)


def pack_kernel(index_ref, pool_ref, out_ref, sem):
    for n in range(out_ref.shape[0]):
        pltpu.make_async_copy(pool_ref.at[index_ref[n]], out_ref.at[n], sem).start()
    pltpu.make_async_copy(out_ref, out_ref, sem).wait()


def pack(index, pool):
    count = index.shape[0]
    return pl.pallas_call(
        pack_kernel,
        out_shape=jax.ShapeDtypeStruct((count,) + pool.shape[1:], BF16),
        in_specs=[smem(), anywhere()],
        out_specs=anywhere(),
        scratch_shapes=[pltpu.SemaphoreType.DMA(())],
        compiler_params=params(),
        name="pack",
    )(index, pool)


def pack_lanes(ref, rows):
    lane = lax.broadcasted_iota(jnp.int32, (ref.shape[1], 128), 1)[: ref[0, rows, :].shape[0]]
    packed = jnp.zeros(lane.shape, F32)
    for head in range(ref.shape[0]):
        packed = jnp.where(lane == head, ref[head, rows, :], packed)
    return packed


def sweep(q_ref, rows, heads, keys, finish_head):
    pending = None
    for head in range(heads):
        cols = slice(head * 128, head * 128 + 128)
        scores = lax.dot_general(q_ref[rows, cols], keys, NT, preferred_element_type=F32)
        if pending is not None:
            finish_head(*pending)
        pending = (head, cols, scores)
    finish_head(*pending)


def moving(q_ref, m_ref, l_ref, acc_ref, rows, keys, values_ext, mask, const, zero):
    def finish_head(head, cols, scores):
        scores = jnp.where(mask, scores, NEG_FILL)
        m_old = m_ref[head, rows, :]
        m_new = jnp.maximum(m_old, jnp.max(scores, axis=1, keepdims=True) * const)
        alpha = jnp.exp2(m_old - m_new)
        reps = scores.shape[1] // 128
        weights = jnp.exp2(scores * const - jnp.concatenate([m_new] * reps, axis=1))
        if zero:
            weights = jnp.where(mask, weights, 0.0)
        mixed = jnp.dot(weights.astype(BF16), values_ext, preferred_element_type=F32)
        m_ref[head, rows, :] = m_new
        l_ref[head, rows, :] = l_ref[head, rows, :] * alpha + mixed[:, 128:]
        acc_ref[rows, cols] = acc_ref[rows, cols] * alpha + mixed[:, :128]

    sweep(q_ref, rows, m_ref.shape[0], keys, finish_head)


def steady(q_ref, m_ref, l_ref, acc_ref, rows, keys, values_ext, mask, const):
    def finish_head(head, cols, scores):
        if mask is not None:
            scores = jnp.where(mask, scores, NEG_FILL)
        reps = scores.shape[1] // 128
        shift = jnp.concatenate([m_ref[head, rows, :]] * reps, axis=1)
        weights = jnp.exp2(scores * const - shift)
        mixed = jnp.dot(weights.astype(BF16), values_ext, preferred_element_type=F32)
        l_ref[head, rows, :] += mixed[:, 128:]
        acc_ref[rows, cols] += mixed[:, :128]

    sweep(q_ref, rows, m_ref.shape[0], keys, finish_head)


def prefix_part(meta_ref, base, q_ref, qn_ref, kv_ref, vx_ref, m_ref, l_ref, acc_ref, new_len, const):
    blocks = kv_ref.shape[0]
    state = (q_ref, m_ref, l_ref, acc_ref)
    all_keys = kv_ref[:, 0].reshape(blocks * 128, 128)
    vx_ref[:, :128] = kv_ref[:, 1].reshape(blocks * 128, 128)
    vx_ref[:, 128:] = jnp.ones((blocks * 128, 128), BF16)
    norms = jnp.dot(all_keys * all_keys, jnp.ones((128, 128), BF16), preferred_element_type=F32)
    reach = jnp.sqrt(jnp.max(norms)) * (1.05 * const)

    def session_body(session, carry):
        row0 = pl.multiple_of(session * new_len, new_len)
        rows = pl.ds(row0, new_len)
        first = meta_ref[base + 2 * session]
        keys_live = meta_ref[base + 2 * session + 1]
        high = first * 128 + keys_live
        total = (keys_live + 127) // 128

        def enough():
            room = qn_ref[rows, :] * reach - pack_lanes(m_ref, rows)
            return (jnp.max(room) <= ROOM).astype(jnp.int32)

        def piece(wanted, count, masked):
            span = count * 128
            begin = jnp.minimum(wanted, blocks - count)
            keys = kv_ref[pl.ds(begin, count), 0].reshape(span, 128)
            values_ext = vx_ref[pl.ds(pl.multiple_of(begin * 128, 128), span), :]
            if not masked:
                return keys, values_ext, None
            index = begin * 128 + lax.broadcasted_iota(jnp.int32, (1, span), 1)
            return keys, values_ext, (index >= wanted * 128) & (index < high)

        def slow_more(now):
            return (now[0] < total) & (now[1] == 0)

        def slow(now):
            moving(*state, rows, *piece(first + now[0], CHUNK, True), const, False)
            return now[0] + CHUNK, enough()

        done, _ = lax.while_loop(slow_more, slow, (0, enough()))
        full = jnp.maximum(keys_live - done * 128, 0) // (CHUNK * 128)

        def fast(step, carry):
            steady(*state, rows, *piece(first + done + step * CHUNK, CHUNK, False), const)
            return carry

        lax.fori_loop(0, full, fast, 0)
        done = done + full * CHUNK

        def tail(step, carry):
            steady(*state, rows, *piece(first + done + step * TAIL, TAIL, True), const)
            return carry

        lax.fori_loop(0, (jnp.maximum(total - done, 0) + TAIL - 1) // TAIL, tail, 0)
        return carry

    lax.fori_loop(0, q_ref.shape[0] // new_len, session_body, 0)


def first_kernel(
    new_len, const, meta_ref, index_ref, a, b, c, d, pool_ref,
    q_ref, qn_ref, acc_ref, mp_ref, lp_ref, kv_ref, vx_ref, m_ref, l_ref, sem,
):
    blocks = kv_ref.shape[0]
    for n in range(blocks):
        pltpu.make_async_copy(pool_ref.at[index_ref[n]], kv_ref.at[n], sem).start()
    tokens, q_cols = q_ref.shape
    part = a.shape[0]
    heads = m_ref.shape[0]
    rank = meta_ref[0]
    for step, ref in enumerate((a, b, c, d)):
        place = lax.rem(rank + CTX - step, CTX)
        q_ref[pl.ds(pl.multiple_of(place * part, part), part), :] = ref[:, :q_cols]
    m_ref[...] = jnp.full(m_ref.shape, NEG_FILL, F32)
    l_ref[...] = jnp.zeros(l_ref.shape, F32)
    acc_ref[...] = jnp.zeros(acc_ref.shape, F32)
    lane = lax.broadcasted_iota(jnp.int32, (tokens, 128), 1)
    squares = jnp.zeros((tokens, 128), F32)
    for head in range(heads):
        wide = q_ref[:, head * 128 : head * 128 + 128].astype(F32)
        squares = jnp.where(lane == head, jnp.sum(wide * wide, axis=1, keepdims=True), squares)
    qn_ref[...] = jnp.sqrt(squares)
    keys = a[:, q_cols : q_cols + 128]
    values_ext = jnp.concatenate(
        [a[:, q_cols + 128 : q_cols + 256], jnp.ones((part, 128), BF16)], axis=1
    )
    per_session = new_len // part
    rows = pl.ds(pl.multiple_of(lax.div(rank, per_session) * new_len, new_len), new_len)
    offset = lax.rem(rank, per_session) * part
    token = lax.broadcasted_iota(jnp.int32, (new_len, part), 0)
    fresh = lax.broadcasted_iota(jnp.int32, (new_len, part), 1) + offset
    moving(q_ref, m_ref, l_ref, acc_ref, rows, keys, values_ext, fresh <= token, const, True)
    pltpu.make_async_copy(kv_ref, kv_ref, sem).wait()
    prefix_part(
        meta_ref, 1, q_ref, qn_ref, kv_ref, vx_ref, m_ref, l_ref, acc_ref, new_len, const
    )
    mp_ref[...] = pack_lanes(m_ref, slice(None))
    lp_ref[...] = pack_lanes(l_ref, slice(None))


def load_state(mp_in, lp_in, m_ref, l_ref):
    shape = m_ref.shape[1:]
    for head in range(m_ref.shape[0]):
        m_ref[head] = jnp.broadcast_to(mp_in[:, head : head + 1], shape)
        l_ref[head] = jnp.broadcast_to(lp_in[:, head : head + 1], shape)


def sources(
    new_len, const, meta_ref, q_ref, qn_ref, bufs, acc_in, mp_in, lp_in,
    acc_ref, kv_ref, vx_ref, m_ref, l_ref, sems,
):
    copies = []
    for n, buf in enumerate(bufs):
        copies.append(pltpu.make_async_copy(buf, kv_ref.at[n], sems.at[n]))
        copies[-1].start()
    acc_ref[...] = acc_in[...]
    load_state(mp_in, lp_in, m_ref, l_ref)
    for n, copy in enumerate(copies):
        copy.wait()
        prefix_part(
            meta_ref, 4 * n, q_ref, qn_ref, kv_ref.at[n], vx_ref, m_ref, l_ref, acc_ref, new_len,
            const,
        )


def near_kernel(
    new_len, const, meta_ref, q_ref, qn_ref, acc_in, mp_in, lp_in, buf_a, buf_b, pool_ref,
    acc_ref, mp_ref, lp_ref, pool_out, kv_ref, vx_ref, m_ref, l_ref, sems, pool_sem,
):
    keep = pltpu.make_async_copy(pool_ref, pool_out, pool_sem)
    keep.start()
    sources(
        new_len, const, meta_ref, q_ref, qn_ref, (buf_a, buf_b), acc_in, mp_in, lp_in,
        acc_ref, kv_ref, vx_ref, m_ref, l_ref, sems,
    )
    mp_ref[...] = pack_lanes(m_ref, slice(None))
    lp_ref[...] = pack_lanes(l_ref, slice(None))
    keep.wait()


def last_kernel(
    new_len, const, meta_ref, place_ref, q_ref, qn_ref, acc_in, mp_in, lp_in, buf,
    new_a, new_b, new_c, new_d, pool_in, out_ref, pool_out,
    acc_ref, kv_ref, vx_ref, m_ref, l_ref, sems, new_sems,
):
    def place(act):
        count = new_a.shape[0]
        for n, ref in enumerate((new_a, new_b, new_c, new_d)):
            for i in range(count):
                at = n * count + i
                slot = place_ref[at]

                @pl.when(slot >= 0)
                def _(ref=ref, i=i, at=at, slot=slot):
                    act(pltpu.make_async_copy(ref.at[i], pool_out.at[slot], new_sems.at[at]))

    place(lambda copy: copy.start())
    sources(
        new_len, const, meta_ref, q_ref, qn_ref, (buf,), acc_in, mp_in, lp_in,
        acc_ref, kv_ref, vx_ref, m_ref, l_ref, sems,
    )
    tokens = q_ref.shape[0]
    heads = m_ref.shape[0]
    part = tokens // CTX
    for head in range(heads):
        cols = slice(head * 128, head * 128 + 128)
        total = l_ref[head]
        empty = total == 0.0
        safe = jnp.where(empty, 1.0, total)
        done = (acc_ref[:, cols] / safe).astype(BF16)
        for c in range(CTX):
            out_ref[c, :part, cols] = done[c * part : (c + 1) * part]
        m_ref[head] = jnp.where(empty, NEG_FILL, m_ref[head] + jnp.log2(safe))
    packed = pack_lanes(m_ref, slice(None))
    row = lax.broadcasted_iota(jnp.int32, (16, heads * 128), 0)
    for c in range(CTX):
        turned = packed[c * part : (c + 1) * part].T
        line = jnp.concatenate([turned[h : h + 1] for h in range(heads)], axis=1)
        high = line.astype(BF16).astype(F32)
        rest = line - high
        mid = rest.astype(BF16).astype(F32)
        low = rest - mid
        tile = jnp.where(row == 0, high, jnp.where(row == 1, mid, jnp.where(row == 2, low, 0.0)))
        out_ref[c, part : part + 16, :] = tile.astype(BF16)
    place(lambda copy: copy.wait())


def attend_cost(blocks, tokens, heads):
    pairs = blocks * 128 * tokens // 2 * heads
    return pl.CostEstimate(flops=pairs * 512, bytes_accessed=8 << 20, transcendentals=pairs)


def scratch(tokens, heads, blocks, lead=()):
    return [
        pltpu.VMEM(lead + (blocks, 2, 128, 128), BF16),
        pltpu.VMEM((blocks * 128, 256), BF16),
        pltpu.VMEM((heads, tokens, 128), F32),
        pltpu.VMEM((heads, tokens, 128), F32),
    ]


def state_shapes(tokens, q_cols):
    return [
        jax.ShapeDtypeStruct((tokens, q_cols), F32),
        jax.ShapeDtypeStruct((tokens, 128), F32),
        jax.ShapeDtypeStruct((tokens, 128), F32),
    ]


def attend_own(meta, index, quarters, pool, new_len, const):
    part = quarters[0].shape[0]
    q_cols = quarters[0].shape[1] - 256
    tokens = part * CTX
    heads = q_cols // 128
    blocks = index.shape[0]
    return pl.pallas_call(
        lambda *refs: first_kernel(new_len, const, *refs),
        out_shape=[
            jax.ShapeDtypeStruct((tokens, q_cols), BF16),
            jax.ShapeDtypeStruct((tokens, 128), F32),
        ]
        + state_shapes(tokens, q_cols),
        in_specs=[smem(), smem()] + [vmem()] * 4 + [anywhere()],
        out_specs=[vmem()] * 5,
        scratch_shapes=scratch(tokens, heads, blocks) + [pltpu.SemaphoreType.DMA(())],
        compiler_params=params(),
        cost_estimate=attend_cost(blocks, tokens, heads),
        name="attend_own",
    )(meta, index, *quarters, pool)


def attend_near(meta, queries, norms, state, bufs, pool, new_len, const):
    tokens, q_cols = queries.shape
    heads = q_cols // 128
    blocks = bufs[0].shape[0]
    return pl.pallas_call(
        lambda *refs: near_kernel(new_len, const, *refs),
        out_shape=state_shapes(tokens, q_cols) + [jax.ShapeDtypeStruct(pool.shape, BF16)],
        in_specs=[smem()] + [vmem()] * 5 + [anywhere()] * 3,
        out_specs=[vmem()] * 3 + [anywhere()],
        scratch_shapes=scratch(tokens, heads, blocks, (2,))
        + [pltpu.SemaphoreType.DMA((2,)), pltpu.SemaphoreType.DMA(())],
        compiler_params=params(),
        cost_estimate=attend_cost(2 * blocks, tokens, heads),
        name="attend_near",
    )(meta, queries, norms, *state, *bufs, pool)


def attend_last(meta, places, queries, norms, state, buf, news, pool, new_len, const):
    tokens, q_cols = queries.shape
    heads = q_cols // 128
    blocks = buf.shape[0]
    return pl.pallas_call(
        lambda *refs: last_kernel(new_len, const, *refs),
        out_shape=[
            jax.ShapeDtypeStruct((CTX, tokens // CTX + 16, q_cols), BF16),
            jax.ShapeDtypeStruct(pool.shape, BF16),
        ],
        in_specs=[smem(), smem()] + [vmem()] * 5 + [anywhere()] * 6,
        out_specs=[vmem(), anywhere()],
        scratch_shapes=[pltpu.VMEM((tokens, q_cols), F32)]
        + scratch(tokens, heads, blocks, (1,))
        + [pltpu.SemaphoreType.DMA((1,)), pltpu.SemaphoreType.DMA((places.shape[0],))],
        input_output_aliases={12: 1},
        compiler_params=params(),
        cost_estimate=attend_cost(blocks, tokens, heads),
        name="attend_last",
    )(meta, places, queries, norms, *state, buf, *news, pool)


def combine_kernel(in_ref, out_ref):
    part, q_cols = out_ref.shape
    heads = q_cols // 128
    lines = []
    for c in range(CTX):
        tile = in_ref[c, part : part + 16, :].astype(F32)
        lines.append(tile[0:1] + tile[1:2] + tile[2:3])
    top = lines[0]
    for line in lines[1:]:
        top = jnp.maximum(top, line)
    shares = [jnp.exp2(line - top) for line in lines]
    total = shares[0] + shares[1] + shares[2] + shares[3]
    pieces = []
    for share in shares:
        share = share / total
        pieces += [share[:, h * 128 : h * 128 + 128] for h in range(heads)]
    pieces.append(jnp.zeros((128 - CTX * heads, 128), F32))
    turned = jnp.concatenate(pieces, axis=0).T
    for head in range(heads):
        cols = slice(head * 128, head * 128 + 128)
        mixed = jnp.zeros((part, 128), F32)
        for c in range(CTX):
            at = c * heads + head
            mixed = mixed + in_ref[c, :part, cols].astype(F32) * turned[:, at : at + 1]
        out_ref[:, cols] = mixed.astype(BF16)


def combine(arrived):
    count, rows, q_cols = arrived.shape
    return pl.pallas_call(
        combine_kernel,
        out_shape=jax.ShapeDtypeStruct((rows - 16, q_cols), BF16),
        in_specs=[vmem()],
        out_specs=vmem(),
        compiler_params=params(),
        name="combine",
    )(arrived)


def out_kernel(meta_ref, a, b, c, d, w_ref, own_ref, send_ref, rows_ref):
    rank = meta_ref[0]
    core = meta_ref[1]
    part = a.shape[0]
    half = own_ref.shape[2]

    @pl.when(pl.program_id(0) == 0)
    def _():
        for step, ref in enumerate((a, b, c, d)):
            place = lax.rem(rank + CTX - step, CTX)
            rows_ref[pl.ds(pl.multiple_of(place * part, part), part), :] = ref[...]

    product = jnp.dot(rows_ref[...], w_ref[...], preferred_element_type=F32)

    @pl.when(core == 0)
    def _():
        own_ref[0] = product[:, :half]
        send_ref[0] = product[:, half:].astype(BF16)

    @pl.when(core != 0)
    def _():
        own_ref[0] = product[:, half:]
        send_ref[0] = product[:, :half].astype(BF16)


def project_out(meta, quarters, w_out, planes):
    part, depth = quarters[0].shape
    tokens = part * CTX
    width = w_out.shape[1] // planes
    whole = pl.BlockSpec((part, depth), lambda i: (0, 0))
    return pl.pallas_call(
        out_kernel,
        grid=(planes,),
        out_shape=[
            jax.ShapeDtypeStruct((planes, tokens, width // 2), F32),
            jax.ShapeDtypeStruct((planes, tokens, width // 2), BF16),
        ],
        in_specs=[smem(), whole, whole, whole, whole, pl.BlockSpec((depth, width), lambda i: (0, i))],
        out_specs=[pl.BlockSpec((1, tokens, width // 2), lambda i: (i, 0, 0))] * 2,
        scratch_shapes=[pltpu.VMEM((tokens, depth), BF16)],
        compiler_params=params(),
        cost_estimate=pl.CostEstimate(
            flops=2 * tokens * depth * w_out.shape[1], bytes_accessed=8 << 20, transcendentals=0
        ),
        name="project_out",
    )(meta, *quarters, w_out)


def shifted(value, axis, step):
    size = lax.axis_size(axis)
    return lax.ppermute(value, axis, [(i, (i + step) % size) for i in range(size)])


def around(value, axis):
    return [value] + [shifted(value, axis, step) for step in (1, 2, 3)]


def local(
    tokens, norm_gain, w_query, w_key, w_value, w_out, kv_pool, block_table, prefix_len, write_slot
):
    groups = lax.axis_size("group")
    ranks = lax.axis_size("ctx")
    tp_size = lax.axis_size("tp")
    rank = lax.axis_index("ctx")
    group = lax.axis_index("group")
    core = lax.axis_index("tp") % 2
    pool_size = kv_pool.shape[0]
    sessions, list_len = block_table.shape
    sess_here = sessions // groups
    per_pair = sess_here * list_len // (groups * ranks)
    new_len = tokens.shape[0] // sess_here
    head_dim = kv_pool.shape[4]
    const = head_dim**-0.5 * LOG2E
    device_id = group * ranks + rank
    pool = kv_pool.reshape(pool_size, 2, head_dim, head_dim)

    table = block_table.reshape(groups, sess_here * list_len)
    steps = jnp.arange(groups, dtype=jnp.int32)
    send_table = jnp.roll(table, -group, axis=0)
    here = send_table // pool_size == device_id
    upper = jnp.triu(jnp.ones((sess_here * list_len,) * 2, BF16))
    order = jnp.dot(here.astype(BF16), upper, preferred_element_type=F32).astype(jnp.int32)
    wanted = jnp.arange(1, per_pair + 1, dtype=jnp.int32)
    picked = here[:, None, :] & (order[:, None, :] == wanted[None, :, None])
    send_index = jnp.sum(jnp.where(picked, send_table[:, None, :] % pool_size, 0), axis=2)
    blocks = {step: pack(send_index[step], pool) for step in (1, 3, 2)}
    arrived = {step: shifted(blocks[step], "group", step) for step in (1, 3, 2)}

    mine = lax.dynamic_index_in_dim(table, group, 0, keepdims=False).reshape(sess_here, list_len)
    lengths = lax.dynamic_slice_in_dim(prefix_len, group * sess_here, sess_here)
    source = ((group - steps) % groups) * ranks + rank
    from_there = mine[None] // pool_size == source[:, None, None]
    slots = jnp.arange(list_len, dtype=jnp.int32)
    keys_in = jnp.clip(lengths[:, None] - slots[None, :] * head_dim, 0, head_dim)
    live_keys = jnp.sum(jnp.where(from_there, keys_in[None], 0), axis=2)
    counts = jnp.sum(from_there.astype(jnp.int32), axis=2)
    starts = jnp.cumsum(counts, axis=1) - counts
    meta = jnp.stack([starts, live_keys], axis=2).reshape(groups, 2 * sess_here).astype(jnp.int32)

    tokens, _ = lax.optimization_barrier((tokens, blocks))
    parts = project(tokens, norm_gain[None, :], w_query, w_key, w_value)
    part_rows = tokens.shape[0] // ranks
    parts = parts.reshape(ranks, part_rows, parts.shape[1])
    parts = lax.all_to_all(parts, "ctx", split_axis=0, concat_axis=0, tiled=True)
    fresh, block = finish(parts, tokens.shape[1] * ranks)
    quarters = around(fresh, "ctx")
    news = around(jnp.stack(around(block, "group")), "ctx")
    targets = write_slot.reshape(groups, ranks)
    targets = jnp.stack(
        [targets[(group - g) % groups, (rank - c) % ranks] for c in range(ranks) for g in range(groups)]
    )
    places = jnp.where(targets // pool_size == device_id, targets % pool_size, -1)

    first_meta = jnp.concatenate([rank[None].astype(jnp.int32), meta[0]])
    queries, norms, *state = attend_own(
        first_meta, send_index[0], quarters, pool, new_len, const
    )
    near_meta = jnp.concatenate([meta[1], meta[3]])
    *state, new_pool = attend_near(
        near_meta, queries, norms, state, [arrived[1], arrived[3]], pool, new_len, const
    )
    partial, new_pool = attend_last(
        meta[2], places, queries, norms, state, arrived[2], news, new_pool, new_len, const
    )
    partial = lax.all_to_all(partial, "ctx", split_axis=0, concat_axis=0, tiled=True)
    attended = combine(partial)

    planes = tp_size // 2
    out_meta = jnp.stack([rank, core]).astype(jnp.int32)
    own, send = project_out(out_meta, around(attended, "ctx"), w_out, planes)
    other = lax.ppermute(send, "tp", [(i, i ^ 1) for i in range(tp_size)])
    pair = (own + other.astype(F32)).astype(BF16)
    terms = lax.all_to_all(
        pair,
        "tp",
        split_axis=0,
        concat_axis=0,
        axis_index_groups=[[2 * z + c for z in range(planes)] for c in range(2)],
        tiled=True,
    )
    attention_out = jnp.sum(terms.astype(F32), axis=0).astype(BF16)

    new_pool = new_pool.reshape(kv_pool.shape)
    return (attention_out, new_pool)


def solution(mesh):
    placed = (
        P("group", "ctx"),
        P("ctx"),
        P("ctx", "tp"),
        P("ctx", "tp"),
        P("ctx", "tp"),
        P("tp", "ctx"),
        P(("group", "ctx"), None, "tp", None, None),
        P(),
        P(),
        P(),
    )
    return jax.shard_map(
        local,
        mesh=mesh,
        in_specs=placed,
        out_specs=(P("group", ("ctx", "tp")), P(("group", "ctx"), None, "tp", None, None)),
        check_vma=False,
    )
```

time: 275 us -> 296 us (1.076)
  blocking collectives: 16.6 us -> 39.9 us
  Pallas kernels: 83 us -> 99.2 us
  between operations: 14.1 us -> 0.91 us
  waiting for transfers between devices: 102 us -> 109 us
  local copies, waits for them, and re-layouts: 31.4 us -> 24.6 us
  other arithmetic: 6.34 us -> 2.26 us
    all_gather x1 -> x0, waiting for transfers between devices: 40.1 us -> none  [local(): every = lax.all_gather(block, ('group', 'ctx'))]
    ppermute x9 -> x15, waiting for transfers between devices: 47.6 us -> 74.9 us  [shifted(): lax.ppermute(value, axis, [(i, (i + step) % size) for i in range(size)])]
    pallas_call x5 -> x8, Pallas kernels: 73.7 us -> 94.3 us  [the longest x1 34.8 us: attend_near(): pl.pallas_call(lambda *refs: near_kernel(new_len, const, *refs), out_shap...]
    all_to_all x0 -> x1, blocking collectives: none -> 20.5 us  [local(): lax.all_to_all(pair, 'tp', split_axis=0, concat_axis=0, axis_index_groups...]
    all_to_all x1, waiting for transfers between devices: 13.2 us -> 31 us  [local(): lax.all_to_all(parts, 'ctx', split_axis=0, concat_axis=0, tiled=True)]
    gather x4 -> x0, local copies, waits for them, and re-layouts: 17.4 us -> none  [local(): blocks = [pool[send_index[step]] for step in range(groups)]]
    another operation x0 -> x1, local copies, waits for them, and re-layouts: none -> 10 us  [local(): jnp.stack([targets[(group - g) % groups, (rank - c) % ranks] for c in ran...]
    ppermute x9 -> x15, starting transfers between devices: 9.54 us -> 15.5 us  [shifted(): lax.ppermute(value, axis, [(i, (i + step) % size) for i in range(size)])]
  transfers between devices with their start and end apart: 13 -> 17, of which waited for: 9 -> 9; matrix products, arithmetic and copies ran while one was open for 11% -> 4% of each run, Pallas kernels for 17% -> 19%
where the time goes in v2:
time: 296 us
  waiting for transfers between devices  109 us (37%)
  Pallas kernels  99.2 us (34%)
  blocking collectives  39.9 us (13%)
  local copies, waits for them, and re-layouts  24.6 us (8%)
  starting transfers between devices  20 us (7%)
    ppermute x15, waiting for transfers between devices, shifted(): lax.ppermute(value, axis, [(i, (i + step) % size) for i in range(size)])  74.9 us
    pallas_call x1, Pallas kernels, attend_near(): pl.pallas_call(lambda *refs: near_kernel(new_len, const, *refs), out_shap...  34.8 us
    all_to_all x1, waiting for transfers between devices, local(): lax.all_to_all(parts, 'ctx', split_axis=0, concat_axis=0, tiled=True)  31 us
    pallas_call x1, Pallas kernels, attend_own(): pl.pallas_call(lambda *refs: first_kernel(new_len, const, *refs), out_sha...  21.8 us
    all_to_all x1, blocking collectives, local(): lax.all_to_all(pair, 'tp', split_axis=0, concat_axis=0, axis_index_groups...  20.5 us
    pallas_call x1, Pallas kernels, attend_last(): pl.pallas_call(lambda *refs: last_kernel(new_len, const, *refs), out_shap...  20 us
    all_to_all x1, blocking collectives, local(): lax.all_to_all(partial, 'ctx', split_axis=0, concat_axis=0, tiled=True)  19.3 us
    ppermute x15, starting transfers between devices, shifted(): lax.ppermute(value, axis, [(i, (i + step) % size) for i in range(size)])  15.5 us
  transfers between devices with their start and end apart: 17, of which 9 were waited for; matrix products, arithmetic and copies ran while one was open for 4% of the time, Pallas kernels for 19%

profile of v2, /device:TPU:24, one launch (start us, length us, event | category | flops | bytes accessed | tf_op | source)
XLA Modules:
  0.0 295.6 jit_solution(2265798515626493755)
XLA Ops:
  0.7 0.7 reshape.162
  1.5 0.3 convolution_convert_fusion
  1.7 0.2 select_reduce_fusion
  2.0 2.2 copy-done
  4.2 3.4 %pack.3 = bf16[32,2,128,128]{3,2,1,0:T(8,128)(2,1)S(1)} custom-call(s32[32]{0:T(128)S(1)} %get-tuple-element.48.index_ref, bf16[64,2,128,128]{3,2,1,0:T(8,128)(2,1)S(1)} %bitcast.40), custom_call_target="tpu_custom_call" | custom-call | tf_op jit(solution)/shard_map/pack/pallas_call | solution.py:122
  7.5 1.3 copy-done.6
  8.8 3.4 %pack.4 = bf16[32,2,128,128]{3,2,1,0:T(8,128)(2,1)S(1)} custom-call(s32[32]{0:T(128)S(1)} %get-tuple-element.47.index_ref, bf16[64,2,128,128]{3,2,1,0:T(8,128)(2,1)S(1)} %bitcast.41), custom_call_target="tpu_custom_call" | custom-call | tf_op jit(solution)/shard_map/pack/pallas_call | solution.py:122
  12.2 1.3 copy-done.4
  13.5 3.4 %pack.5 = bf16[32,2,128,128]{3,2,1,0:T(8,128)(2,1)S(1)} custom-call(s32[32]{0:T(128)S(1)} %get-tuple-element.46.index_ref, bf16[64,2,128,128]{3,2,1,0:T(8,128)(2,1)S(1)} %bitcast.42), custom_call_target="tpu_custom_call" | custom-call | tf_op jit(solution)/shard_map/pack/pallas_call | solution.py:122
  16.9 1.4 copy-done.5
  18.3 7.5 %project.1 = f32[512,1408]{1,0:T(8,128)S(1)} custom-call(bf16[512,2048]{1,0:T(8,128)(2,1)S(1)} %copy-done.9, f32[1,2048]{1,0:T(1,128)S(1)} %bitcast.47, bf16[2048,1024]{1,0:T(8,128)(2,1)S(1)} %copy-done.7, bf16[2048,128]{1,0:T(8,128)(2,1)S(1)} %copy-done.10, bf16[2048,128]{1,0:T(8,128)(2,1)S(1)} %copy-done.11), custom_call_target="tpu_custom_call" | custom-call | flops 2952790016 | bytes 10485760 | tf_op jit(solution)/shard_map/project/pallas_call | solution.py:67
  25.9 1.6 copy-done.3
  27.4 4.4 %all-to-all-start = ((f32[4,128,1408]{2,1,0:T(8,128)}), f32[4,128,1408]{2,1,0:T(8,128)S(1)}, u32[]{:S(2)}, u32[]{:S(2)}) async-start(f32[4,128,1408]{2,1,0:T(8,128)} %bitcast.45), calls=%async_computation | async-start | bytes 5767168 | tf_op jit(solution)/shard_map/all_to_all | solution.py:595
  31.9 0.2 collective-permute-start.3
  32.1 1.8 collective-permute-start.4
  33.9 1.2 collective-permute-start.5
  35.3 0.2 fusion.6
  35.6 31.0 %all-to-all-done.refs_0_ = f32[4,128,1408]{2,1,0:T(8,128)S(1)} async-done(((f32[4,128,1408]{2,1,0:T(8,128)}), f32[4,128,1408]{2,1,0:T(8,128)S(1)}, u32[]{:S(2)}, u32[]{:S(2)}) %all-to-all-start) | async-done | bytes 2883616 | tf_op jit(solution)/shard_map/all_to_all | solution.py:595
  66.6 0.1 finish.1
  66.8 0.6 collective-permute-start
  67.4 0.7 collective-permute-start.8
  68.2 0.1 copy.25
  68.3 0.1 squeeze.26.refs_0_
  68.4 0.1 copy.26
  68.5 0.1 reshape.163
  68.6 0.1 copy.27
  68.7 0.1 squeeze.27
  68.7 0.1 copy.29
  68.8 0.1 squeeze.33
  68.9 0.1 copy.28
  69.0 0.1 squeeze.32
  69.1 0.7 fusion.18
  69.8 10.0 %stack.39 = s32[16]{0:T(128)S(1)} concatenate(s32[1]{0:T(128)} %bitcast.4, s32[1]{0:T(128)} %bitcast.5, s32[1]{0:T(128)} %bitcast.6, s32[1]{0:T(128)} %bitcast.7, s32[1]{0:T(128)} %bitcast.8, s32[1]{0:T(128)} %bitcast.9, s32[1]{0:T(128)} %bitcast.10, s32[1]{0:T(128)} %bitcast.11, s32[1]{0:T(128)} %bitcast.12, s32[1]{0:T(128)} %bitcast.13, s32[1]{0:T(128)} %bitcast.14, ...), dimensions={0} | concatenate | bytes 128 | tf_op jit(solution)/shard_map/stack | solution.py:600
  79.8 46.9 %collective-permute-done.8 = bf16[2,128,128]{2,1,0:T(8,128)(2,1)S(1)} collective-permute-done((bf16[2,128,128]{2,1,0:T(8,128)(2,1)S(1)}, bf16[2,128,128]{2,1,0:T(8,128)(2,1)S(1)}, u32[]{:S(2)}, u32[]{:S(2)}) %collective-permute-start.8) | collective-permute-done | bytes 65568 | tf_op jit(solution)/shard_map/ppermute | solution.py:542
  126.8 0.1 collective-permute-start.7
  127.0 5.6 %collective-permute-done.7 = bf16[2,128,128]{2,1,0:T(8,128)(2,1)S(1)} collective-permute-done((bf16[2,128,128]{2,1,0:T(8,128)(2,1)S(1)}, bf16[2,128,128]{2,1,0:T(8,128)(2,1)S(1)}, u32[]{:S(2)}, u32[]{:S(2)}) %collective-permute-start.7) | collective-permute-done | bytes 65568 | tf_op jit(solution)/shard_map/ppermute | solution.py:542
  132.5 0.3 collective-permute-start.6
  132.8 0.1 pad_add_fusion.3.refs_0_
  132.9 3.9 %collective-permute-done.6 = bf16[2,128,128]{2,1,0:T(8,128)(2,1)S(1)} collective-permute-done((bf16[2,128,128]{2,1,0:T(8,128)(2,1)S(1)}, bf16[2,128,128]{2,1,0:T(8,128)(2,1)S(1)}, u32[]{:S(2)}, u32[]{:S(2)}) %collective-permute-start.6) | collective-permute-done | bytes 65568 | tf_op jit(solution)/shard_map/ppermute | solution.py:542
  136.8 3.2 %collective-permute-start.1 = (bf16[128,1280]{1,0:T(8,128)(2,1)S(1)}, bf16[128,1280]{1,0:T(8,128)(2,1)S(1)}, u32[]{:S(2)}, u32[]{:S(2)}) collective-permute-start(bf16[128,1280]{1,0:T(8,128)(2,1)S(1)} %get-tuple-element.19.refs_2_), channel_id=1, source_target_pairs={{0,16},{8,24},{16,0},{24,8},{1,17},{9,25},{17,1},{25,9},{2,18},{10... | collective-permute-start | bytes 983048 | tf_op jit(solution)/shard_map/ppermute | solution.py:542
  140.0 1.2 collective-permute-start.2
  141.2 6.8 %collective-permute-done.1.refs_4_ = bf16[128,1280]{1,0:T(8,128)(2,1)S(1)} collective-permute-done((bf16[128,1280]{1,0:T(8,128)(2,1)S(1)}, bf16[128,1280]{1,0:T(8,128)(2,1)S(1)}, u32[]{:S(2)}, u32[]{:S(2)}) %collective-permute-start.1) | collective-permute-done | bytes 327712 | tf_op jit(solution)/shard_map/ppermute | solution.py:542
  148.0 4.1 %collective-permute-done.2.refs_5_ = bf16[128,1280]{1,0:T(8,128)(2,1)S(1)} collective-permute-done((bf16[128,1280]{1,0:T(8,128)(2,1)S(1)}, bf16[128,1280]{1,0:T(8,128)(2,1)S(1)}, u32[]{:S(2)}, u32[]{:S(2)}) %collective-permute-start.2) | collective-permute-done | bytes 327712 | tf_op jit(solution)/shard_map/ppermute | solution.py:542
  152.1 2.1 collective-permute-start.10
  154.2 2.2 copy-done.1
  156.4 21.8 %attend_own.1 = (bf16[512,1024]{1,0:T(8,128)(2,1)S(1)}, f32[512,128]{1,0:T(8,128)S(1)}, f32[512,1024]{1,0:T(8,128)S(1)}, f32[512,128]{1,0:T(8,128)S(1)}, f32[512,128]{1,0:T(8,128)S(1)}) custom-call(s32[5]{0:T(128)S(1)} %pad_add_fusion.2.refs_0_, s32[32]{0:T(128)S(1)} %get-tuple-element.49.refs_1_, bf16[128,1280]{1,0:T(8,128)(2,1)S(1)} %get-tuple-element.19.refs_2_, ...), custom_call_target="tpu_custom_call" | custom-call | flops 4294967296 | bytes 8388608 | tf_op jit(solution)/shard_map/attend_own/pallas_call | solution.py:398
  178.1 0.3 collective-permute-start.11
  178.5 34.8 %attend_near.1 = (f32[512,1024]{1,0:T(8,128)S(1)}, f32[512,128]{1,0:T(8,128)S(1)}, f32[512,128]{1,0:T(8,128)S(1)}, bf16[64,2,128,128]{3,2,1,0:T(8,128)(2,1)}) custom-call(s32[8]{0:T(128)S(1)} %pad_add_fusion.3.refs_0_, bf16[512,1024]{1,0:T(8,128)(2,1)S(1)} %get-tuple-element.20.refs_1_.refs_2_, f32[512,128]{1,0:T(8,128)S(1)} %get-tuple-element.21.refs_2_.refs_3_, ...), custom_call_target="tpu_custom_call" | custom-call | flops 8589934592 | bytes 8388608 | tf_op jit(solution)/shard_map/attend_near/pallas_call | solution.py:418
  213.3 20.0 %attend_last.1 = (bf16[4,144,1024]{2,1,0:T(8,128)(2,1)S(1)}, bf16[64,2,128,128]{3,2,1,0:T(8,128)(2,1)}) custom-call(s32[4]{0:T(128)S(1)} %squeeze.26.refs_0_, s32[16]{0:T(128)S(1)} %compare_select_fusion.3.refs_1_, bf16[512,1024]{1,0:T(8,128)(2,1)S(1)} %get-tuple-element.20.refs_1_.refs_2_, ...), custom_call_target="tpu_custom_call", output_to_operand_aliasing={{1}: (12, {})} | custom-call | flops 4294967296 | bytes 8388608 | tf_op jit(solution)/shard_map/attend_last/pallas_call | solution.py:435
  233.4 19.3 %all_to_all.15.in_ref = bf16[4,144,1024]{2,1,0:T(8,128)(2,1)S(1)} all-to-all(bf16[4,144,1024]{2,1,0:T(8,128)(2,1)S(1)} %get-tuple-element.30), channel_id=1, replica_groups=mesh['group'=4,'ctx'=4,'tp'=8] {'ctx'}, dimensions={0} | all-to-all | bytes 2359296 | tf_op jit(solution)/shard_map/all_to_all | solution.py:616
  252.7 0.8 combine.1.a
  253.5 0.9 collective-permute-start.12
  254.5 0.8 collective-permute-start.13
  255.2 2.0 collective-permute-start.14
  257.2 0.1 pad_add_fusion.1.meta_ref
  257.3 6.7 %collective-permute-done.12.b = bf16[128,1024]{1,0:T(8,128)(2,1)S(1)} collective-permute-done((bf16[128,1024]{1,0:T(8,128)(2,1)S(1)}, bf16[128,1024]{1,0:T(8,128)(2,1)S(1)}, u32[]{:S(2)}, u32[]{:S(2)}) %collective-permute-start.12) | collective-permute-done | bytes 262176 | tf_op jit(solution)/shard_map/ppermute | solution.py:542
  264.0 0.9 collective-permute-done.14.d
  264.9 2.2 copy-done.8
  267.1 4.0 %project_out.1 = (f32[4,512,256]{2,1,0:T(8,128)S(1)}, bf16[4,512,256]{2,1,0:T(8,128)(2,1)S(1)}) custom-call(s32[2]{0:T(128)S(1)} %pad_add_fusion.1.meta_ref, bf16[128,1024]{1,0:T(8,128)(2,1)S(1)} %combine.1.a, bf16[128,1024]{1,0:T(8,128)(2,1)S(1)} %collective-permute-done.12.b, bf16[128,1024]{1,0:T(8,128)(2,1)S(1)} %collective-permute-done.13.c, ...), custom_call_target="tpu_custom_call" | custom-call | flops 2147483648 | bytes 8388608 | tf_op jit(solution)/shard_map/project_out/pallas_call | solution.py:522
  271.1 0.1 collective-permute-start.15
  271.2 2.6 collective-permute-done.15
  273.8 0.4 add_convert_fusion
  274.2 20.5 %all_to_all.16 = bf16[4,512,256]{2,1,0:T(8,128)(2,1)S(1)} all-to-all(bf16[4,512,256]{2,1,0:T(8,128)(2,1)S(1)} %add_convert_fusion), channel_id=1, replica_groups={{0,2,4,6},{1,3,5,7},{8,10,12,14},{9,11,13,15},{16,18,20,22},{17,19,21,2..., dimensions={0} | all-to-all | bytes 2097152 | tf_op jit(solution)/shard_map/all_to_all | solution.py:624
  294.7 0.9 reduce_sum.42
  (49 shorter events, 0.6 us)
Async XLA Ops:
  2.0 2.2 copy-start
  7.5 1.3 copy-start.6
  8.8 9.5 %copy-start.10 = (bf16[2048,128]{1,0:T(8,128)(2,1)S(1)}, bf16[2048,128]{1,0:T(8,128)(2,1)}, u32[]{:S(2)}) copy-start(bf16[2048,128]{1,0:T(8,128)(2,1)} %wk_ref.1) | copy-start | bytes 1572868
  8.8 9.5 %copy-start.11 = (bf16[2048,128]{1,0:T(8,128)(2,1)S(1)}, bf16[2048,128]{1,0:T(8,128)(2,1)}, u32[]{:S(2)}) copy-start(bf16[2048,128]{1,0:T(8,128)(2,1)} %wv_ref.1) | copy-start | bytes 1572868
  8.8 9.5 %copy-start.12 = (f32[2048]{0:T(1024)S(1)}, f32[2048]{0:T(1024)}, u32[]{:S(2)}) copy-start(f32[2048]{0:T(1024)} %param.11) | copy-start | bytes 24580
  12.2 1.3 copy-start.4
  13.5 4.8 %copy-start.7 = (bf16[2048,1024]{1,0:T(8,128)(2,1)S(1)}, bf16[2048,1024]{1,0:T(8,128)(2,1)}, u32[]{:S(2)}) copy-start(bf16[2048,1024]{1,0:T(8,128)(2,1)} %wq_ref.1) | copy-start | bytes 12582916
  13.5 4.8 %copy-start.9 = (bf16[512,2048]{1,0:T(8,128)(2,1)S(1)}, bf16[512,2048]{1,0:T(8,128)(2,1)}, u32[]{:S(2)}) copy-start(bf16[512,2048]{1,0:T(8,128)(2,1)} %tok_ref) | copy-start | bytes 6291460
  16.9 1.4 copy-start.5
  25.8 1.6 copy-start.3
  27.4 7.7 %copy-start.14 = (s32[8]{0:T(128)S(1)}, s32[8]{0:T(128)}, u32[]{:S(2)}) copy-start(s32[8]{0:T(128)} %param.18) | copy-start | bytes 100
  27.4 39.2 %all-to-all-start = ((f32[4,128,1408]{2,1,0:T(8,128)}), f32[4,128,1408]{2,1,0:T(8,128)S(1)}, u32[]{:S(2)}, u32[]{:S(2)}) async-start(f32[4,128,1408]{2,1,0:T(8,128)} %bitcast.45), calls=%async_computation | async-start | bytes 5767168 | tf_op jit(solution)/shard_map/all_to_all | solution.py:595
  31.9 36.5 %copy-start.13 = (s32[8,2]{0,1:T(2,128)S(1)}, s32[8,2]{0,1:T(2,128)}, u32[]{:S(2)}) copy-start(s32[8,2]{0,1:T(2,128)} %param.19) | copy-start | bytes 196
  31.9 146.3 %collective-permute-start.3 = (bf16[32,2,128,128]{3,2,1,0:T(8,128)(2,1)}, bf16[32,2,128,128]{3,2,1,0:T(8,128)(2,1)}, u32[]{:S(2)}, u32[]{:S(2)}) collective-permute-start(bf16[32,2,128,128]{3,2,1,0:T(8,128)(2,1)} %copy-done.6), channel_id=1, source_target_pairs={{0,32},{32,64},{64,96},{96,0},{1,33},{33,65},{65,97},{97,1},{2,34}... | collective-permute-start | bytes 6291464 | tf_op jit(solution)/shard_map/ppermute | solution.py:542
  32.1 146.4 %collective-permute-start.4 = (bf16[32,2,128,128]{3,2,1,0:T(8,128)(2,1)}, bf16[32,2,128,128]{3,2,1,0:T(8,128)(2,1)}, u32[]{:S(2)}, u32[]{:S(2)}) collective-permute-start(bf16[32,2,128,128]{3,2,1,0:T(8,128)(2,1)} %copy-done.5), channel_id=1, source_target_pairs={{0,96},{32,0},{64,32},{96,64},{1,97},{33,1},{65,33},{97,65},{2,98}... | collective-permute-start | bytes 6291464 | tf_op jit(solution)/shard_map/ppermute | solution.py:542
  33.9 179.4 %collective-permute-start.5 = (bf16[32,2,128,128]{3,2,1,0:T(8,128)(2,1)}, bf16[32,2,128,128]{3,2,1,0:T(8,128)(2,1)}, u32[]{:S(2)}, u32[]{:S(2)}) collective-permute-start(bf16[32,2,128,128]{3,2,1,0:T(8,128)(2,1)} %copy-done.4), channel_id=1, source_target_pairs={{0,64},{32,96},{64,0},{96,32},{1,65},{33,97},{65,1},{97,33},{2,66}... | collective-permute-start | bytes 6291464 | tf_op jit(solution)/shard_map/ppermute | solution.py:542
  66.8 73.2 %collective-permute-start = (bf16[128,1280]{1,0:T(8,128)(2,1)S(1)}, bf16[128,1280]{1,0:T(8,128)(2,1)S(1)}, u32[]{:S(2)}, u32[]{:S(2)}) collective-permute-start(bf16[128,1280]{1,0:T(8,128)(2,1)S(1)} %get-tuple-element.19.refs_2_), channel_id=1, source_target_pairs={{0,8},{8,16},{16,24},{24,0},{1,9},{9,17},{17,25},{25,1},{2,10},{10... | collective-permute-start | bytes 983048 | tf_op jit(solution)/shard_map/ppermute | solution.py:542
  67.4 59.4 %collective-permute-start.8 = (bf16[2,128,128]{2,1,0:T(8,128)(2,1)S(1)}, bf16[2,128,128]{2,1,0:T(8,128)(2,1)S(1)}, u32[]{:S(2)}, u32[]{:S(2)}) collective-permute-start(bf16[2,128,128]{2,1,0:T(8,128)(2,1)S(1)} %get-tuple-element.28), channel_id=1, source_target_pairs={{0,96},{32,0},{64,32},{96,64},{1,97},{33,1},{65,33},{97,65},{2,98}... | collective-permute-start | bytes 196616 | tf_op jit(solution)/shard_map/ppermute | solution.py:542
  126.8 5.8 %collective-permute-start.7 = (bf16[2,128,128]{2,1,0:T(8,128)(2,1)S(1)}, bf16[2,128,128]{2,1,0:T(8,128)(2,1)S(1)}, u32[]{:S(2)}, u32[]{:S(2)}) collective-permute-start(bf16[2,128,128]{2,1,0:T(8,128)(2,1)S(1)} %get-tuple-element.28), channel_id=1, source_target_pairs={{0,64},{32,96},{64,0},{96,32},{1,65},{33,97},{65,1},{97,33},{2,66}... | collective-permute-start | bytes 196616 | tf_op jit(solution)/shard_map/ppermute | solution.py:542
  132.5 4.3 %collective-permute-start.6 = (bf16[2,128,128]{2,1,0:T(8,128)(2,1)S(1)}, bf16[2,128,128]{2,1,0:T(8,128)(2,1)S(1)}, u32[]{:S(2)}, u32[]{:S(2)}) collective-permute-start(bf16[2,128,128]{2,1,0:T(8,128)(2,1)S(1)} %get-tuple-element.28), channel_id=1, source_target_pairs={{0,32},{32,64},{64,96},{96,0},{1,33},{33,65},{65,97},{97,1},{2,34}... | collective-permute-start | bytes 196616 | tf_op jit(solution)/shard_map/ppermute | solution.py:542
  136.8 11.2 %collective-permute-start.1 = (bf16[128,1280]{1,0:T(8,128)(2,1)S(1)}, bf16[128,1280]{1,0:T(8,128)(2,1)S(1)}, u32[]{:S(2)}, u32[]{:S(2)}) collective-permute-start(bf16[128,1280]{1,0:T(8,128)(2,1)S(1)} %get-tuple-element.19.refs_2_), channel_id=1, source_target_pairs={{0,16},{8,24},{16,0},{24,8},{1,17},{9,25},{17,1},{25,9},{2,18},{10... | collective-permute-start | bytes 983048 | tf_op jit(solution)/shard_map/ppermute | solution.py:542
  140.0 12.1 %collective-permute-start.2 = (bf16[128,1280]{1,0:T(8,128)(2,1)S(1)}, bf16[128,1280]{1,0:T(8,128)(2,1)S(1)}, u32[]{:S(2)}, u32[]{:S(2)}) collective-permute-start(bf16[128,1280]{1,0:T(8,128)(2,1)S(1)} %get-tuple-element.19.refs_2_), channel_id=1, source_target_pairs={{0,24},{8,0},{16,8},{24,16},{1,25},{9,1},{17,9},{25,17},{2,26},{10... | collective-permute-start | bytes 983048 | tf_op jit(solution)/shard_map/ppermute | solution.py:542
  148.0 65.2 %collective-permute-start.9 = (bf16[4,2,128,128]{3,2,1,0:T(8,128)(2,1)S(1)}, bf16[4,2,128,128]{3,2,1,0:T(8,128)(2,1)S(1)}, u32[]{:S(2)}, u32[]{:S(2)}) collective-permute-start(bf16[4,2,128,128]{3,2,1,0:T(8,128)(2,1)S(1)} %pad_maximum_fusion.refs_8_), channel_id=1, source_target_pairs={{0,8},{8,16},{16,24},{24,0},{1,9},{9,17},{17,25},{25,1},{2,10},{10... | collective-permute-start | bytes 786440 | tf_op jit(solution)/shard_map/ppermute | solution.py:542
  152.1 61.2 %collective-permute-start.10 = (bf16[4,2,128,128]{3,2,1,0:T(8,128)(2,1)S(1)}, bf16[4,2,128,128]{3,2,1,0:T(8,128)(2,1)S(1)}, u32[]{:S(2)}, u32[]{:S(2)}) collective-permute-start(bf16[4,2,128,128]{3,2,1,0:T(8,128)(2,1)S(1)} %pad_maximum_fusion.refs_8_), channel_id=1, source_target_pairs={{0,16},{8,24},{16,0},{24,8},{1,17},{9,25},{17,1},{25,9},{2,18},{10... | collective-permute-start | bytes 786440 | tf_op jit(solution)/shard_map/ppermute | solution.py:542
  154.2 2.2 copy-start.1
  156.4 22.1 %copy-start.2 = (bf16[64,2,1,128,128]{4,3,2,1,0:T(8,128)(2,1)S(1)}, bf16[64,2,1,128,128]{4,3,2,1,0:T(8,128)(2,1)}, u32[]{:S(2)}) copy-start(bf16[64,2,1,128,128]{4,3,2,1,0:T(8,128)(2,1)} %param.16) | copy-start | bytes 12582916
  178.1 35.2 %collective-permute-start.11 = (bf16[4,2,128,128]{3,2,1,0:T(8,128)(2,1)S(1)}, bf16[4,2,128,128]{3,2,1,0:T(8,128)(2,1)S(1)}, u32[]{:S(2)}, u32[]{:S(2)}) collective-permute-start(bf16[4,2,128,128]{3,2,1,0:T(8,128)(2,1)S(1)} %pad_maximum_fusion.refs_8_), channel_id=1, source_target_pairs={{0,24},{8,0},{16,8},{24,16},{1,25},{9,1},{17,9},{25,17},{2,26},{10... | collective-permute-start | bytes 786440 | tf_op jit(solution)/shard_map/ppermute | solution.py:542
  253.5 10.5 %collective-permute-start.12 = (bf16[128,1024]{1,0:T(8,128)(2,1)S(1)}, bf16[128,1024]{1,0:T(8,128)(2,1)S(1)}, u32[]{:S(2)}, u32[]{:S(2)}) collective-permute-start(bf16[128,1024]{1,0:T(8,128)(2,1)S(1)} %combine.1.a), channel_id=1, source_target_pairs={{0,8},{8,16},{16,24},{24,0},{1,9},{9,17},{17,25},{25,1},{2,10},{10... | collective-permute-start | bytes 786440 | tf_op jit(solution)/shard_map/ppermute | solution.py:542
  254.5 9.5 %collective-permute-start.13 = (bf16[128,1024]{1,0:T(8,128)(2,1)S(1)}, bf16[128,1024]{1,0:T(8,128)(2,1)S(1)}, u32[]{:S(2)}, u32[]{:S(2)}) collective-permute-start(bf16[128,1024]{1,0:T(8,128)(2,1)S(1)} %combine.1.a), channel_id=1, source_target_pairs={{0,16},{8,24},{16,0},{24,8},{1,17},{9,25},{17,1},{25,9},{2,18},{10... | collective-permute-start | bytes 786440 | tf_op jit(solution)/shard_map/ppermute | solution.py:542
  255.2 9.7 %collective-permute-start.14 = (bf16[128,1024]{1,0:T(8,128)(2,1)S(1)}, bf16[128,1024]{1,0:T(8,128)(2,1)S(1)}, u32[]{:S(2)}, u32[]{:S(2)}) collective-permute-start(bf16[128,1024]{1,0:T(8,128)(2,1)S(1)} %combine.1.a), channel_id=1, source_target_pairs={{0,24},{8,0},{16,8},{24,16},{1,25},{9,1},{17,9},{25,17},{2,26},{10... | collective-permute-start | bytes 786440 | tf_op jit(solution)/shard_map/ppermute | solution.py:542
  264.9 2.2 copy-start.8
  271.1 2.7 collective-permute-start.15

commit v3 on v2

--- a/solution.py
+++ b/solution.py
@@ -13,6 +13,7 @@
 CHUNK = 4
 TAIL = 2
 ROOM = 60.0
+NO_COST = pl.CostEstimate(flops=1, bytes_accessed=1, transcendentals=0)
 CTX = 4
 NT = (((1,), (1,)), ((), ()))
 
@@ -77,44 +78,36 @@
         ],
         out_specs=pl.BlockSpec((rows, cols), lambda i: (0, 0)),
         compiler_params=params(),
-        cost_estimate=pl.CostEstimate(
-            flops=2 * rows * cols * features, bytes_accessed=10 << 20, transcendentals=0
-        ),
+        cost_estimate=NO_COST,
         name="project",
     )(tokens, gain, w_query, w_key, w_value)
 
 
-def finish_kernel(features, part_ref, out_ref, block_ref):
+def finish_kernel(features, part_ref, out_ref):
     q_cols = out_ref.shape[1]
     total = part_ref[0]
     for c in range(1, part_ref.shape[0]):
         total = total + part_ref[c]
     scale = lax.rsqrt(total[:, q_cols : q_cols + 1] / features + 1e-05)
-    done = (total[:, :q_cols] * scale).astype(BF16)
-    out_ref[...] = done
-    block_ref[0] = done[:, q_cols - 256 : q_cols - 128]
-    block_ref[1] = done[:, q_cols - 128 :]
+    out_ref[...] = (total[:, :q_cols] * scale).astype(BF16)
 
 
 def finish(parts, features):
     count, rows, cols = parts.shape
     return pl.pallas_call(
         lambda *refs: finish_kernel(features, *refs),
-        out_shape=[
-            jax.ShapeDtypeStruct((rows, cols - 128), BF16),
-            jax.ShapeDtypeStruct((2, rows, 128), BF16),
-        ],
+        out_shape=jax.ShapeDtypeStruct((rows, cols - 128), BF16),
         in_specs=[vmem()],
-        out_specs=[vmem()] * 2,
+        out_specs=vmem(),
         compiler_params=params(),
+        cost_estimate=NO_COST,
         name="finish",
     )(parts)
 
 
-def pack_kernel(index_ref, pool_ref, out_ref, sem):
+def pack_kernel(index_ref, pool_ref, out_ref):
     for n in range(out_ref.shape[0]):
-        pltpu.make_async_copy(pool_ref.at[index_ref[n]], out_ref.at[n], sem).start()
-    pltpu.make_async_copy(out_ref, out_ref, sem).wait()
+        out_ref[n] = pool_ref[index_ref[n]]
 
 
 def pack(index, pool):
@@ -122,10 +115,10 @@
     return pl.pallas_call(
         pack_kernel,
         out_shape=jax.ShapeDtypeStruct((count,) + pool.shape[1:], BF16),
-        in_specs=[smem(), anywhere()],
-        out_specs=anywhere(),
-        scratch_shapes=[pltpu.SemaphoreType.DMA(())],
-        compiler_params=params(),
+        in_specs=[smem(), vmem()],
+        out_specs=vmem(),
+        compiler_params=pltpu.CompilerParams(vmem_limit_bytes=20 * 1024 * 1024),
+        cost_estimate=NO_COST,
         name="pack",
     )(index, pool)
 
@@ -240,12 +233,11 @@
 
 
 def first_kernel(
-    new_len, const, meta_ref, index_ref, a, b, c, d, pool_ref,
-    q_ref, qn_ref, acc_ref, mp_ref, lp_ref, kv_ref, vx_ref, m_ref, l_ref, sem,
+    new_len, const, meta_ref, a, b, c, d, buf,
+    q_ref, qn_ref, acc_ref, mp_ref, lp_ref, new_ref, kv_ref, vx_ref, m_ref, l_ref, sem,
 ):
-    blocks = kv_ref.shape[0]
-    for n in range(blocks):
-        pltpu.make_async_copy(pool_ref.at[index_ref[n]], kv_ref.at[n], sem).start()
+    fetch = pltpu.make_async_copy(buf, kv_ref, sem)
+    fetch.start()
     tokens, q_cols = q_ref.shape
     part = a.shape[0]
     heads = m_ref.shape[0]
@@ -253,6 +245,8 @@
     for step, ref in enumerate((a, b, c, d)):
         place = lax.rem(rank + CTX - step, CTX)
         q_ref[pl.ds(pl.multiple_of(place * part, part), part), :] = ref[:, :q_cols]
+        new_ref[place, 0] = ref[:, q_cols : q_cols + 128]
+        new_ref[place, 1] = ref[:, q_cols + 128 :]
     m_ref[...] = jnp.full(m_ref.shape, NEG_FILL, F32)
     l_ref[...] = jnp.zeros(l_ref.shape, F32)
     acc_ref[...] = jnp.zeros(acc_ref.shape, F32)
@@ -272,7 +266,7 @@
     token = lax.broadcasted_iota(jnp.int32, (new_len, part), 0)
     fresh = lax.broadcasted_iota(jnp.int32, (new_len, part), 1) + offset
     moving(q_ref, m_ref, l_ref, acc_ref, rows, keys, values_ext, fresh <= token, const, True)
-    pltpu.make_async_copy(kv_ref, kv_ref, sem).wait()
+    fetch.wait()
     prefix_part(
         meta_ref, 1, q_ref, qn_ref, kv_ref, vx_ref, m_ref, l_ref, acc_ref, new_len, const
     )
@@ -321,22 +315,9 @@
 
 
 def last_kernel(
-    new_len, const, meta_ref, place_ref, q_ref, qn_ref, acc_in, mp_in, lp_in, buf,
-    new_a, new_b, new_c, new_d, pool_in, out_ref, pool_out,
-    acc_ref, kv_ref, vx_ref, m_ref, l_ref, sems, new_sems,
+    new_len, const, meta_ref, q_ref, qn_ref, acc_in, mp_in, lp_in, buf, out_ref,
+    acc_ref, kv_ref, vx_ref, m_ref, l_ref, sems,
 ):
-    def place(act):
-        count = new_a.shape[0]
-        for n, ref in enumerate((new_a, new_b, new_c, new_d)):
-            for i in range(count):
-                at = n * count + i
-                slot = place_ref[at]
-
-                @pl.when(slot >= 0)
-                def _(ref=ref, i=i, at=at, slot=slot):
-                    act(pltpu.make_async_copy(ref.at[i], pool_out.at[slot], new_sems.at[at]))
-
-    place(lambda copy: copy.start())
     sources(
         new_len, const, meta_ref, q_ref, qn_ref, (buf,), acc_in, mp_in, lp_in,
         acc_ref, kv_ref, vx_ref, m_ref, l_ref, sems,
@@ -364,12 +345,6 @@
         low = rest - mid
         tile = jnp.where(row == 0, high, jnp.where(row == 1, mid, jnp.where(row == 2, low, 0.0)))
         out_ref[c, part : part + 16, :] = tile.astype(BF16)
-    place(lambda copy: copy.wait())
-
-
-def attend_cost(blocks, tokens, heads):
-    pairs = blocks * 128 * tokens // 2 * heads
-    return pl.CostEstimate(flops=pairs * 512, bytes_accessed=8 << 20, transcendentals=pairs)
 
 
 def scratch(tokens, heads, blocks, lead=()):
@@ -389,26 +364,27 @@
     ]
 
 
-def attend_own(meta, index, quarters, pool, new_len, const):
+def attend_own(meta, quarters, buf, new_len, const):
     part = quarters[0].shape[0]
     q_cols = quarters[0].shape[1] - 256
     tokens = part * CTX
     heads = q_cols // 128
-    blocks = index.shape[0]
+    blocks = buf.shape[0]
     return pl.pallas_call(
         lambda *refs: first_kernel(new_len, const, *refs),
         out_shape=[
             jax.ShapeDtypeStruct((tokens, q_cols), BF16),
             jax.ShapeDtypeStruct((tokens, 128), F32),
         ]
-        + state_shapes(tokens, q_cols),
-        in_specs=[smem(), smem()] + [vmem()] * 4 + [anywhere()],
-        out_specs=[vmem()] * 5,
+        + state_shapes(tokens, q_cols)
+        + [jax.ShapeDtypeStruct((CTX, 2, part, 128), BF16)],
+        in_specs=[smem()] + [vmem()] * 4 + [anywhere()],
+        out_specs=[vmem()] * 6,
         scratch_shapes=scratch(tokens, heads, blocks) + [pltpu.SemaphoreType.DMA(())],
         compiler_params=params(),
-        cost_estimate=attend_cost(blocks, tokens, heads),
+        cost_estimate=NO_COST,
         name="attend_own",
-    )(meta, index, *quarters, pool)
+    )(meta, *quarters, buf)
 
 
 def attend_near(meta, queries, norms, state, bufs, pool, new_len, const):
@@ -423,31 +399,27 @@
         scratch_shapes=scratch(tokens, heads, blocks, (2,))
         + [pltpu.SemaphoreType.DMA((2,)), pltpu.SemaphoreType.DMA(())],
         compiler_params=params(),
-        cost_estimate=attend_cost(2 * blocks, tokens, heads),
+        cost_estimate=NO_COST,
         name="attend_near",
     )(meta, queries, norms, *state, *bufs, pool)
 
 
-def attend_last(meta, places, queries, norms, state, buf, news, pool, new_len, const):
+def attend_last(meta, queries, norms, state, buf, new_len, const):
     tokens, q_cols = queries.shape
     heads = q_cols // 128
     blocks = buf.shape[0]
     return pl.pallas_call(
         lambda *refs: last_kernel(new_len, const, *refs),
-        out_shape=[
-            jax.ShapeDtypeStruct((CTX, tokens // CTX + 16, q_cols), BF16),
-            jax.ShapeDtypeStruct(pool.shape, BF16),
-        ],
-        in_specs=[smem(), smem()] + [vmem()] * 5 + [anywhere()] * 6,
-        out_specs=[vmem(), anywhere()],
+        out_shape=jax.ShapeDtypeStruct((CTX, tokens // CTX + 16, q_cols), BF16),
+        in_specs=[smem()] + [vmem()] * 5 + [anywhere()],
+        out_specs=vmem(),
         scratch_shapes=[pltpu.VMEM((tokens, q_cols), F32)]
         + scratch(tokens, heads, blocks, (1,))
-        + [pltpu.SemaphoreType.DMA((1,)), pltpu.SemaphoreType.DMA((places.shape[0],))],
-        input_output_aliases={12: 1},
+        + [pltpu.SemaphoreType.DMA((1,))],
         compiler_params=params(),
-        cost_estimate=attend_cost(blocks, tokens, heads),
+        cost_estimate=NO_COST,
         name="attend_last",
-    )(meta, places, queries, norms, *state, buf, *news, pool)
+    )(meta, queries, norms, *state, buf)
 
 
 def combine_kernel(in_ref, out_ref):
@@ -485,18 +457,34 @@
         in_specs=[vmem()],
         out_specs=vmem(),
         compiler_params=params(),
+        cost_estimate=NO_COST,
         name="combine",
     )(arrived)
 
 
-def out_kernel(meta_ref, a, b, c, d, w_ref, own_ref, send_ref, rows_ref):
+def out_kernel(
+    meta_ref, place_ref, a, b, c, d, w_ref, new_a, new_b, new_c, new_d, pool_in,
+    own_ref, send_ref, pool_out, rows_ref, sems,
+):
     rank = meta_ref[0]
     core = meta_ref[1]
     part = a.shape[0]
     half = own_ref.shape[2]
 
+    def place_blocks(act):
+        count = new_a.shape[0]
+        for n, ref in enumerate((new_a, new_b, new_c, new_d)):
+            for i in range(count):
+                at = n * count + i
+                slot = place_ref[at]
+
+                @pl.when(slot >= 0)
+                def _(ref=ref, i=i, at=at, slot=slot):
+                    act(pltpu.make_async_copy(ref.at[i], pool_out.at[slot], sems.at[at]))
+
     @pl.when(pl.program_id(0) == 0)
     def _():
+        place_blocks(lambda copy: copy.start())
         for step, ref in enumerate((a, b, c, d)):
             place = lax.rem(rank + CTX - step, CTX)
             rows_ref[pl.ds(pl.multiple_of(place * part, part), part), :] = ref[...]
@@ -513,8 +501,12 @@
         own_ref[0] = product[:, half:]
         send_ref[0] = product[:, :half].astype(BF16)
 
-
-def project_out(meta, quarters, w_out, planes):
+    @pl.when(pl.program_id(0) == pl.num_programs(0) - 1)
+    def _():
+        place_blocks(lambda copy: copy.wait())
+
+
+def project_out(meta, places, quarters, w_out, news, pool, planes):
     part, depth = quarters[0].shape
     tokens = part * CTX
     width = w_out.shape[1] // planes
@@ -525,16 +517,22 @@
         out_shape=[
             jax.ShapeDtypeStruct((planes, tokens, width // 2), F32),
             jax.ShapeDtypeStruct((planes, tokens, width // 2), BF16),
+            jax.ShapeDtypeStruct(pool.shape, BF16),
         ],
-        in_specs=[smem(), whole, whole, whole, whole, pl.BlockSpec((depth, width), lambda i: (0, i))],
-        out_specs=[pl.BlockSpec((1, tokens, width // 2), lambda i: (i, 0, 0))] * 2,
-        scratch_shapes=[pltpu.VMEM((tokens, depth), BF16)],
+        in_specs=[smem(), smem()]
+        + [whole] * 4
+        + [pl.BlockSpec((depth, width), lambda i: (0, i))]
+        + [anywhere()] * 5,
+        out_specs=[pl.BlockSpec((1, tokens, width // 2), lambda i: (i, 0, 0))] * 2 + [anywhere()],
+        scratch_shapes=[
+            pltpu.VMEM((tokens, depth), BF16),
+            pltpu.SemaphoreType.DMA((places.shape[0],)),
+        ],
+        input_output_aliases={11: 2},
         compiler_params=params(),
-        cost_estimate=pl.CostEstimate(
-            flops=2 * tokens * depth * w_out.shape[1], bytes_accessed=8 << 20, transcendentals=0
-        ),
+        cost_estimate=NO_COST,
         name="project_out",
-    )(meta, *quarters, w_out)
+    )(meta, places, *quarters, w_out, *news, pool)
 
 
 def shifted(value, axis, step):
@@ -574,7 +572,7 @@
     wanted = jnp.arange(1, per_pair + 1, dtype=jnp.int32)
     picked = here[:, None, :] & (order[:, None, :] == wanted[None, :, None])
     send_index = jnp.sum(jnp.where(picked, send_table[:, None, :] % pool_size, 0), axis=2)
-    blocks = {step: pack(send_index[step], pool) for step in (1, 3, 2)}
+    blocks = {step: pack(send_index[step], pool) for step in (1, 3, 2, 0)}
     arrived = {step: shifted(blocks[step], "group", step) for step in (1, 3, 2)}
 
     mine = lax.dynamic_index_in_dim(table, group, 0, keepdims=False).reshape(sess_here, list_len)
@@ -588,37 +586,32 @@
     starts = jnp.cumsum(counts, axis=1) - counts
     meta = jnp.stack([starts, live_keys], axis=2).reshape(groups, 2 * sess_here).astype(jnp.int32)
 
-    tokens, _ = lax.optimization_barrier((tokens, blocks))
+    tokens, _ = lax.optimization_barrier((tokens, [blocks[step] for step in (1, 2, 3)]))
     parts = project(tokens, norm_gain[None, :], w_query, w_key, w_value)
     part_rows = tokens.shape[0] // ranks
     parts = parts.reshape(ranks, part_rows, parts.shape[1])
     parts = lax.all_to_all(parts, "ctx", split_axis=0, concat_axis=0, tiled=True)
-    fresh, block = finish(parts, tokens.shape[1] * ranks)
+    fresh = finish(parts, tokens.shape[1] * ranks)
     quarters = around(fresh, "ctx")
-    news = around(jnp.stack(around(block, "group")), "ctx")
-    targets = write_slot.reshape(groups, ranks)
-    targets = jnp.stack(
-        [targets[(group - g) % groups, (rank - c) % ranks] for c in range(ranks) for g in range(groups)]
-    )
-    places = jnp.where(targets // pool_size == device_id, targets % pool_size, -1)
 
     first_meta = jnp.concatenate([rank[None].astype(jnp.int32), meta[0]])
-    queries, norms, *state = attend_own(
-        first_meta, send_index[0], quarters, pool, new_len, const
-    )
+    queries, norms, *state, block = attend_own(first_meta, quarters, blocks[0], new_len, const)
     near_meta = jnp.concatenate([meta[1], meta[3]])
     *state, new_pool = attend_near(
         near_meta, queries, norms, state, [arrived[1], arrived[3]], pool, new_len, const
     )
-    partial, new_pool = attend_last(
-        meta[2], places, queries, norms, state, arrived[2], news, new_pool, new_len, const
-    )
+    partial = attend_last(meta[2], queries, norms, state, arrived[2], new_len, const)
     partial = lax.all_to_all(partial, "ctx", split_axis=0, concat_axis=0, tiled=True)
     attended = combine(partial)
 
     planes = tp_size // 2
     out_meta = jnp.stack([rank, core]).astype(jnp.int32)
-    own, send = project_out(out_meta, around(attended, "ctx"), w_out, planes)
+    news = around(block, "group")
+    targets = jnp.roll(write_slot.reshape(groups, ranks)[::-1], group + 1, axis=0).reshape(-1)
+    places = jnp.where(targets // pool_size == device_id, targets % pool_size, -1)
+    own, send, new_pool = project_out(
+        out_meta, places, around(attended, "ctx"), w_out, news, new_pool, planes
+    )
     other = lax.ppermute(send, "tp", [(i, i ^ 1) for i in range(tp_size)])
     pair = (own + other.astype(F32)).astype(BF16)
     terms = lax.all_to_all(

time: 296 us -> 227 us (0.77)
  waiting for transfers between devices: 109 us -> 80.6 us
  Pallas kernels: 99.2 us -> 74.3 us
  blocking collectives: 39.9 us -> 20.5 us
  starting transfers between devices: 20 us -> 25.6 us
  local copies, waits for them, and re-layouts: 24.6 us -> 20.6 us
    ppermute x15 -> x12, waiting for transfers between devices: 74.9 us -> 43.2 us  [shifted(): lax.ppermute(value, axis, [(i, (i + step) % size) for i in range(size)])]
    all_to_all x1 -> x0, blocking collectives: 19.3 us -> none  [local(): lax.all_to_all(partial, 'ctx', split_axis=0, concat_axis=0, tiled=True)]
    another operation x1 -> x0, local copies, waits for them, and re-layouts: 10 us -> none  [local(): jnp.stack([targets[(group - g) % groups, (rank - c) % ranks] for c in ran...]
    pallas_call x1, Pallas kernels: 21.8 us -> 13.6 us  [attend_own(): pl.pallas_call(lambda *refs: first_kernel(new_len, const, *refs), out_sha...]
    all_to_all x0 -> x1, waiting for transfers between devices: none -> 7.61 us  [local(): lax.all_to_all(partial, 'ctx', split_axis=0, concat_axis=0, tiled=True)]
    pallas_call x3 -> x4, Pallas kernels: 10.1 us -> 2.72 us  [pack(): pl.pallas_call(pack_kernel, out_shape=jax.ShapeDtypeStruct((count,) + poo...]
    pallas_call x1, Pallas kernels: 34.8 us -> 27.5 us  [attend_near(): pl.pallas_call(lambda *refs: near_kernel(new_len, const, *refs), out_shap...]
    unnamed x31 -> x35, local copies, waits for them, and re-layouts: 12.3 us -> 18.9 us
  transfers between devices with their start and end apart: 17 -> 15, of which waited for: 9 -> 9; matrix products, arithmetic and copies ran while one was open for 4% -> 1% of each run, Pallas kernels for 19% -> 19%
where the time goes in v3:
time: 227 us; the launch traced here: 225 us
  waiting for transfers between devices  80.6 us (36%)
  Pallas kernels  74.3 us (33%)
  starting transfers between devices  25.6 us (11%)
  local copies, waits for them, and re-layouts  20.6 us (9%)
  blocking collectives  20.5 us (9%)
    ppermute x12, waiting for transfers between devices, shifted(): lax.ppermute(value, axis, [(i, (i + step) % size) for i in range(size)])  43.2 us
    pallas_call x1, Pallas kernels, attend_near(): pl.pallas_call(lambda *refs: near_kernel(new_len, const, *refs), out_shap...  27.5 us
    all_to_all x1, waiting for transfers between devices, local(): lax.all_to_all(parts, 'ctx', split_axis=0, concat_axis=0, tiled=True)  27.1 us
    all_to_all x1, blocking collectives, local(): lax.all_to_all(pair, 'tp', split_axis=0, concat_axis=0, axis_index_groups...  20.5 us
    unnamed x35, local copies, waits for them, and re-layouts  18.9 us
    ppermute x12, starting transfers between devices, shifted(): lax.ppermute(value, axis, [(i, (i + step) % size) for i in range(size)])  17.7 us
    pallas_call x1, Pallas kernels, attend_last(): pl.pallas_call(lambda *refs: last_kernel(new_len, const, *refs), out_shap...  17.5 us
    pallas_call x1, Pallas kernels, attend_own(): pl.pallas_call(lambda *refs: first_kernel(new_len, const, *refs), out_sha...  13.6 us
  transfers between devices with their start and end apart: 15, of which 9 were waited for; matrix products, arithmetic and copies ran while one was open for 1% of the time, Pallas kernels for 19%

profile of v3, /device:TPU:24, one launch (start us, length us, event | category | flops | bytes accessed | tf_op | source)
XLA Modules:
  0.0 225.1 jit_solution(11249764047405121382)
XLA Ops:
  0.7 0.7 reshape.167
  1.5 0.3 convolution_convert_fusion
  1.7 0.2 select_reduce_fusion
  2.0 2.2 copy-done
  4.2 0.7 pack.6
  4.9 1.3 copy-done.9
  6.2 0.7 pack.5
  6.8 1.3 copy-done.8
  8.2 0.7 pack.4
  8.9 1.3 copy-done.10
  10.2 0.9 copy-done.6
  11.1 0.7 copy-done.11
  11.8 7.5 %project.1 = f32[512,1408]{1,0:T(8,128)S(1)} custom-call(bf16[512,2048]{1,0:T(8,128)(2,1)S(1)} %copy-done.11, f32[1,2048]{1,0:T(1,128)S(1)} %bitcast.26, bf16[2048,1024]{1,0:T(8,128)(2,1)S(1)} %copy-done.6, bf16[2048,128]{1,0:T(8,128)(2,1)S(1)} %copy-done.12, bf16[2048,128]{1,0:T(8,128)(2,1)S(1)} %copy-done.13), custom_call_target="tpu_custom_call" | custom-call | flops 1 | bytes 1 | tf_op jit(solution)/shard_map/project/pallas_call | solution.py:68
  19.3 1.6 copy-done.3
  20.8 4.3 %all-to-all-start = ((f32[4,128,1408]{2,1,0:T(8,128)}), f32[4,128,1408]{2,1,0:T(8,128)S(1)}, u32[]{:S(2)}, u32[]{:S(2)}) async-start(f32[4,128,1408]{2,1,0:T(8,128)} %bitcast.25), calls=%async_computation | async-start | bytes 5767168 | tf_op jit(solution)/shard_map/all_to_all | solution.py:593
  25.1 0.2 collective-permute-start.3
  25.4 1.8 collective-permute-start.4
  27.2 1.2 collective-permute-start.5
  28.4 2.2 copy-done.1
  30.6 0.7 pack.7.refs_5_
  31.3 1.3 copy-done.4
  32.8 27.1 %all-to-all-done.refs_0_ = f32[4,128,1408]{2,1,0:T(8,128)S(1)} async-done(((f32[4,128,1408]{2,1,0:T(8,128)}), f32[4,128,1408]{2,1,0:T(8,128)S(1)}, u32[]{:S(2)}, u32[]{:S(2)}) %all-to-all-start) | async-done | bytes 2883616 | tf_op jit(solution)/shard_map/all_to_all | solution.py:593
  59.9 0.1 finish.1.refs_1_
  60.0 1.2 collective-permute-start.2
  61.3 0.2 fusion.6
  61.5 1.5 collective-permute-start.1
  63.1 7.7 %collective-permute-done.2.refs_4_ = bf16[128,1280]{1,0:T(8,128)(2,1)S(1)} collective-permute-done((bf16[128,1280]{1,0:T(8,128)(2,1)S(1)}, bf16[128,1280]{1,0:T(8,128)(2,1)S(1)}, u32[]{:S(2)}, u32[]{:S(2)}) %collective-permute-start.2) | collective-permute-done | bytes 327712 | tf_op jit(solution)/shard_map/ppermute | solution.py:540
  70.8 5.3 %collective-permute-start = (bf16[128,1280]{1,0:T(8,128)(2,1)S(1)}, bf16[128,1280]{1,0:T(8,128)(2,1)S(1)}, u32[]{:S(2)}, u32[]{:S(2)}) collective-permute-start(bf16[128,1280]{1,0:T(8,128)(2,1)S(1)} %finish.1.refs_1_), channel_id=1, source_target_pairs={{0,8},{8,16},{16,24},{24,0},{1,9},{9,17},{17,25},{25,1},{2,10},{10... | collective-permute-start | bytes 983048 | tf_op jit(solution)/shard_map/ppermute | solution.py:540
  76.1 0.1 copy.28
  76.2 0.1 squeeze.32
  76.3 0.1 copy.26
  76.4 0.1 squeeze.26.refs_0_
  76.5 0.1 copy.27
  76.6 0.1 squeeze.27
  76.7 0.1 copy.29
  76.8 0.1 squeeze.33
  76.9 0.1 pad_add_fusion.3.refs_0_
  77.0 3.6 %collective-permute-done.refs_2_ = bf16[128,1280]{1,0:T(8,128)(2,1)S(1)} collective-permute-done((bf16[128,1280]{1,0:T(8,128)(2,1)S(1)}, bf16[128,1280]{1,0:T(8,128)(2,1)S(1)}, u32[]{:S(2)}, u32[]{:S(2)}) %collective-permute-start) | collective-permute-done | bytes 327712 | tf_op jit(solution)/shard_map/ppermute | solution.py:540
  80.7 1.6 copy-done.5
  82.3 13.6 %attend_own.1 = (bf16[512,1024]{1,0:T(8,128)(2,1)S(1)}, f32[512,128]{1,0:T(8,128)S(1)}, f32[512,1024]{1,0:T(8,128)S(1)}, f32[512,128]{1,0:T(8,128)S(1)}, f32[512...) custom-call(s32[5]{0:T(128)S(1)} %pad_add_fusion.3.refs_0_, bf16[128,1280]{1,0:T(8,128)(2,1)S(1)} %finish.1.refs_1_, ...), custom_call_target="tpu_custom_call" | custom-call | flops 1 | bytes 1 | tf_op jit(solution)/shard_map/attend_own/pallas_call | solution.py:373
  95.8 22.9 %collective-permute-done.4.refs_7_ = bf16[32,2,128,128]{3,2,1,0:T(8,128)(2,1)} collective-permute-done((bf16[32,2,128,128]{3,2,1,0:T(8,128)(2,1)}, bf16[32,2,128,128]{3,2,1,0:T(8,128)(2,1)}, u32[]{:S(2)}, u32[]{:S(2)}) %collective-permute-start.4) | collective-permute-done | bytes 2097184 | tf_op jit(solution)/shard_map/ppermute | solution.py:540
  118.7 2.2 copy-done.2
  120.9 27.5 %attend_near.1 = (f32[512,1024]{1,0:T(8,128)S(1)}, f32[512,128]{1,0:T(8,128)S(1)}, f32[512,128]{1,0:T(8,128)S(1)}, bf16[64,2,128,128]{3,2,1,0:T(8,128)(2,1)}) custom-call(s32[8]{0:T(128)S(1)} %pad_add_fusion.4.refs_0_, bf16[512,1024]{1,0:T(8,128)(2,1)S(1)} %get-tuple-element.17.refs_1_, f32[512,128]{1,0:T(8,128)S(1)} %get-tuple-element.18.refs_2_, ...), custom_call_target="tpu_custom_call" | custom-call | flops 1 | bytes 1 | tf_op jit(solution)/shard_map/attend_near/pallas_call | solution.py:394
  148.4 17.5 %attend_last.1 = bf16[4,144,1024]{2,1,0:T(8,128)(2,1)} custom-call(s32[4]{0:T(128)S(1)} %squeeze.26.refs_0_, bf16[512,1024]{1,0:T(8,128)(2,1)S(1)} %get-tuple-element.17.refs_1_, f32[512,128]{1,0:T(8,128)S(1)} %get-tuple-element.18.refs_2_, f32[512,1024]{1,0:T(8,128)S(1)} %get-tuple-element.22.refs_3_, f32[512,128]{1,0:T(8,128)S(1)} %get-tuple-element.23.refs_4_, ...), custom_call_target="tpu_custom_call" | custom-call | flops 1 | bytes 1 | tf_op jit(solution)/shard_map/attend_last/pallas_call | solution.py:411
  165.9 3.5 %all-to-all-start.1 = ((bf16[4,144,1024]{2,1,0:T(8,128)(2,1)}), bf16[4,144,1024]{2,1,0:T(8,128)(2,1)S(1)}, u32[]{:S(2)}, u32[]{:S(2)}) async-start(bf16[4,144,1024]{2,1,0:T(8,128)(2,1)} %attend_last.1), calls=%async_computation.1 | async-start | bytes 2359296 | tf_op jit(solution)/shard_map/all_to_all | solution.py:604
  169.6 0.1 copy.25
  169.7 0.1 reshape.165
  169.8 0.1 collective-permute-start.10
  169.9 3.5 %collective-permute-start.9 = (bf16[4,2,128,128]{3,2,1,0:T(8,128)(2,1)S(1)}, bf16[4,2,128,128]{3,2,1,0:T(8,128)(2,1)S(1)}, u32[]{:S(2)}, u32[]{:S(2)}) collective-permute-start(bf16[4,2,128,128]{3,2,1,0:T(8,128)(2,1)S(1)} %get-tuple-element.25.new_a), channel_id=1, source_target_pairs={{0,32},{32,64},{64,96},{96,0},{1,33},{33,65},{65,97},{97,1},{2,34}... | collective-permute-start | bytes 786440 | tf_op jit(solution)/shard_map/ppermute | solution.py:540
  173.4 7.6 %all-to-all-done.1.in_ref = bf16[4,144,1024]{2,1,0:T(8,128)(2,1)S(1)} async-done(((bf16[4,144,1024]{2,1,0:T(8,128)(2,1)}), bf16[4,144,1024]{2,1,0:T(8,128)(2,1)S(1)}, u32[]{:S(2)}, u32[]{:S(2)}) %all-to-all-start.1) | async-done | bytes 1179680 | tf_op jit(solution)/shard_map/all_to_all | solution.py:604
  181.0 0.8 combine.1.a
  181.9 1.2 collective-permute-start.8
  183.1 1.5 collective-permute-start.7
  184.7 0.1 reshape.166
  184.8 3.5 %collective-permute-done.8.d = bf16[128,1024]{1,0:T(8,128)(2,1)S(1)} collective-permute-done((bf16[128,1024]{1,0:T(8,128)(2,1)S(1)}, bf16[128,1024]{1,0:T(8,128)(2,1)S(1)}, u32[]{:S(2)}, u32[]{:S(2)}) %collective-permute-start.8) | collective-permute-done | bytes 262176 | tf_op jit(solution)/shard_map/ppermute | solution.py:540
  188.3 2.8 %collective-permute-done.7.c = bf16[128,1024]{1,0:T(8,128)(2,1)S(1)} collective-permute-done((bf16[128,1024]{1,0:T(8,128)(2,1)S(1)}, bf16[128,1024]{1,0:T(8,128)(2,1)S(1)}, u32[]{:S(2)}, u32[]{:S(2)}) %collective-permute-start.7) | collective-permute-done | bytes 262176 | tf_op jit(solution)/shard_map/ppermute | solution.py:540
  191.1 2.7 %collective-permute-done.6.b = bf16[128,1024]{1,0:T(8,128)(2,1)S(1)} collective-permute-done((bf16[128,1024]{1,0:T(8,128)(2,1)S(1)}, bf16[128,1024]{1,0:T(8,128)(2,1)S(1)}, u32[]{:S(2)}, u32[]{:S(2)}) %collective-permute-start.6) | collective-permute-done | bytes 262176 | tf_op jit(solution)/shard_map/ppermute | solution.py:540
  193.8 2.2 copy-done.7
  196.0 4.6 %project_out.1 = (f32[4,512,256]{2,1,0:T(8,128)S(1)}, bf16[4,512,256]{2,1,0:T(8,128)(2,1)S(1)}, bf16[64,2,128,128]{3,2,1,0:T(8,128)(2,1)}) custom-call(s32[2]{0:T(128)S(1)} %pad_add_fusion.2.meta_ref, s32[16]{0:T(128)S(1)} %compare_select_fusion.3.place_ref, bf16[128,1024]{1,0:T(8,128)(2,1)S(1)} %combine.1.a, ...), custom_call_target="tpu_custom_call", output_to_operand_aliasing={{2}: (11, {})} | custom-call | flops 1 | bytes 1 | tf_op jit(solution)/shard_map/project_out/pallas_call | solution.py:514
  200.5 0.1 collective-permute-start.12
  200.6 2.6 %collective-permute-done.12 = bf16[4,512,256]{2,1,0:T(8,128)(2,1)S(1)} collective-permute-done((bf16[4,512,256]{2,1,0:T(8,128)(2,1)S(1)}, bf16[4,512,256]{2,1,0:T(8,128)(2,1)S(1)}, u32[]{:S(2)}, u32[]{:S(2)}) %collective-permute-start.12) | collective-permute-done | bytes 1048608 | tf_op jit(solution)/shard_map/ppermute | solution.py:615
  203.3 0.4 add_convert_fusion
  203.7 20.5 %all_to_all.15 = bf16[4,512,256]{2,1,0:T(8,128)(2,1)S(1)} all-to-all(bf16[4,512,256]{2,1,0:T(8,128)(2,1)S(1)} %add_convert_fusion), channel_id=1, replica_groups={{0,2,4,6},{1,3,5,7},{8,10,12,14},{9,11,13,15},{16,18,20,22},{17,19,21,2..., dimensions={0} | all-to-all | bytes 2097152 | tf_op jit(solution)/shard_map/all_to_all | solution.py:617
  224.2 0.9 reduce_sum.42
  (50 shorter events, 0.7 us)
Async XLA Ops:
  2.0 2.2 copy-start
  4.8 1.3 copy-start.9
  6.1 4.1 %copy-start.12 = (bf16[2048,128]{1,0:T(8,128)(2,1)S(1)}, bf16[2048,128]{1,0:T(8,128)(2,1)}, u32[]{:S(2)}) copy-start(bf16[2048,128]{1,0:T(8,128)(2,1)} %wk_ref.1) | copy-start | bytes 1572868
  6.1 4.1 %copy-start.13 = (bf16[2048,128]{1,0:T(8,128)(2,1)S(1)}, bf16[2048,128]{1,0:T(8,128)(2,1)}, u32[]{:S(2)}) copy-start(bf16[2048,128]{1,0:T(8,128)(2,1)} %wv_ref.1) | copy-start | bytes 1572868
  6.2 4.1 %copy-start.14 = (f32[2048]{0:T(1024)S(1)}, f32[2048]{0:T(1024)}, u32[]{:S(2)}) copy-start(f32[2048]{0:T(1024)} %param.11) | copy-start | bytes 24580
  6.8 1.3 copy-start.8
  8.2 2.9 %copy-start.6 = (bf16[2048,1024]{1,0:T(8,128)(2,1)S(1)}, bf16[2048,1024]{1,0:T(8,128)(2,1)}, u32[]{:S(2)}) copy-start(bf16[2048,1024]{1,0:T(8,128)(2,1)} %wq_ref.1) | copy-start | bytes 12582916
  8.2 3.6 %copy-start.11 = (bf16[512,2048]{1,0:T(8,128)(2,1)S(1)}, bf16[512,2048]{1,0:T(8,128)(2,1)}, u32[]{:S(2)}) copy-start(bf16[512,2048]{1,0:T(8,128)(2,1)} %tok_ref) | copy-start | bytes 6291460
  8.9 1.3 copy-start.10
  19.3 1.6 copy-start.3
  20.8 39.1 %all-to-all-start = ((f32[4,128,1408]{2,1,0:T(8,128)}), f32[4,128,1408]{2,1,0:T(8,128)S(1)}, u32[]{:S(2)}, u32[]{:S(2)}) async-start(f32[4,128,1408]{2,1,0:T(8,128)} %bitcast.25), calls=%async_computation | async-start | bytes 5767168 | tf_op jit(solution)/shard_map/all_to_all | solution.py:593
  25.1 70.7 %collective-permute-start.3 = (bf16[32,2,128,128]{3,2,1,0:T(8,128)(2,1)}, bf16[32,2,128,128]{3,2,1,0:T(8,128)(2,1)}, u32[]{:S(2)}, u32[]{:S(2)}) collective-permute-start(bf16[32,2,128,128]{3,2,1,0:T(8,128)(2,1)} %copy-done.10), channel_id=1, source_target_pairs={{0,32},{32,64},{64,96},{96,0},{1,33},{33,65},{65,97},{97,1},{2,34}... | collective-permute-start | bytes 6291464 | tf_op jit(solution)/shard_map/ppermute | solution.py:540
  25.4 93.3 %collective-permute-start.4 = (bf16[32,2,128,128]{3,2,1,0:T(8,128)(2,1)}, bf16[32,2,128,128]{3,2,1,0:T(8,128)(2,1)}, u32[]{:S(2)}, u32[]{:S(2)}) collective-permute-start(bf16[32,2,128,128]{3,2,1,0:T(8,128)(2,1)} %copy-done.9), channel_id=1, source_target_pairs={{0,96},{32,0},{64,32},{96,64},{1,97},{33,1},{65,33},{97,65},{2,98}... | collective-permute-start | bytes 6291464 | tf_op jit(solution)/shard_map/ppermute | solution.py:540
  27.2 121.3 %collective-permute-start.5 = (bf16[32,2,128,128]{3,2,1,0:T(8,128)(2,1)}, bf16[32,2,128,128]{3,2,1,0:T(8,128)(2,1)}, u32[]{:S(2)}, u32[]{:S(2)}) collective-permute-start(bf16[32,2,128,128]{3,2,1,0:T(8,128)(2,1)} %copy-done.8), channel_id=1, source_target_pairs={{0,64},{32,96},{64,0},{96,32},{1,65},{33,97},{65,1},{97,33},{2,66}... | collective-permute-start | bytes 6291464 | tf_op jit(solution)/shard_map/ppermute | solution.py:540
  28.4 2.2 copy-start.1
  30.6 2.1 copy-start.16
  31.3 1.3 copy-start.4
  60.0 10.7 %collective-permute-start.2 = (bf16[128,1280]{1,0:T(8,128)(2,1)S(1)}, bf16[128,1280]{1,0:T(8,128)(2,1)S(1)}, u32[]{:S(2)}, u32[]{:S(2)}) collective-permute-start(bf16[128,1280]{1,0:T(8,128)(2,1)S(1)} %finish.1.refs_1_), channel_id=1, source_target_pairs={{0,24},{8,0},{16,8},{24,16},{1,25},{9,1},{17,9},{25,17},{2,26},{10... | collective-permute-start | bytes 983048 | tf_op jit(solution)/shard_map/ppermute | solution.py:540
  61.5 15.5 %collective-permute-start.1 = (bf16[128,1280]{1,0:T(8,128)(2,1)S(1)}, bf16[128,1280]{1,0:T(8,128)(2,1)S(1)}, u32[]{:S(2)}, u32[]{:S(2)}) collective-permute-start(bf16[128,1280]{1,0:T(8,128)(2,1)S(1)} %finish.1.refs_1_), channel_id=1, source_target_pairs={{0,16},{8,24},{16,0},{24,8},{1,17},{9,25},{17,1},{25,9},{2,18},{10... | collective-permute-start | bytes 983048 | tf_op jit(solution)/shard_map/ppermute | solution.py:540
  70.8 9.9 %collective-permute-start = (bf16[128,1280]{1,0:T(8,128)(2,1)S(1)}, bf16[128,1280]{1,0:T(8,128)(2,1)S(1)}, u32[]{:S(2)}, u32[]{:S(2)}) collective-permute-start(bf16[128,1280]{1,0:T(8,128)(2,1)S(1)} %finish.1.refs_1_), channel_id=1, source_target_pairs={{0,8},{8,16},{16,24},{24,0},{1,9},{9,17},{17,25},{25,1},{2,10},{10... | collective-permute-start | bytes 983048 | tf_op jit(solution)/shard_map/ppermute | solution.py:540
  80.7 1.6 copy-start.5
  118.7 2.2 copy-start.2
  165.9 3.7 %copy-start.15 = (s32[8,2]{0,1:T(2,128)S(1)}, s32[8,2]{0,1:T(2,128)}, u32[]{:S(2)}) copy-start(s32[8,2]{0,1:T(2,128)} %param.19) | copy-start | bytes 196
  165.9 15.1 %all-to-all-start.1 = ((bf16[4,144,1024]{2,1,0:T(8,128)(2,1)}), bf16[4,144,1024]{2,1,0:T(8,128)(2,1)S(1)}, u32[]{:S(2)}, u32[]{:S(2)}) async-start(bf16[4,144,1024]{2,1,0:T(8,128)(2,1)} %attend_last.1), calls=%async_computation.1 | async-start | bytes 2359296 | tf_op jit(solution)/shard_map/all_to_all | solution.py:604
  169.5 15.1 %collective-permute-start.11 = (bf16[4,2,128,128]{3,2,1,0:T(8,128)(2,1)S(1)}, bf16[4,2,128,128]{3,2,1,0:T(8,128)(2,1)S(1)}, u32[]{:S(2)}, u32[]{:S(2)}) collective-permute-start(bf16[4,2,128,128]{3,2,1,0:T(8,128)(2,1)S(1)} %get-tuple-element.25.new_a), channel_id=1, source_target_pairs={{0,96},{32,0},{64,32},{96,64},{1,97},{33,1},{65,33},{97,65},{2,98}... | collective-permute-start | bytes 786440 | tf_op jit(solution)/shard_map/ppermute | solution.py:540
  169.8 14.9 %collective-permute-start.10 = (bf16[4,2,128,128]{3,2,1,0:T(8,128)(2,1)S(1)}, bf16[4,2,128,128]{3,2,1,0:T(8,128)(2,1)S(1)}, u32[]{:S(2)}, u32[]{:S(2)}) collective-permute-start(bf16[4,2,128,128]{3,2,1,0:T(8,128)(2,1)S(1)} %get-tuple-element.25.new_a), channel_id=1, source_target_pairs={{0,64},{32,96},{64,0},{96,32},{1,65},{33,97},{65,1},{97,33},{2,66}... | collective-permute-start | bytes 786440 | tf_op jit(solution)/shard_map/ppermute | solution.py:540
  169.9 14.9 %collective-permute-start.9 = (bf16[4,2,128,128]{3,2,1,0:T(8,128)(2,1)S(1)}, bf16[4,2,128,128]{3,2,1,0:T(8,128)(2,1)S(1)}, u32[]{:S(2)}, u32[]{:S(2)}) collective-permute-start(bf16[4,2,128,128]{3,2,1,0:T(8,128)(2,1)S(1)} %get-tuple-element.25.new_a), channel_id=1, source_target_pairs={{0,32},{32,64},{64,96},{96,0},{1,33},{33,65},{65,97},{97,1},{2,34}... | collective-permute-start | bytes 786440 | tf_op jit(solution)/shard_map/ppermute | solution.py:540
  181.9 6.4 %collective-permute-start.8 = (bf16[128,1024]{1,0:T(8,128)(2,1)S(1)}, bf16[128,1024]{1,0:T(8,128)(2,1)S(1)}, u32[]{:S(2)}, u32[]{:S(2)}) collective-permute-start(bf16[128,1024]{1,0:T(8,128)(2,1)S(1)} %combine.1.a), channel_id=1, source_target_pairs={{0,24},{8,0},{16,8},{24,16},{1,25},{9,1},{17,9},{25,17},{2,26},{10... | collective-permute-start | bytes 786440 | tf_op jit(solution)/shard_map/ppermute | solution.py:540
  183.1 8.0 %collective-permute-start.7 = (bf16[128,1024]{1,0:T(8,128)(2,1)S(1)}, bf16[128,1024]{1,0:T(8,128)(2,1)S(1)}, u32[]{:S(2)}, u32[]{:S(2)}) collective-permute-start(bf16[128,1024]{1,0:T(8,128)(2,1)S(1)} %combine.1.a), channel_id=1, source_target_pairs={{0,16},{8,24},{16,0},{24,8},{1,17},{9,25},{17,1},{25,9},{2,18},{10... | collective-permute-start | bytes 786440 | tf_op jit(solution)/shard_map/ppermute | solution.py:540
  184.6 9.2 %collective-permute-start.6 = (bf16[128,1024]{1,0:T(8,128)(2,1)S(1)}, bf16[128,1024]{1,0:T(8,128)(2,1)S(1)}, u32[]{:S(2)}, u32[]{:S(2)}) collective-permute-start(bf16[128,1024]{1,0:T(8,128)(2,1)S(1)} %combine.1.a), channel_id=1, source_target_pairs={{0,8},{8,16},{16,24},{24,0},{1,9},{9,17},{17,25},{25,1},{2,10},{10... | collective-permute-start | bytes 786440 | tf_op jit(solution)/shard_map/ppermute | solution.py:540
  193.8 2.2 copy-start.7
  200.5 2.7 %collective-permute-start.12 = (bf16[4,512,256]{2,1,0:T(8,128)(2,1)S(1)}, bf16[4,512,256]{2,1,0:T(8,128)(2,1)S(1)}, u32[]{:S(2)}, u32[]{:S(2)}) collective-permute-start(bf16[4,512,256]{2,1,0:T(8,128)(2,1)S(1)} %get-tuple-element.28), channel_id=1, source_target_pairs={{0,1},{1,0},{2,3},{3,2},{4,5},{5,4},{6,7},{7,6},{8,9},{9,8},{10,11... | collective-permute-start | bytes 3145736 | tf_op jit(solution)/shard_map/ppermute | solution.py:615

commit v4 on v2

--- a/solution.py
+++ b/solution.py
@@ -10,15 +10,17 @@
 F32 = jnp.float32
 BF16 = jnp.bfloat16
 VMEM_BYTES = 30 * 1024 * 1024
+VMEM_MOST = 58 * 1024 * 1024
 CHUNK = 4
 TAIL = 2
 ROOM = 60.0
+NO_COST = pl.CostEstimate(flops=1, bytes_accessed=1, transcendentals=0)
 CTX = 4
 NT = (((1,), (1,)), ((), ()))
 
 
-def params():
-    return pltpu.CompilerParams(vmem_limit_bytes=VMEM_BYTES)
+def params(size=VMEM_BYTES):
+    return pltpu.CompilerParams(vmem_limit_bytes=size)
 
 
 def vmem():
@@ -33,53 +35,82 @@
     return pl.BlockSpec(memory_space=pl.ANY)
 
 
-def project_kernel(tok_ref, gain_ref, wq_ref, wk_ref, wv_ref, out_ref):
-    wide = tok_ref[...].astype(F32)
-    normalized = (wide * gain_ref[...]).astype(BF16)
-    q_cols = wq_ref.shape[1]
-    rows = tok_ref.shape[0]
-    start = pl.program_id(0) == 0
-
-    def add(cols, value):
-        @pl.when(start)
-        def _():
-            out_ref[:, cols] = value
-
-        @pl.when(jnp.logical_not(start))
-        def _():
-            out_ref[:, cols] += value
-
-    for j in range(0, q_cols, 512):
-        add(
-            slice(j, j + 512),
-            jnp.dot(normalized, wq_ref[:, j : j + 512], preferred_element_type=F32),
+def project_kernel(
+    tok_ref, gain_ref, wq_ref, wk_ref, wv_ref, out_ref, tok, wq, wkv, norm, total, in_sems, out_sems
+):
+    rows, features = tok.shape
+    q_cols = wq.shape[1]
+    step = 256
+    count = q_cols // step
+    half = rows // 2
+    fetch_tok = [
+        pltpu.make_async_copy(
+            tok_ref.at[pl.ds(n * half, half)], tok.at[pl.ds(n * half, half)], in_sems.at[n]
         )
-    both = jnp.concatenate([wk_ref[...], wv_ref[...]], axis=1)
-    add(slice(q_cols, q_cols + 256), jnp.dot(normalized, both, preferred_element_type=F32))
-    squares = jnp.sum(wide * wide, axis=1, keepdims=True)
-    add(slice(q_cols + 256, q_cols + 384), jnp.broadcast_to(squares, (rows, 128)))
+        for n in range(2)
+    ]
+    fetch_w = [
+        pltpu.make_async_copy(
+            wq_ref.at[:, pl.ds(n * step, step)], wq.at[:, pl.ds(n * step, step)], in_sems.at[2 + n]
+        )
+        for n in range(count)
+    ]
+    fetch_kv = [
+        pltpu.make_async_copy(ref, wkv.at[:, pl.ds(n * 128, 128)], in_sems.at[2 + count + n])
+        for n, ref in enumerate((wk_ref, wv_ref))
+    ]
+    for copy in fetch_tok + fetch_w + fetch_kv:
+        copy.start()
+    sent = []
+
+    def send(first, width):
+        cols = pl.ds(first, width)
+        sent.append(
+            pltpu.make_async_copy(total.at[:, cols], out_ref.at[:, cols], out_sems.at[len(sent)])
+        )
+        sent[-1].start()
+
+    for n, copy in enumerate(fetch_tok):
+        copy.wait()
+        part = slice(n * half, n * half + half)
+        wide = tok[part].astype(F32)
+        norm[part] = (wide * gain_ref[...]).astype(BF16)
+        squares = jnp.sum(wide * wide, axis=1, keepdims=True)
+        total[part, q_cols + 256 :] = jnp.broadcast_to(squares, (half, 128))
+    send(q_cols + 256, 128)
+    for n, copy in enumerate(fetch_w):
+        copy.wait()
+        cols = slice(n * step, n * step + step)
+        total[:, cols] = jnp.dot(norm[...], wq[:, cols], preferred_element_type=F32)
+        send(n * step, step)
+    for copy in fetch_kv:
+        copy.wait()
+    total[:, q_cols : q_cols + 256] = jnp.dot(norm[...], wkv[...], preferred_element_type=F32)
+    send(q_cols, 256)
+    for copy in sent:
+        copy.wait()
 
 
 def project(tokens, gain, w_query, w_key, w_value):
     rows, features = tokens.shape
-    cols = w_query.shape[1] + 384
-    deep = features // 4
+    q_cols = w_query.shape[1]
+    cols = q_cols + 384
     return pl.pallas_call(
         project_kernel,
-        grid=(4,),
         out_shape=jax.ShapeDtypeStruct((rows, cols), F32),
-        in_specs=[
-            pl.BlockSpec((rows, deep), lambda i: (0, i)),
-            pl.BlockSpec((1, deep), lambda i: (0, i)),
-            pl.BlockSpec((deep, w_query.shape[1]), lambda i: (i, 0)),
-            pl.BlockSpec((deep, 128), lambda i: (i, 0)),
-            pl.BlockSpec((deep, 128), lambda i: (i, 0)),
+        in_specs=[anywhere(), vmem(), anywhere(), anywhere(), anywhere()],
+        out_specs=anywhere(),
+        scratch_shapes=[
+            pltpu.VMEM((rows, features), BF16),
+            pltpu.VMEM((features, q_cols), BF16),
+            pltpu.VMEM((features, 256), BF16),
+            pltpu.VMEM((rows, features), BF16),
+            pltpu.VMEM((rows, cols), F32),
+            pltpu.SemaphoreType.DMA((4 + q_cols // 256,)),
+            pltpu.SemaphoreType.DMA((2 + q_cols // 256,)),
         ],
-        out_specs=pl.BlockSpec((rows, cols), lambda i: (0, 0)),
-        compiler_params=params(),
-        cost_estimate=pl.CostEstimate(
-            flops=2 * rows * cols * features, bytes_accessed=10 << 20, transcendentals=0
-        ),
+        compiler_params=params(VMEM_MOST),
+        cost_estimate=NO_COST,
         name="project",
     )(tokens, gain, w_query, w_key, w_value)
 
@@ -107,25 +138,46 @@
         in_specs=[vmem()],
         out_specs=[vmem()] * 2,
         compiler_params=params(),
+        cost_estimate=NO_COST,
         name="finish",
     )(parts)
 
 
-def pack_kernel(index_ref, pool_ref, out_ref, sem):
-    for n in range(out_ref.shape[0]):
-        pltpu.make_async_copy(pool_ref.at[index_ref[n]], out_ref.at[n], sem).start()
-    pltpu.make_async_copy(out_ref, out_ref, sem).wait()
+def pack_kernel(index_ref, pool_ref, *refs):
+    steps = index_ref.shape[0]
+    outs = refs[:steps]
+    pool_out, pool, held, sems = refs[steps:]
+    fetch = pltpu.make_async_copy(pool_ref, pool, sems.at[steps])
+    fetch.start()
+    fetch.wait()
+    copies = []
+    for step in range(steps):
+        for n in range(held.shape[1]):
+            held[step, n] = pool[index_ref[step, n]]
+        copies.append(pltpu.make_async_copy(held.at[step], outs[step], sems.at[step]))
+        copies[-1].start()
+    copies.append(pltpu.make_async_copy(pool, pool_out, sems.at[steps]))
+    copies[-1].start()
+    for copy in copies:
+        copy.wait()
 
 
 def pack(index, pool):
-    count = index.shape[0]
+    steps, count = index.shape
+    block = pool.shape[1:]
     return pl.pallas_call(
         pack_kernel,
-        out_shape=jax.ShapeDtypeStruct((count,) + pool.shape[1:], BF16),
+        out_shape=[jax.ShapeDtypeStruct((count,) + block, BF16)] * steps
+        + [jax.ShapeDtypeStruct(pool.shape, BF16)],
         in_specs=[smem(), anywhere()],
-        out_specs=anywhere(),
-        scratch_shapes=[pltpu.SemaphoreType.DMA(())],
-        compiler_params=params(),
+        out_specs=[anywhere()] * (steps + 1),
+        scratch_shapes=[
+            pltpu.VMEM(pool.shape, BF16),
+            pltpu.VMEM((steps, count) + block, BF16),
+            pltpu.SemaphoreType.DMA((steps + 1,)),
+        ],
+        compiler_params=params(VMEM_MOST),
+        cost_estimate=NO_COST,
         name="pack",
     )(index, pool)
 
@@ -240,12 +292,11 @@
 
 
 def first_kernel(
-    new_len, const, meta_ref, index_ref, a, b, c, d, pool_ref,
+    new_len, const, meta_ref, a, b, c, d, buf,
     q_ref, qn_ref, acc_ref, mp_ref, lp_ref, kv_ref, vx_ref, m_ref, l_ref, sem,
 ):
-    blocks = kv_ref.shape[0]
-    for n in range(blocks):
-        pltpu.make_async_copy(pool_ref.at[index_ref[n]], kv_ref.at[n], sem).start()
+    fetch = pltpu.make_async_copy(buf, kv_ref, sem)
+    fetch.start()
     tokens, q_cols = q_ref.shape
     part = a.shape[0]
     heads = m_ref.shape[0]
@@ -272,7 +323,7 @@
     token = lax.broadcasted_iota(jnp.int32, (new_len, part), 0)
     fresh = lax.broadcasted_iota(jnp.int32, (new_len, part), 1) + offset
     moving(q_ref, m_ref, l_ref, acc_ref, rows, keys, values_ext, fresh <= token, const, True)
-    pltpu.make_async_copy(kv_ref, kv_ref, sem).wait()
+    fetch.wait()
     prefix_part(
         meta_ref, 1, q_ref, qn_ref, kv_ref, vx_ref, m_ref, l_ref, acc_ref, new_len, const
     )
@@ -306,37 +357,30 @@
 
 
 def near_kernel(
-    new_len, const, meta_ref, q_ref, qn_ref, acc_in, mp_in, lp_in, buf_a, buf_b, pool_ref,
-    acc_ref, mp_ref, lp_ref, pool_out, kv_ref, vx_ref, m_ref, l_ref, sems, pool_sem,
+    new_len, const, meta_ref, q_ref, qn_ref, acc_in, mp_in, lp_in, buf_a, buf_b,
+    acc_ref, mp_ref, lp_ref, kv_ref, vx_ref, m_ref, l_ref, sems,
 ):
-    keep = pltpu.make_async_copy(pool_ref, pool_out, pool_sem)
-    keep.start()
     sources(
         new_len, const, meta_ref, q_ref, qn_ref, (buf_a, buf_b), acc_in, mp_in, lp_in,
         acc_ref, kv_ref, vx_ref, m_ref, l_ref, sems,
     )
     mp_ref[...] = pack_lanes(m_ref, slice(None))
     lp_ref[...] = pack_lanes(l_ref, slice(None))
-    keep.wait()
 
 
 def last_kernel(
-    new_len, const, meta_ref, place_ref, q_ref, qn_ref, acc_in, mp_in, lp_in, buf,
-    new_a, new_b, new_c, new_d, pool_in, out_ref, pool_out,
-    acc_ref, kv_ref, vx_ref, m_ref, l_ref, sems, new_sems,
+    new_len, const, meta_ref, place_ref, q_ref, qn_ref, acc_in, mp_in, lp_in, buf, new_ref, pool_in,
+    out_a, out_b, out_c, out_d, pool_out, acc_ref, kv_ref, vx_ref, m_ref, l_ref, sems, new_sems,
 ):
-    def place(act):
-        count = new_a.shape[0]
-        for n, ref in enumerate((new_a, new_b, new_c, new_d)):
-            for i in range(count):
-                at = n * count + i
-                slot = place_ref[at]
-
-                @pl.when(slot >= 0)
-                def _(ref=ref, i=i, at=at, slot=slot):
-                    act(pltpu.make_async_copy(ref.at[i], pool_out.at[slot], new_sems.at[at]))
-
-    place(lambda copy: copy.start())
+    def place_blocks(act):
+        for n in range(new_ref.shape[0]):
+            slot = place_ref[n]
+
+            @pl.when(slot >= 0)
+            def _(n=n, slot=slot):
+                act(pltpu.make_async_copy(new_ref.at[n], pool_out.at[slot], new_sems.at[n]))
+
+    place_blocks(lambda copy: copy.start())
     sources(
         new_len, const, meta_ref, q_ref, qn_ref, (buf,), acc_in, mp_in, lp_in,
         acc_ref, kv_ref, vx_ref, m_ref, l_ref, sems,
@@ -344,32 +388,29 @@
     tokens = q_ref.shape[0]
     heads = m_ref.shape[0]
     part = tokens // CTX
-    for head in range(heads):
-        cols = slice(head * 128, head * 128 + 128)
-        total = l_ref[head]
-        empty = total == 0.0
-        safe = jnp.where(empty, 1.0, total)
-        done = (acc_ref[:, cols] / safe).astype(BF16)
-        for c in range(CTX):
-            out_ref[c, :part, cols] = done[c * part : (c + 1) * part]
-        m_ref[head] = jnp.where(empty, NEG_FILL, m_ref[head] + jnp.log2(safe))
-    packed = pack_lanes(m_ref, slice(None))
+    rank = meta_ref[4]
     row = lax.broadcasted_iota(jnp.int32, (16, heads * 128), 0)
-    for c in range(CTX):
-        turned = packed[c * part : (c + 1) * part].T
+    for step, out_ref in enumerate((out_a, out_b, out_c, out_d)):
+        place = lax.rem(rank + step, CTX)
+        rows = pl.ds(pl.multiple_of(place * part, part), part)
+        for head in range(heads):
+            cols = slice(head * 128, head * 128 + 128)
+            total = l_ref[head, rows, :]
+            empty = total == 0.0
+            safe = jnp.where(empty, 1.0, total)
+            out_ref[:part, cols] = (acc_ref[rows, cols] / safe).astype(BF16)
+            m_ref[head, rows, :] = jnp.where(
+                empty, NEG_FILL, m_ref[head, rows, :] + jnp.log2(safe)
+            )
+        turned = pack_lanes(m_ref, rows).T
         line = jnp.concatenate([turned[h : h + 1] for h in range(heads)], axis=1)
         high = line.astype(BF16).astype(F32)
         rest = line - high
         mid = rest.astype(BF16).astype(F32)
         low = rest - mid
         tile = jnp.where(row == 0, high, jnp.where(row == 1, mid, jnp.where(row == 2, low, 0.0)))
-        out_ref[c, part : part + 16, :] = tile.astype(BF16)
-    place(lambda copy: copy.wait())
-
-
-def attend_cost(blocks, tokens, heads):
-    pairs = blocks * 128 * tokens // 2 * heads
-    return pl.CostEstimate(flops=pairs * 512, bytes_accessed=8 << 20, transcendentals=pairs)
+        out_ref[part : part + 16, :] = tile.astype(BF16)
+    place_blocks(lambda copy: copy.wait())
 
 
 def scratch(tokens, heads, blocks, lead=()):
@@ -389,12 +430,12 @@
     ]
 
 
-def attend_own(meta, index, quarters, pool, new_len, const):
+def attend_own(meta, quarters, buf, new_len, const):
     part = quarters[0].shape[0]
     q_cols = quarters[0].shape[1] - 256
     tokens = part * CTX
     heads = q_cols // 128
-    blocks = index.shape[0]
+    blocks = buf.shape[0]
     return pl.pallas_call(
         lambda *refs: first_kernel(new_len, const, *refs),
         out_shape=[
@@ -402,30 +443,30 @@
             jax.ShapeDtypeStruct((tokens, 128), F32),
         ]
         + state_shapes(tokens, q_cols),
-        in_specs=[smem(), smem()] + [vmem()] * 4 + [anywhere()],
+        in_specs=[smem()] + [vmem()] * 4 + [anywhere()],
         out_specs=[vmem()] * 5,
         scratch_shapes=scratch(tokens, heads, blocks) + [pltpu.SemaphoreType.DMA(())],
         compiler_params=params(),
-        cost_estimate=attend_cost(blocks, tokens, heads),
+        cost_estimate=NO_COST,
         name="attend_own",
-    )(meta, index, *quarters, pool)
-
-
-def attend_near(meta, queries, norms, state, bufs, pool, new_len, const):
+    )(meta, *quarters, buf)
+
+
+def attend_near(meta, queries, norms, state, bufs, new_len, const):
     tokens, q_cols = queries.shape
     heads = q_cols // 128
     blocks = bufs[0].shape[0]
     return pl.pallas_call(
         lambda *refs: near_kernel(new_len, const, *refs),
-        out_shape=state_shapes(tokens, q_cols) + [jax.ShapeDtypeStruct(pool.shape, BF16)],
-        in_specs=[smem()] + [vmem()] * 5 + [anywhere()] * 3,
-        out_specs=[vmem()] * 3 + [anywhere()],
+        out_shape=state_shapes(tokens, q_cols),
+        in_specs=[smem()] + [vmem()] * 5 + [anywhere()] * 2,
+        out_specs=[vmem()] * 3,
         scratch_shapes=scratch(tokens, heads, blocks, (2,))
-        + [pltpu.SemaphoreType.DMA((2,)), pltpu.SemaphoreType.DMA(())],
+        + [pltpu.SemaphoreType.DMA((2,))],
         compiler_params=params(),
-        cost_estimate=attend_cost(2 * blocks, tokens, heads),
+        cost_estimate=NO_COST,
         name="attend_near",
-    )(meta, queries, norms, *state, *bufs, pool)
+    )(meta, queries, norms, *state, *bufs)
 
 
 def attend_last(meta, places, queries, norms, state, buf, news, pool, new_len, const):
@@ -434,28 +475,27 @@
     blocks = buf.shape[0]
     return pl.pallas_call(
         lambda *refs: last_kernel(new_len, const, *refs),
-        out_shape=[
-            jax.ShapeDtypeStruct((CTX, tokens // CTX + 16, q_cols), BF16),
-            jax.ShapeDtypeStruct(pool.shape, BF16),
-        ],
-        in_specs=[smem(), smem()] + [vmem()] * 5 + [anywhere()] * 6,
-        out_specs=[vmem(), anywhere()],
+        out_shape=[jax.ShapeDtypeStruct((tokens // CTX + 16, q_cols), BF16)] * CTX
+        + [jax.ShapeDtypeStruct(pool.shape, BF16)],
+        in_specs=[smem(), smem()] + [vmem()] * 5 + [anywhere()] * 3,
+        out_specs=[vmem()] * CTX + [anywhere()],
         scratch_shapes=[pltpu.VMEM((tokens, q_cols), F32)]
         + scratch(tokens, heads, blocks, (1,))
         + [pltpu.SemaphoreType.DMA((1,)), pltpu.SemaphoreType.DMA((places.shape[0],))],
-        input_output_aliases={12: 1},
+        input_output_aliases={9: CTX},
         compiler_params=params(),
-        cost_estimate=attend_cost(blocks, tokens, heads),
+        cost_estimate=NO_COST,
         name="attend_last",
-    )(meta, places, queries, norms, *state, buf, *news, pool)
-
-
-def combine_kernel(in_ref, out_ref):
+    )(meta, places, queries, norms, *state, buf, news, pool)
+
+
+def combine_kernel(*refs):
+    in_refs, out_ref = refs[:CTX], refs[CTX]
     part, q_cols = out_ref.shape
     heads = q_cols // 128
     lines = []
     for c in range(CTX):
-        tile = in_ref[c, part : part + 16, :].astype(F32)
+        tile = in_refs[c][part : part + 16, :].astype(F32)
         lines.append(tile[0:1] + tile[1:2] + tile[2:3])
     top = lines[0]
     for line in lines[1:]:
@@ -473,20 +513,21 @@
         mixed = jnp.zeros((part, 128), F32)
         for c in range(CTX):
             at = c * heads + head
-            mixed = mixed + in_ref[c, :part, cols].astype(F32) * turned[:, at : at + 1]
+            mixed = mixed + in_refs[c][:part, cols].astype(F32) * turned[:, at : at + 1]
         out_ref[:, cols] = mixed.astype(BF16)
 
 
 def combine(arrived):
-    count, rows, q_cols = arrived.shape
+    rows, q_cols = arrived[0].shape
     return pl.pallas_call(
         combine_kernel,
         out_shape=jax.ShapeDtypeStruct((rows - 16, q_cols), BF16),
-        in_specs=[vmem()],
+        in_specs=[vmem()] * CTX,
         out_specs=vmem(),
         compiler_params=params(),
+        cost_estimate=NO_COST,
         name="combine",
-    )(arrived)
+    )(*arrived)
 
 
 def out_kernel(meta_ref, a, b, c, d, w_ref, own_ref, send_ref, rows_ref):
@@ -518,21 +559,24 @@
     part, depth = quarters[0].shape
     tokens = part * CTX
     width = w_out.shape[1] // planes
-    whole = pl.BlockSpec((part, depth), lambda i: (0, 0))
+    whole = pl.BlockSpec((part, depth), lambda i, meta: (0, 0))
+    out = pl.BlockSpec((1, tokens, width // 2), lambda i, meta: (i, 0, 0))
     return pl.pallas_call(
         out_kernel,
-        grid=(planes,),
+        grid_spec=pltpu.PrefetchScalarGridSpec(
+            num_scalar_prefetch=1,
+            grid=(planes,),
+            in_specs=[whole] * 4
+            + [pl.BlockSpec((depth, width), lambda i, meta: (0, lax.rem(meta[2] + i, planes)))],
+            out_specs=[out] * 2,
+            scratch_shapes=[pltpu.VMEM((tokens, depth), BF16)],
+        ),
         out_shape=[
             jax.ShapeDtypeStruct((planes, tokens, width // 2), F32),
             jax.ShapeDtypeStruct((planes, tokens, width // 2), BF16),
         ],
-        in_specs=[smem(), whole, whole, whole, whole, pl.BlockSpec((depth, width), lambda i: (0, i))],
-        out_specs=[pl.BlockSpec((1, tokens, width // 2), lambda i: (i, 0, 0))] * 2,
-        scratch_shapes=[pltpu.VMEM((tokens, depth), BF16)],
-        compiler_params=params(),
-        cost_estimate=pl.CostEstimate(
-            flops=2 * tokens * depth * w_out.shape[1], bytes_accessed=8 << 20, transcendentals=0
-        ),
+        compiler_params=params(VMEM_MOST),
+        cost_estimate=NO_COST,
         name="project_out",
     )(meta, *quarters, w_out)
 
@@ -555,6 +599,7 @@
     rank = lax.axis_index("ctx")
     group = lax.axis_index("group")
     core = lax.axis_index("tp") % 2
+    plane = lax.axis_index("tp") // 2
     pool_size = kv_pool.shape[0]
     sessions, list_len = block_table.shape
     sess_here = sessions // groups
@@ -574,7 +619,7 @@
     wanted = jnp.arange(1, per_pair + 1, dtype=jnp.int32)
     picked = here[:, None, :] & (order[:, None, :] == wanted[None, :, None])
     send_index = jnp.sum(jnp.where(picked, send_table[:, None, :] % pool_size, 0), axis=2)
-    blocks = {step: pack(send_index[step], pool) for step in (1, 3, 2)}
+    *blocks, new_pool = pack(send_index, pool)
     arrived = {step: shifted(blocks[step], "group", step) for step in (1, 3, 2)}
 
     mine = lax.dynamic_index_in_dim(table, group, 0, keepdims=False).reshape(sess_here, list_len)
@@ -588,51 +633,39 @@
     starts = jnp.cumsum(counts, axis=1) - counts
     meta = jnp.stack([starts, live_keys], axis=2).reshape(groups, 2 * sess_here).astype(jnp.int32)
 
-    tokens, _ = lax.optimization_barrier((tokens, blocks))
     parts = project(tokens, norm_gain[None, :], w_query, w_key, w_value)
     part_rows = tokens.shape[0] // ranks
     parts = parts.reshape(ranks, part_rows, parts.shape[1])
     parts = lax.all_to_all(parts, "ctx", split_axis=0, concat_axis=0, tiled=True)
     fresh, block = finish(parts, tokens.shape[1] * ranks)
+    news = lax.all_gather(block, ("group", "ctx"))
+    targets = write_slot.reshape(-1)
+    places = jnp.where(targets // pool_size == device_id, targets % pool_size, -1)
     quarters = around(fresh, "ctx")
-    news = around(jnp.stack(around(block, "group")), "ctx")
-    targets = write_slot.reshape(groups, ranks)
-    targets = jnp.stack(
-        [targets[(group - g) % groups, (rank - c) % ranks] for c in range(ranks) for g in range(groups)]
-    )
-    places = jnp.where(targets // pool_size == device_id, targets % pool_size, -1)
-
-    first_meta = jnp.concatenate([rank[None].astype(jnp.int32), meta[0]])
-    queries, norms, *state = attend_own(
-        first_meta, send_index[0], quarters, pool, new_len, const
-    )
+
+    rank_only = rank[None].astype(jnp.int32)
+    first_meta = jnp.concatenate([rank_only, meta[0]])
+    queries, norms, *state = attend_own(first_meta, quarters, blocks[0], new_len, const)
     near_meta = jnp.concatenate([meta[1], meta[3]])
-    *state, new_pool = attend_near(
-        near_meta, queries, norms, state, [arrived[1], arrived[3]], pool, new_len, const
-    )
-    partial, new_pool = attend_last(
-        meta[2], places, queries, norms, state, arrived[2], news, new_pool, new_len, const
-    )
-    partial = lax.all_to_all(partial, "ctx", split_axis=0, concat_axis=0, tiled=True)
+    state = attend_near(
+        near_meta, queries, norms, state, [arrived[1], arrived[3]], new_len, const
+    )
+    last_meta = jnp.concatenate([meta[2], rank_only])
+    *partial, new_pool = attend_last(
+        last_meta, places, queries, norms, state, arrived[2], news, new_pool, new_len, const
+    )
+    partial = [partial[0]] + [shifted(partial[step], "ctx", step) for step in (1, 2, 3)]
     attended = combine(partial)
 
     planes = tp_size // 2
-    out_meta = jnp.stack([rank, core]).astype(jnp.int32)
+    out_meta = jnp.stack([rank, core, plane]).astype(jnp.int32)
     own, send = project_out(out_meta, around(attended, "ctx"), w_out, planes)
     other = lax.ppermute(send, "tp", [(i, i ^ 1) for i in range(tp_size)])
-    pair = (own + other.astype(F32)).astype(BF16)
-    terms = lax.all_to_all(
-        pair,
-        "tp",
-        split_axis=0,
-        concat_axis=0,
-        axis_index_groups=[[2 * z + c for z in range(planes)] for c in range(2)],
-        tiled=True,
-    )
-    attention_out = jnp.sum(terms.astype(F32), axis=0).astype(BF16)
-
-    new_pool = new_pool.reshape(kv_pool.shape)
-    return (attention_out, new_pool)
+    total = own[0] + other[0].astype(F32)
+    for step in range(1, planes):
+        pair = (own[step] + other[step].astype(F32)).astype(BF16)
+        total = total + shifted(pair, "tp", 2 * step).astype(F32)
+    return (total.astype(BF16), new_pool.reshape(kv_pool.shape))
 
 
 def solution(mesh):

time: 296 us -> 229 us (0.77); the launches traced: 296 us -> 225 us
  blocking collectives: 39.9 us -> 0 us
  waiting for transfers between devices: 109 us -> 76.9 us
  local copies, waits for them, and re-layouts: 24.6 us -> 9.69 us
  between operations: 0.91 us -> 14.2 us
  Pallas kernels: 99.2 us -> 95.3 us
  other arithmetic: 2.26 us -> 5.62 us
    all_to_all x2 -> x0, blocking collectives: 39.9 us -> none  [the longest x1 20.5 us: local(): lax.all_to_all(pair, 'tp', split_axis=0, concat_axis=0, axis_index_groups...]
    ppermute x15, waiting for transfers between devices: 74.9 us -> 51.5 us  [shifted(): lax.ppermute(value, axis, [(i, (i + step) % size) for i in range(size)])]
    another operation x1 -> x0, local copies, waits for them, and re-layouts: 10 us -> none  [local(): jnp.stack([targets[(group - g) % groups, (rank - c) % ranks] for c in ran...]
    all_to_all x1, waiting for transfers between devices: 31 us -> 22.5 us  [local(): lax.all_to_all(parts, 'ctx', split_axis=0, concat_axis=0, tiled=True)]
    pallas_call x1, Pallas kernels: 21.8 us -> 16.9 us  [attend_own(): pl.pallas_call(lambda *refs: first_kernel(new_len, const, *refs), out_sha...]
    unnamed x31, local copies, waits for them, and re-layouts: 12.3 us -> 8.75 us
    convert_element_type x1 -> x2, other arithmetic: 0.37 us -> 3.49 us  [the longest x1 1.91 us: local(): return (total.astype(BF16), new_pool.reshape(kv_pool.shape))]
    pallas_call x5 -> x3, Pallas kernels: 21.6 us -> 24.1 us  [the longest x1 9.26 us: project(): pl.pallas_call(project_kernel, out_shape=jax.ShapeDtypeStruct((rows, cols...]
  transfers between devices with their start and end apart: 17 -> 18, of which waited for: 9 -> 9; matrix products, arithmetic and copies ran while one was open for 4% -> 2% of each run, Pallas kernels for 19% -> 26%
where the time goes in v4:
time: 229 us; the launch traced here: 225 us
  Pallas kernels  95.3 us (42%)
  waiting for transfers between devices  76.9 us (34%)
  starting transfers between devices  22.7 us (10%)
  between operations  14.2 us (6%)
  local copies, waits for them, and re-layouts  9.69 us (4%)
  other arithmetic  5.62 us (2%)
    ppermute x15, waiting for transfers between devices, shifted(): lax.ppermute(value, axis, [(i, (i + step) % size) for i in range(size)])  51.5 us
    pallas_call x1, Pallas kernels, attend_near(): pl.pallas_call(lambda *refs: near_kernel(new_len, const, *refs), out_shap...  32.9 us
    all_to_all x1, waiting for transfers between devices, local(): lax.all_to_all(parts, 'ctx', split_axis=0, concat_axis=0, tiled=True)  22.5 us
    pallas_call x1, Pallas kernels, attend_last(): pl.pallas_call(lambda *refs: last_kernel(new_len, const, *refs), out_shap...  19.8 us
    ppermute x15, starting transfers between devices, shifted(): lax.ppermute(value, axis, [(i, (i + step) % size) for i in range(size)])  18.3 us
    pallas_call x1, Pallas kernels, attend_own(): pl.pallas_call(lambda *refs: first_kernel(new_len, const, *refs), out_sha...  16.9 us
    pallas_call x1, Pallas kernels, project(): pl.pallas_call(project_kernel, out_shape=jax.ShapeDtypeStruct((rows, cols...  9.26 us
    unnamed x31, local copies, waits for them, and re-layouts  8.75 us
  transfers between devices with their start and end apart: 18, of which 9 were waited for; matrix products, arithmetic and copies ran while one was open for 2% of the time, Pallas kernels for 26%

profile of v4, /device:TPU:24, one launch (start us, length us, event | category | flops | bytes accessed | tf_op | source)
XLA Modules:
  0.0 224.7 jit_solution(14017717072848048801)
XLA Ops:
  7.2 9.3 %project.1 = f32[512,1408]{1,0:T(8,128)} custom-call(bf16[512,2048]{1,0:T(8,128)(2,1)} %tok_ref.1, f32[1,2048]{1,0:T(1,128)} %bitcast.33, bf16[2048,1024]{1,0:T(8,128)(2,1)} %wq_ref.1, bf16[2048,128]{1,0:T(8,128)(2,1)} %wk_ref.1, bf16[2048,128]{1,0:T(8,128)(2,1)} %wv_ref.1), custom_call_target="tpu_custom_call" | custom-call | flops 1 | bytes 1 | tf_op jit(solution)/shard_map/project/pallas_call | solution.py:98
  16.4 4.3 %all-to-all-start = ((f32[4,128,1408]{2,1,0:T(8,128)}), f32[4,128,1408]{2,1,0:T(8,128)S(1)}, u32[]{:S(2)}, u32[]{:S(2)}) async-start(f32[4,128,1408]{2,1,0:T(8,128)} %bitcast.29), calls=%async_computation | async-start | bytes 5767168 | tf_op jit(solution)/shard_map/all_to_all | solution.py:639
  20.9 0.3 convolution_convert_fusion
  21.1 0.8 select_reduce_fusion.index_ref
  22.0 7.7 %pack.1 = (bf16[32,2,128,128]{3,2,1,0:T(8,128)(2,1)}, bf16[32,2,128,128]{3,2,1,0:T(8,128)(2,1)}, bf16[32,2,128,128]{3,2,1,0:T(8,128)(2,1)}, bf16[32,2,128,128]{3,2,1,0:T(8,128)(2,1)}, bf16[64,2,128,128]{3,2,1,0:T(8,128)(2,1)}) custom-call(s32[4,32]{1,0:T(4,128)} %select_reduce_fusion.index_ref, bf16[64,2,128,128]{3,2,1,0:T(8,128)(2,1)} %bitcast.31), custom_call_target="tpu_custom_call" | custom-call | flops 1 | bytes 1 | tf_op jit(solution)/shard_map/pack/pallas_call | solution.py:168
  29.7 0.3 collective-permute-start.3
  30.0 1.8 collective-permute-start.4
  31.8 1.2 collective-permute-start.5
  33.0 22.5 %all-to-all-done.refs_0_ = f32[4,128,1408]{2,1,0:T(8,128)S(1)} async-done(((f32[4,128,1408]{2,1,0:T(8,128)}), f32[4,128,1408]{2,1,0:T(8,128)S(1)}, u32[]{:S(2)}, u32[]{:S(2)}) %all-to-all-start) | async-done | bytes 2883616 | tf_op jit(solution)/shard_map/all_to_all | solution.py:639
  55.5 0.8 finish.1
  56.4 0.1 dynamic_slice.12
  56.4 0.1 and_select_fusion
  56.5 0.2 fusion.12
  56.8 0.6 collective-permute-start
  57.4 0.1 fusion.16
  57.5 0.1 copy.31
  57.6 0.1 squeeze.10
  57.7 0.1 copy.32
  57.7 0.1 reshape.174
  57.8 0.1 copy.33
  57.9 0.1 squeeze.11
  58.0 0.1 copy.35
  58.1 0.1 squeeze.13
  58.2 0.1 copy.34
  58.3 0.1 squeeze.12
  58.4 0.1 pad_add_fusion.2.refs_0_
  58.5 0.1 pad_add_fusion.3.refs_0_
  58.5 2.1 collective-permute-start.1
  60.6 13.4 %collective-permute-done.refs_2_ = bf16[128,1280]{1,0:T(8,128)(2,1)S(1)} collective-permute-done((bf16[128,1280]{1,0:T(8,128)(2,1)S(1)}, bf16[128,1280]{1,0:T(8,128)(2,1)S(1)}, u32[]{:S(2)}, u32[]{:S(2)}) %collective-permute-start) | collective-permute-done | bytes 327712 | tf_op jit(solution)/shard_map/ppermute | solution.py:586
  74.0 0.7 copy-done.3
  74.7 0.1 pad_add_fusion.4.refs_0_
  74.8 6.4 %collective-permute-done.2.refs_4_ = bf16[128,1280]{1,0:T(8,128)(2,1)S(1)} collective-permute-done((bf16[128,1280]{1,0:T(8,128)(2,1)S(1)}, bf16[128,1280]{1,0:T(8,128)(2,1)S(1)}, u32[]{:S(2)}, u32[]{:S(2)}) %collective-permute-start.2) | collective-permute-done | bytes 327712 | tf_op jit(solution)/shard_map/ppermute | solution.py:586
  81.2 1.6 copy-done
  82.8 1.0 copy-done.4
  83.8 16.9 %attend_own.1 = (bf16[512,1024]{1,0:T(8,128)(2,1)S(1)}, f32[512,128]{1,0:T(8,128)S(1)}, f32[512,1024]{1,0:T(8,128)S(1)}, f32[512,128]{1,0:T(8,128)S(1)}, f32[512,128]{1,0:T(8,128)S(1)}) custom-call(s32[5]{0:T(128)S(1)} %pad_add_fusion.3.refs_0_, bf16[128,1280]{1,0:T(8,128)(2,1)S(1)} %copy-done.4, bf16[128,1280]{1,0:T(8,128)(2,1)S(1)} %collective-permute-done.refs_2_, ...), custom_call_target="tpu_custom_call" | custom-call | flops 1 | bytes 1 | tf_op jit(solution)/shard_map/attend_own/pallas_call | solution.py:439
  100.8 32.9 %attend_near.1 = (f32[512,1024]{1,0:T(8,128)S(1)}, f32[512,128]{1,0:T(8,128)S(1)}, f32[512,128]{1,0:T(8,128)S(1)}) custom-call(s32[8]{0:T(128)S(1)} %pad_add_fusion.4.refs_0_, bf16[512,1024]{1,0:T(8,128)(2,1)S(1)} %get-tuple-element.26.refs_1_.refs_2_, f32[512,128]{1,0:T(8,128)S(1)} %get-tuple-element.27.refs_2_.refs_3_, ...), custom_call_target="tpu_custom_call" | custom-call | flops 1 | bytes 1 | tf_op jit(solution)/shard_map/attend_near/pallas_call | solution.py:459
  133.7 0.7 copy-done.5
  134.4 0.7 copy-done.7
  135.1 1.2 copy-done.1
  136.3 0.9 copy-done.6
  137.3 0.9 copy-done.8
  138.2 19.8 %attend_last.1 = (bf16[144,1024]{1,0:T(8,128)(2,1)S(1)}, bf16[144,1024]{1,0:T(8,128)(2,1)S(1)}, bf16[144,1024]{1,0:T(8,128)(2,1)S(1)}, bf16[144,1024]{1,0:T(8,128)(2,1)S(1)}, bf16[64,2,128,128]{3,2,1,0:T(8,128)(2,1)}) custom-call(s32[5]{0:T(128)S(1)} %pad_add_fusion.2.refs_0_, s32[16]{0:T(128)S(1)} %compare_select_fusion.3.refs_1_, ...), custom_call_target="tpu_custom_call", output_to_operand_aliasing={{4}: (9, {})} | custom-call | flops 1 | bytes 1 | tf_op jit(solution)/shard_map/attend_last/pallas_call | solution.py:476
  158.0 0.1 collective-permute-start.6
  158.1 0.1 collective-permute-start.7
  158.2 3.1 %collective-permute-start.8 = (bf16[144,1024]{1,0:T(8,128)(2,1)S(1)}, bf16[144,1024]{1,0:T(8,128)(2,1)S(1)}, u32[]{:S(2)}, u32[]{:S(2)}) collective-permute-start(bf16[144,1024]{1,0:T(8,128)(2,1)S(1)} %get-tuple-element.42), channel_id=1, source_target_pairs={{0,24},{8,0},{16,8},{24,16},{1,25},{9,1},{17,9},{25,17},{2,26},{10... | collective-permute-start | bytes 884744 | tf_op jit(solution)/shard_map/ppermute | solution.py:586
  161.3 10.2 %collective-permute-done.6.refs_1_ = bf16[144,1024]{1,0:T(8,128)(2,1)S(1)} collective-permute-done((bf16[144,1024]{1,0:T(8,128)(2,1)S(1)}, bf16[144,1024]{1,0:T(8,128)(2,1)S(1)}, u32[]{:S(2)}, u32[]{:S(2)}) %collective-permute-start.6) | collective-permute-done | bytes 294944 | tf_op jit(solution)/shard_map/ppermute | solution.py:586
  171.5 0.8 combine.1.a
  172.4 0.1 collective-permute-start.9
  172.5 2.3 %collective-permute-start.10 = (bf16[128,1024]{1,0:T(8,128)(2,1)S(1)}, bf16[128,1024]{1,0:T(8,128)(2,1)S(1)}, u32[]{:S(2)}, u32[]{:S(2)}) collective-permute-start(bf16[128,1024]{1,0:T(8,128)(2,1)S(1)} %combine.1.a), channel_id=1, source_target_pairs={{0,16},{8,24},{16,0},{24,8},{1,17},{9,25},{17,1},{25,9},{2,18},{10... | collective-permute-start | bytes 786440 | tf_op jit(solution)/shard_map/ppermute | solution.py:586
  174.8 1.1 collective-permute-start.11
  175.9 0.6 pad_add_fusion.1.meta_ref
  176.5 7.2 %collective-permute-done.9.b = bf16[128,1024]{1,0:T(8,128)(2,1)S(1)} collective-permute-done((bf16[128,1024]{1,0:T(8,128)(2,1)S(1)}, bf16[128,1024]{1,0:T(8,128)(2,1)S(1)}, u32[]{:S(2)}, u32[]{:S(2)}) %collective-permute-start.9) | collective-permute-done | bytes 262176 | tf_op jit(solution)/shard_map/ppermute | solution.py:586
  183.7 0.7 collective-permute-done.11.d
  184.4 0.1 copy-done.10
  184.5 0.7 copy-done.11
  185.2 7.1 %project_out.1 = (f32[4,512,256]{2,1,0:T(8,128)}, bf16[4,512,256]{2,1,0:T(8,128)(2,1)}) custom-call(s32[3]{0:T(128)} %pad_add_fusion.1.meta_ref, bf16[128,1024]{1,0:T(8,128)(2,1)} %copy-done.2, bf16[128,1024]{1,0:T(8,128)(2,1)} %copy-done.9, bf16[128,1024]{1,0:T(8,128)(2,1)} %copy-done.10, bf16[128,1024]{1,0:T(8,128)(2,1)} %copy-done.11, ...), custom_call_target="tpu_custom_call" | custom-call | flops 1 | bytes 1 | tf_op jit(solution)/shard_map/project_out/pallas_call | solution.py:564
  192.3 2.9 %collective-permute-done.12 = bf16[4,512,256]{2,1,0:T(8,128)(2,1)S(1)} collective-permute-done((bf16[4,512,256]{2,1,0:T(8,128)(2,1)}, bf16[4,512,256]{2,1,0:T(8,128)(2,1)S(1)}, u32[]{:S(2)}, u32[]{:S(2)}) %collective-permute-start.12) | collective-permute-done | bytes 1048608 | tf_op jit(solution)/shard_map/ppermute | solution.py:663
  195.2 1.6 fusion.6
  196.8 4.1 %collective-permute-start.15 = (bf16[512,256]{1,0:T(8,128)(2,1)S(1)}, bf16[512,256]{1,0:T(8,128)(2,1)S(1)}, u32[]{:S(2)}, u32[]{:S(2)}) collective-permute-start(bf16[512,256]{1,0:T(8,128)(2,1)S(1)} %get-tuple-element.57), channel_id=1, source_target_pairs={{0,6},{1,7},{2,0},{3,1},{4,2},{5,3},{6,4},{7,5},{8,14},{9,15},{10,... | collective-permute-start | bytes 786440 | tf_op jit(solution)/shard_map/ppermute | solution.py:586
  200.9 0.1 collective-permute-start.14
  201.0 1.3 collective-permute-start.13
  202.3 10.1 %collective-permute-done.15 = bf16[512,256]{1,0:T(8,128)(2,1)S(1)} collective-permute-done((bf16[512,256]{1,0:T(8,128)(2,1)S(1)}, bf16[512,256]{1,0:T(8,128)(2,1)S(1)}, u32[]{:S(2)}, u32[]{:S(2)}) %collective-permute-start.15) | collective-permute-done | bytes 262176 | tf_op jit(solution)/shard_map/ppermute | solution.py:586
  212.4 3.5 %collective-permute-done.13 = bf16[512,256]{1,0:T(8,128)(2,1)S(1)} collective-permute-done((bf16[512,256]{1,0:T(8,128)(2,1)S(1)}, bf16[512,256]{1,0:T(8,128)(2,1)S(1)}, u32[]{:S(2)}, u32[]{:S(2)}) %collective-permute-start.13) | collective-permute-done | bytes 262176 | tf_op jit(solution)/shard_map/ppermute | solution.py:586
  215.9 1.9 fusion.4
  (45 shorter events, 0.3 us)
Async XLA Ops:
  16.4 4.3 %copy-start.12 = (s32[8,256]{1,0:T(8,128)S(1)}, s32[8,256]{1,0:T(8,128)}, u32[]{:S(2)}) copy-start(s32[8,256]{1,0:T(8,128)} %param.17) | copy-start | bytes 24580
  16.4 39.1 %all-to-all-start = ((f32[4,128,1408]{2,1,0:T(8,128)}), f32[4,128,1408]{2,1,0:T(8,128)S(1)}, u32[]{:S(2)}, u32[]{:S(2)}) async-start(f32[4,128,1408]{2,1,0:T(8,128)} %bitcast.29), calls=%async_computation | async-start | bytes 5767168 | tf_op jit(solution)/shard_map/all_to_all | solution.py:639
  20.8 114.3 %all-gather.3.cloned.1.call-start = ((), (), s32[]{:S(2)}) async-start(), calls=%async_computation.1 | async-start | bytes 1114112 | tf_op jit(solution)/shard_map/all_gather | solution.py:641
  29.7 26.7 %copy-start.14 = (s32[8]{0:T(128)S(1)}, s32[8]{0:T(128)}, u32[]{:S(2)}) copy-start(s32[8]{0:T(128)} %param.18) | copy-start | bytes 100
  29.7 28.0 %copy-start.13 = (s32[8,2]{0,1:T(2,128)S(1)}, s32[8,2]{0,1:T(2,128)}, u32[]{:S(2)}) copy-start(s32[8,2]{0,1:T(2,128)} %param.19) | copy-start | bytes 196
  29.7 71.0 %collective-permute-start.3 = (bf16[32,2,128,128]{3,2,1,0:T(8,128)(2,1)}, bf16[32,2,128,128]{3,2,1,0:T(8,128)(2,1)}, u32[]{:S(2)}, u32[]{:S(2)}) collective-permute-start(bf16[32,2,128,128]{3,2,1,0:T(8,128)(2,1)} %get-tuple-element.31), channel_id=1, source_target_pairs={{0,32},{32,64},{64,96},{96,0},{1,33},{33,65},{65,97},{97,1},{2,34}... | collective-permute-start | bytes 6291464 | tf_op jit(solution)/shard_map/ppermute | solution.py:586
  30.0 70.8 %collective-permute-start.4 = (bf16[32,2,128,128]{3,2,1,0:T(8,128)(2,1)}, bf16[32,2,128,128]{3,2,1,0:T(8,128)(2,1)}, u32[]{:S(2)}, u32[]{:S(2)}) collective-permute-start(bf16[32,2,128,128]{3,2,1,0:T(8,128)(2,1)} %get-tuple-element.32), channel_id=1, source_target_pairs={{0,96},{32,0},{64,32},{96,64},{1,97},{33,1},{65,33},{97,65},{2,98}... | collective-permute-start | bytes 6291464 | tf_op jit(solution)/shard_map/ppermute | solution.py:586
  31.8 103.3 %collective-permute-start.5 = (bf16[32,2,128,128]{3,2,1,0:T(8,128)(2,1)}, bf16[32,2,128,128]{3,2,1,0:T(8,128)(2,1)}, u32[]{:S(2)}, u32[]{:S(2)}) collective-permute-start(bf16[32,2,128,128]{3,2,1,0:T(8,128)(2,1)} %get-tuple-element.36), channel_id=1, source_target_pairs={{0,64},{32,96},{64,0},{96,32},{1,65},{33,97},{65,1},{97,33},{2,66}... | collective-permute-start | bytes 6291464 | tf_op jit(solution)/shard_map/ppermute | solution.py:586
  56.8 17.2 %collective-permute-start = (bf16[128,1280]{1,0:T(8,128)(2,1)S(1)}, bf16[128,1280]{1,0:T(8,128)(2,1)S(1)}, u32[]{:S(2)}, u32[]{:S(2)}) collective-permute-start(bf16[128,1280]{1,0:T(8,128)(2,1)S(1)} %get-tuple-element.24.refs_1_), channel_id=1, source_target_pairs={{0,8},{8,16},{16,24},{24,0},{1,9},{9,17},{17,25},{25,1},{2,10},{10... | collective-permute-start | bytes 983048 | tf_op jit(solution)/shard_map/ppermute | solution.py:586
  58.5 16.3 %collective-permute-start.1 = (bf16[128,1280]{1,0:T(8,128)(2,1)S(1)}, bf16[128,1280]{1,0:T(8,128)(2,1)S(1)}, u32[]{:S(2)}, u32[]{:S(2)}) collective-permute-start(bf16[128,1280]{1,0:T(8,128)(2,1)S(1)} %get-tuple-element.24.refs_1_), channel_id=1, source_target_pairs={{0,16},{8,24},{16,0},{24,8},{1,17},{9,25},{17,1},{25,9},{2,18},{10... | collective-permute-start | bytes 983048 | tf_op jit(solution)/shard_map/ppermute | solution.py:586
  74.0 7.3 %collective-permute-start.2 = (bf16[128,1280]{1,0:T(8,128)(2,1)S(1)}, bf16[128,1280]{1,0:T(8,128)(2,1)S(1)}, u32[]{:S(2)}, u32[]{:S(2)}) collective-permute-start(bf16[128,1280]{1,0:T(8,128)(2,1)S(1)} %get-tuple-element.24.refs_1_), channel_id=1, source_target_pairs={{0,24},{8,0},{16,8},{24,16},{1,25},{9,1},{17,9},{25,17},{2,26},{10... | collective-permute-start | bytes 983048 | tf_op jit(solution)/shard_map/ppermute | solution.py:586
  74.0 0.7 copy-start.3
  81.2 1.6 copy-start
  82.8 1.0 copy-start.4
  133.7 0.7 copy-start.5
  134.4 0.7 copy-start.7
  135.1 1.2 copy-start.1
  136.3 0.9 copy-start.6
  137.3 0.9 copy-start.8
  158.0 13.5 %collective-permute-start.6 = (bf16[144,1024]{1,0:T(8,128)(2,1)S(1)}, bf16[144,1024]{1,0:T(8,128)(2,1)S(1)}, u32[]{:S(2)}, u32[]{:S(2)}) collective-permute-start(bf16[144,1024]{1,0:T(8,128)(2,1)S(1)} %get-tuple-element.40), channel_id=1, source_target_pairs={{0,8},{8,16},{16,24},{24,0},{1,9},{9,17},{17,25},{25,1},{2,10},{10... | collective-permute-start | bytes 884744 | tf_op jit(solution)/shard_map/ppermute | solution.py:586
  158.1 13.4 %collective-permute-start.7 = (bf16[144,1024]{1,0:T(8,128)(2,1)S(1)}, bf16[144,1024]{1,0:T(8,128)(2,1)S(1)}, u32[]{:S(2)}, u32[]{:S(2)}) collective-permute-start(bf16[144,1024]{1,0:T(8,128)(2,1)S(1)} %get-tuple-element.41), channel_id=1, source_target_pairs={{0,16},{8,24},{16,0},{24,8},{1,17},{9,25},{17,1},{25,9},{2,18},{10... | collective-permute-start | bytes 884744 | tf_op jit(solution)/shard_map/ppermute | solution.py:586
  158.2 13.4 %collective-permute-start.8 = (bf16[144,1024]{1,0:T(8,128)(2,1)S(1)}, bf16[144,1024]{1,0:T(8,128)(2,1)S(1)}, u32[]{:S(2)}, u32[]{:S(2)}) collective-permute-start(bf16[144,1024]{1,0:T(8,128)(2,1)S(1)} %get-tuple-element.42), channel_id=1, source_target_pairs={{0,24},{8,0},{16,8},{24,16},{1,25},{9,1},{17,9},{25,17},{2,26},{10... | collective-permute-start | bytes 884744 | tf_op jit(solution)/shard_map/ppermute | solution.py:586
  172.4 12.0 %copy-start.2 = (bf16[128,1024]{1,0:T(8,128)(2,1)}, bf16[128,1024]{1,0:T(8,128)(2,1)S(1)}, u32[]{:S(2)}) copy-start(bf16[128,1024]{1,0:T(8,128)(2,1)S(1)} %combine.1.a) | copy-start | bytes 786436
  172.4 11.3 %collective-permute-start.9 = (bf16[128,1024]{1,0:T(8,128)(2,1)S(1)}, bf16[128,1024]{1,0:T(8,128)(2,1)S(1)}, u32[]{:S(2)}, u32[]{:S(2)}) collective-permute-start(bf16[128,1024]{1,0:T(8,128)(2,1)S(1)} %combine.1.a), channel_id=1, source_target_pairs={{0,8},{8,16},{16,24},{24,0},{1,9},{9,17},{17,25},{25,1},{2,10},{10... | collective-permute-start | bytes 786440 | tf_op jit(solution)/shard_map/ppermute | solution.py:586
  172.5 11.2 %collective-permute-start.10 = (bf16[128,1024]{1,0:T(8,128)(2,1)S(1)}, bf16[128,1024]{1,0:T(8,128)(2,1)S(1)}, u32[]{:S(2)}, u32[]{:S(2)}) collective-permute-start(bf16[128,1024]{1,0:T(8,128)(2,1)S(1)} %combine.1.a), channel_id=1, source_target_pairs={{0,16},{8,24},{16,0},{24,8},{1,17},{9,25},{17,1},{25,9},{2,18},{10... | collective-permute-start | bytes 786440 | tf_op jit(solution)/shard_map/ppermute | solution.py:586
  174.8 9.6 %collective-permute-start.11 = (bf16[128,1024]{1,0:T(8,128)(2,1)S(1)}, bf16[128,1024]{1,0:T(8,128)(2,1)S(1)}, u32[]{:S(2)}, u32[]{:S(2)}) collective-permute-start(bf16[128,1024]{1,0:T(8,128)(2,1)S(1)} %combine.1.a), channel_id=1, source_target_pairs={{0,24},{8,0},{16,8},{24,16},{1,25},{9,1},{17,9},{25,17},{2,26},{10... | collective-permute-start | bytes 786440 | tf_op jit(solution)/shard_map/ppermute | solution.py:586
  183.7 0.7 copy-start.9
  183.7 0.8 copy-start.10
  184.5 0.7 copy-start.11
  192.3 2.9 %collective-permute-start.12 = (bf16[4,512,256]{2,1,0:T(8,128)(2,1)}, bf16[4,512,256]{2,1,0:T(8,128)(2,1)S(1)}, u32[]{:S(2)}, u32[]{:S(2)}) collective-permute-start(bf16[4,512,256]{2,1,0:T(8,128)(2,1)} %get-tuple-element.44), channel_id=1, source_target_pairs={{0,1},{1,0},{2,3},{3,2},{4,5},{5,4},{6,7},{7,6},{8,9},{9,8},{10,11... | collective-permute-start | bytes 3145736 | tf_op jit(solution)/shard_map/ppermute | solution.py:663
  196.8 15.6 %collective-permute-start.15 = (bf16[512,256]{1,0:T(8,128)(2,1)S(1)}, bf16[512,256]{1,0:T(8,128)(2,1)S(1)}, u32[]{:S(2)}, u32[]{:S(2)}) collective-permute-start(bf16[512,256]{1,0:T(8,128)(2,1)S(1)} %get-tuple-element.57), channel_id=1, source_target_pairs={{0,6},{1,7},{2,0},{3,1},{4,2},{5,3},{6,4},{7,5},{8,14},{9,15},{10,... | collective-permute-start | bytes 786440 | tf_op jit(solution)/shard_map/ppermute | solution.py:586
  200.9 11.5 %collective-permute-start.14 = (bf16[512,256]{1,0:T(8,128)(2,1)S(1)}, bf16[512,256]{1,0:T(8,128)(2,1)S(1)}, u32[]{:S(2)}, u32[]{:S(2)}) collective-permute-start(bf16[512,256]{1,0:T(8,128)(2,1)S(1)} %get-tuple-element.58), channel_id=1, source_target_pairs={{0,4},{1,5},{2,6},{3,7},{4,0},{5,1},{6,2},{7,3},{8,12},{9,13},{10,... | collective-permute-start | bytes 786440 | tf_op jit(solution)/shard_map/ppermute | solution.py:586
  201.0 14.9 %collective-permute-start.13 = (bf16[512,256]{1,0:T(8,128)(2,1)S(1)}, bf16[512,256]{1,0:T(8,128)(2,1)S(1)}, u32[]{:S(2)}, u32[]{:S(2)}) collective-permute-start(bf16[512,256]{1,0:T(8,128)(2,1)S(1)} %get-tuple-element.56), channel_id=1, source_target_pairs={{0,2},{1,3},{2,4},{3,5},{4,6},{5,7},{6,0},{7,1},{8,10},{9,11},{10,... | collective-permute-start | bytes 786440 | tf_op jit(solution)/shard_map/ppermute | solution.py:586
Sparse Core Ops, SparseCore 0:
  56.4 72.6 all-gather.2
